TPU v7x, 32 devices: a whole 2x2x4 slice. The times are simulated.
32 devices in a mesh: seq: 8 (over z, y), doc: 4 (over x, core).
Axes of the slice: x: 2, y: 2, z: 4, core: 2. Of those that a mesh axis runs over, the one named last changes fastest.
Arguments:
- tokens: bfloat16 [4, 1024, 4096], P('doc', 'seq'), may hold values from -6 to 6
- norm_gain: float32 [4096], replicated, may hold values from 0.5 to 9
- w_query: bfloat16 [4096, 2048], P(None, 'doc'), may hold values from -0.09375 to 0.09375
- key_weight: bfloat16 [4096, 512], P(None, 'doc'), may hold values from -0.09375 to 0.09375
- value_weight: bfloat16 [4096, 512], P(None, 'doc'), may hold values from -0.09375 to 0.09375
- vertical_blocks: int32 [4, 4, 4], replicated, may hold values from 0 to 7, as said below
- slash_offsets: int32 [4, 4, 4], replicated, may hold values from 2 to 7, as said below
Outputs:
- attended: bfloat16 [4, 1024, 2048], P('doc', 'seq')
Inputs may be any that keep to these rules, and one draw needn't show every extreme that they name: `vertical_blocks`: within one document and key-value head the 4 block indices are distinct. `slash_offsets`: within one document and key-value head the 4 offsets are distinct.
All inputs are finite; a program needn't handle non-finite values.
Results may differ from a plain program's by a relative error of at most 0.013.
The roundings to bfloat16 on the way count: a program that leaves them out, or rounds other values in their place, can miss the bound.
Values may be sent and summed in bfloat16 or wider, within the bound.
No kernel may reach another device: no remote copies, remote signals or barrier semaphores. Data moves between devices by JAX's collectives and lax.ppermute only.
A program may use at most 64 MiB of HBM per device.

v0:
```python
import functools

import jax
import jax.numpy as jnp
from jax import lax
from jax.experimental import pallas as pl
from jax.experimental.pallas import tpu as pltpu
from jax.sharding import PartitionSpec as P

HEAD_WIDTH = 128
QUERY_HEADS = 16
KEY_VALUE_HEADS = 4
QUERY_GROUP = QUERY_HEADS // KEY_VALUE_HEADS
EPSILON = 1e-05
BAND = 16
MIB = 1024 * 1024

SMEM = pl.BlockSpec(memory_space=pltpu.SMEM)
VMEM = pl.BlockSpec(memory_space=pltpu.VMEM)
ANYWHERE = pl.BlockSpec(memory_space=pl.ANY)
HBM = pl.BlockSpec(memory_space=pltpu.HBM)


def swap(value, axis, mask):
    count = lax.axis_size(axis)
    return lax.ppermute(value, axis, [(source, source ^ mask) for source in range(count)])


def after(value, *others):
    return lax.optimization_barrier((value,) + others)[0]


def in_hbm(array):
    return pltpu.with_memory_space_constraint(array, pltpu.HBM)


def rope_table(positions, width):
    inverse = jnp.power(jnp.float32(500000.0), -jnp.arange(0, width, 2, dtype=jnp.float32) / width)
    angles = positions.astype(jnp.float32)[:, None] * inverse[None, :]
    return (jnp.cos(angles), jnp.sin(angles))


def project_kernel(places, table_rows, early, info_ref, *refs):
    token_refs = list(refs[:len(places)])
    refs = list(refs[len(places):])
    gain_ref, wq_ref, wk_ref, wv_ref, table_ref, q_ref, kv_ref = refs[:7]
    refs = refs[7:]
    core = info_ref[1] % 2
    copies = []
    if early:
        sources = (gain_ref, token_refs[0], wk_ref, wv_ref, wq_ref)
        held, refs = refs[:1] + refs[5:6] + refs[1:4], refs[4:5] + refs[6:]
        sems = refs[1]
        gain_ref, token_refs[0], wk_ref, wv_ref, wq_ref = held
        for at, (source, target) in enumerate(zip(sources, held)):
            copies.append(pltpu.make_async_copy(source, target, sems.at[at]))
            copies[-1].start()
        copies[0].wait()
    normed = refs[0]
    width = gain_ref.shape[1]
    heads = wk_ref.shape[1] // HEAD_WIDTH
    deep = min(1024, width)

    for piece, place in reversed(list(enumerate(places))):
        if piece == 0 and early:
            copies[1].wait()
        first = place(core)
        ref = token_refs[piece]

        def norm_band(index, carry, ref=ref, first=first):
            at = pl.ds(pl.multiple_of(index * BAND, BAND), BAND)
            wide = ref[at, :].astype(jnp.float32)
            scale = lax.rsqrt(jnp.mean(wide * wide, axis=-1, keepdims=True) + EPSILON)
            normed[pl.ds(pl.multiple_of(first + index * BAND, BAND), BAND), :] = (
                wide * scale * gain_ref[...]
            ).astype(jnp.bfloat16)
            return carry

        lax.fori_loop(0, ref.shape[0] // BAND, norm_band, 0, unroll=2)

    half = HEAD_WIDTH // 2

    def rotate(value, rows):
        cosine = table_ref[rows, :HEAD_WIDTH]
        sine = table_ref[rows, HEAD_WIDTH:]
        turned = jnp.concatenate([value[:, half:], value[:, :half]], axis=1)
        return (value * cosine + turned * sine).astype(jnp.bfloat16)

    def multiply(weight_of):
        total = None
        for start in range(0, width, deep):
            part = jnp.dot(
                normed[:, start:start + deep],
                weight_of(slice(start, start + deep)),
                preferred_element_type=jnp.float32,
            )
            total = part if total is None else total + part
        return total

    if early:
        copies[2].wait()
        copies[3].wait()
    for head in range(heads):
        at = slice(head * HEAD_WIDTH, (head + 1) * HEAD_WIDTH)
        both = multiply(lambda k: jnp.concatenate([wk_ref[k, at], wv_ref[k, at]], axis=1))
        out = 2 * head * HEAD_WIDTH
        row = 0
        for begin, count in table_rows:
            mine = both[row:row + count]
            kv_ref[row:row + count, out:out + HEAD_WIDTH] = rotate(
                mine[:, :HEAD_WIDTH], slice(begin, begin + count)
            )
            kv_ref[row:row + count, out + HEAD_WIDTH:out + 2 * HEAD_WIDTH] = mine[
                :, HEAD_WIDTH:
            ].astype(jnp.bfloat16)
            row += count
    if early:
        copies[4].wait()
    pair = 2 * HEAD_WIDTH
    for start in range(0, wq_ref.shape[1], pair):
        both = multiply(lambda k: wq_ref[k, start:start + pair])
        row = 0
        for begin, count in table_rows:
            for at in (0, HEAD_WIDTH):
                q_ref[row:row + count, start + at:start + at + HEAD_WIDTH] = rotate(
                    both[row:row + count, at:at + HEAD_WIDTH], slice(begin, begin + count)
                )
            row += count


def project(info, pieces, places, table_rows, gain, w_query, key_weight, value_weight, table, early=False):
    width = gain.shape[1]
    q_cols, k_cols = w_query.shape[1], key_weight.shape[1]
    total = sum(count for _, count in table_rows)
    params = (gain, w_query, key_weight, value_weight)
    scratch = [pltpu.VMEM((total, width), jnp.bfloat16)]
    kind = [VMEM] * (len(pieces) + len(params))
    shapes = [
        jax.ShapeDtypeStruct((total, q_cols), jnp.bfloat16),
        jax.ShapeDtypeStruct((total, 2 * k_cols), jnp.bfloat16),
    ]
    if early:
        scratch.append(pltpu.VMEM(pieces[0].shape, pieces[0].dtype))
        scratch.append(pltpu.SemaphoreType.DMA((5,)))
        params = tuple(in_hbm(array) for array in params)
        shapes += [
            jax.ShapeDtypeStruct(array.shape, array.dtype)
            for array in (gain, key_weight, value_weight, w_query)
        ]
        pieces = [in_hbm(pieces[0])] + list(pieces[1:])
        kind = [HBM] + [VMEM] * (len(pieces) - 1) + [HBM] * len(params)
    return pl.pallas_call(
        functools.partial(project_kernel, places, table_rows, early),
        in_specs=[SMEM] + kind + [VMEM],
        out_specs=[VMEM] * len(shapes),
        out_shape=shapes,
        scratch_shapes=scratch,
        compiler_params=pltpu.CompilerParams(vmem_limit_bytes=28 * MIB),
        cost_estimate=pl.CostEstimate(
            flops=2 * total * width * (q_cols + 2 * k_cols),
            bytes_accessed=2 * width * (q_cols + 2 * k_cols) + 2 * total * width,
            transcendentals=0,
        ),
        name="project",
    )(info, *pieces, *params, table)


def cut_kernel(source, *refs):
    sems = refs[-1]
    copies, first = [], 0
    for at, target in enumerate(refs[:-1]):
        count = target.shape[0]
        copies.append(pltpu.make_async_copy(source.at[pl.ds(first, count)], target, sems.at[at]))
        copies[-1].start()
        first += count
    for copy in copies:
        copy.wait()


def cut(array, counts):
    return pl.pallas_call(
        cut_kernel,
        in_specs=[HBM],
        out_specs=[VMEM] * len(counts),
        out_shape=[jax.ShapeDtypeStruct((rows,) + array.shape[1:], array.dtype) for rows in counts],
        scratch_shapes=[pltpu.SemaphoreType.DMA((len(counts),))],
        compiler_params=pltpu.CompilerParams(vmem_limit_bytes=16 * MIB),
        name="cut",
    )(in_hbm(array))


class Ring:
    def __init__(self, kv):
        count = lax.axis_size("seq")
        total = kv.shape[0]
        self.count, self.chunks, self.stage = count, 1, 0
        self.arrays, self.slots, self.latest = [], [], ()
        if count > 8 or count % 2:
            chunk = 8 if count % 8 == 0 else 1
            self.chunks = count // chunk
            self.arrays.append(lax.all_gather(kv, "seq", axis=0, tiled=True))
            for j in range(chunk):
                self.slots.append(
                    lambda place, index, j=j: (
                        0,
                        pl.multiple_of((index * chunk + j) * total, BAND),
                        index * chunk + j,
                    )
                )
        else:
            self.order = list(range(0, count, 2)) + list(range(count - 1, 0, -2))
            self.front = {1: kv, -1: kv}
            self.hold(kv, 0)

    def hold(self, array, steps):
        count, half = self.count, self.count // 2

        def slot(place, index, r=len(self.arrays)):
            z, y = place // 2, place % 2
            at = jnp.where(y == 0, z, count - 1 - z) + count - steps
            at = at % count
            return r, 0, jnp.where(at < half, 2 * at, 2 * (count - 1 - at) + 1)

        self.slots.append(slot)
        self.arrays.append(array)

    def advance(self, *others):
        if self.chunks > 1 or self.stage >= self.count // 2:
            return
        self.stage += 1
        ways = (1, -1) if 2 * self.stage < self.count else (1,)
        fresh = []
        for way in ways:
            value = after(self.front[way], *others) if others else self.front[way]
            pairs = [
                (source, self.order[(at + way) % self.count]) for at, source in enumerate(self.order)
            ]
            self.front[way] = lax.ppermute(value, "seq", pairs)
            fresh.append(self.front[way])
            self.hold(self.front[way], way * self.stage)
        self.latest = tuple(fresh)


def attend_kernel(lanes, spreads, q_count, info_ref, vertical_ref, slash_ref, *refs):
    q_refs = refs[:q_count]
    kv_refs, at = [], q_count
    for arrays, _, _ in spreads:
        kv_refs.append(refs[at:at + arrays])
        at += arrays
    out_refs = refs[at:]
    slots, chunks = spreads[0][1], spreads[0][2]
    heads = kv_refs[0][0].shape[1] // (2 * HEAD_WIDTH)
    rows = out_refs[0].shape[0]
    place = info_ref[0]
    group_place = info_ref[1]
    rank = QUERY_GROUP * rows
    span = len(slots) * rows
    factor = HEAD_WIDTH ** (-0.5)
    query_at = place * rows + lax.broadcasted_iota(jnp.int32, (rows, rows), 0)
    key_at = lax.broadcasted_iota(jnp.int32, (rows, rows), 1)

    def block_allowed(doc, group, block):
        found = (block == place) | (block == place - 1)
        for s in range(slash_ref.shape[2]):
            found = found | (block == place - slash_ref[doc, group, s])
        for s in range(vertical_ref.shape[2]):
            found = found | ((block == vertical_ref[doc, group, s]) & (block < place - 1))
        return found & (block >= 0)

    for lane, (doc_of, segments) in enumerate(lanes):
        doc = doc_of(info_ref[1])
        for head in range(heads):
            group = group_place * heads + head
            queries = jnp.concatenate(
                [
                    q_refs[source][
                        start:start + count,
                        (head * QUERY_GROUP + h) * HEAD_WIDTH:(head * QUERY_GROUP + h + 1) * HEAD_WIDTH,
                    ]
                    for h in range(QUERY_GROUP)
                    for source, start, count in segments
                ],
                axis=0,
            )

            def column(index, at):
                cols = slice(at * HEAD_WIDTH, (at + 1) * HEAD_WIDTH)
                parts = []
                for number in range(len(slots)):
                    for source, start, count in segments:
                        r, first, _ = spreads[source][1][number](place, index)
                        if isinstance(first, int):
                            where = slice(first + start, first + start + count)
                        else:
                            where = pl.ds(pl.multiple_of(first + start, BAND), count)
                        parts.append(kv_refs[source][r][where, cols])
                return jnp.concatenate(parts, axis=0)

            def step(index, carry):
                highest, total, mixed = carry
                keys, values = column(index, 2 * head), column(index, 2 * head + 1)
                scores = lax.dot_general(
                    queries, keys, (((1,), (1,)), ((), ())), preferred_element_type=jnp.float32
                ) * factor
                bias = []
                for slot in slots:
                    block = slot(place, index)[2]
                    bias.append(
                        jnp.where(
                            (key_at + block * rows <= query_at) & block_allowed(doc, group, block),
                            jnp.float32(0),
                            -jnp.inf,
                        )
                    )
                bias = jnp.concatenate(bias, axis=1)
                scores = (scores.reshape(QUERY_GROUP, rows, span) + bias[None]).reshape(rank, span)
                top = jnp.max(scores, axis=1, keepdims=True)
                if chunks > 1:
                    fresh = jnp.maximum(highest, top)
                    safe = jnp.where(fresh == -jnp.inf, jnp.float32(0), fresh)
                    fade = jnp.exp(highest - safe)
                else:
                    fresh = safe = top
                raised = jnp.exp(scores - safe)
                part = jnp.sum(raised, axis=1, keepdims=True)
                product = jnp.dot(
                    raised.astype(jnp.bfloat16), values, preferred_element_type=jnp.float32
                )
                if chunks > 1:
                    return fresh, total * fade + part, mixed * fade + product
                return fresh, part, product

            initial = (
                jnp.full((rank, 1), -jnp.inf, jnp.float32),
                jnp.zeros((rank, 1), jnp.float32),
                jnp.zeros((rank, HEAD_WIDTH), jnp.float32),
            )
            if chunks > 1:
                _, total, mixed = lax.fori_loop(0, chunks, step, initial)
            else:
                _, total, mixed = step(0, initial)
            result = (mixed / total).astype(jnp.bfloat16)
            for h in range(QUERY_GROUP):
                cols = slice(
                    (head * QUERY_GROUP + h) * HEAD_WIDTH, (head * QUERY_GROUP + h + 1) * HEAD_WIDTH
                )
                out_refs[lane][:, cols] = result[h * rows:(h + 1) * rows]


def attend(info, vertical, slash, lanes, queries, spreads):
    q_cols = queries[0].shape[1]
    rows = sum(count for _, _, count in lanes[0][1])
    span = len(spreads[0].slots) * spreads[0].chunks * rows
    arrays = [array for spread in spreads for array in spread.arrays]
    layout = [(len(spread.arrays), spread.slots, spread.chunks) for spread in spreads]
    return pl.pallas_call(
        functools.partial(attend_kernel, lanes, layout, len(queries)),
        in_specs=[SMEM] * 3 + [VMEM] * (len(queries) + len(arrays)),
        out_specs=[VMEM] * len(lanes),
        out_shape=[jax.ShapeDtypeStruct((rows, q_cols), jnp.bfloat16)] * len(lanes),
        compiler_params=pltpu.CompilerParams(vmem_limit_bytes=28 * MIB),
        cost_estimate=pl.CostEstimate(
            flops=4 * len(lanes) * rows * q_cols * span,
            bytes_accessed=2 * sum(a.size for a in arrays) + 4 * len(lanes) * rows * q_cols,
            transcendentals=len(lanes) * rows * span * q_cols // HEAD_WIDTH,
        ),
        name="attend",
    )(info, vertical, slash, *queries, *arrays)


def assemble_kernel(info_ref, *refs):
    out_ref = refs[-1]
    cols = refs[0].shape[1]
    for mask, ref in enumerate(refs[:-1]):
        at = pl.multiple_of((info_ref[1] ^ mask) * cols, cols)
        out_ref[0, :, pl.ds(at, cols)] = ref[...]


def assemble(info, *pieces):
    rows, cols = pieces[0].shape
    return pl.pallas_call(
        assemble_kernel,
        in_specs=[SMEM] + [VMEM] * len(pieces),
        out_specs=VMEM,
        out_shape=jax.ShapeDtypeStruct((1, rows, len(pieces) * cols), jnp.bfloat16),
        compiler_params=pltpu.CompilerParams(vmem_limit_bytes=16 * MIB),
        name="assemble",
    )(info, *pieces)


def local(tokens, norm_gain, w_query, key_weight, value_weight, vertical_blocks, slash_offsets):
    _, rows, width = tokens.shape
    assert lax.axis_size("doc") == 4
    place = lax.axis_index("seq")
    doc_place = lax.axis_index("doc")
    info = jnp.stack([place, doc_place]).astype(jnp.int32)
    cosine, sine = rope_table(place * rows + jnp.arange(rows, dtype=jnp.int32), HEAD_WIDTH)
    table = jnp.concatenate([cosine, cosine, -sine, sine], axis=1)
    own = tokens[0]
    gain = norm_gain.reshape(1, width)
    weights = (w_query, key_weight, value_weight)
    pattern = (info, vertical_blocks, slash_offsets)
    head = rows * 3 // 4 // BAND * BAND
    tail = rows - head

    twin = swap(own, "doc", 1)
    send_head, send_tail = cut(own, (head, tail))
    got_head = swap(send_head, "doc", 2)
    q_near, kv_near, gain_in, wk_in, wv_in, wq_in = project(
        info,
        [own, twin],
        [lambda c: 0, lambda c: rows],
        [(0, rows), (0, rows)],
        gain,
        *weights,
        table,
        early=True,
    )
    params = (gain_in, wq_in, wk_in, wv_in, table)
    near = Ring(kv_near)
    near.advance()
    near.advance()
    got_head = after(got_head, *near.latest)

    got_tail = swap(after(send_tail, got_head), "doc", 2)
    head_twin = swap(got_head, "doc", 1)
    near.advance()
    q_head, kv_head = project(
        info,
        [got_head, head_twin],
        [lambda c: 0, lambda c: head],
        [(0, head), (0, head)],
        *params,
    )
    ring_head = Ring(kv_head)
    ring_head.advance()

    got_tail = after(got_tail, *near.latest, *ring_head.latest)
    near.advance()
    tail_twin = swap(got_tail, "doc", 1)
    ring_head.advance()
    q_tail, kv_tail = project(
        info,
        [got_tail, tail_twin],
        [lambda c: 0, lambda c: tail],
        [(head, tail), (head, tail)],
        *params,
    )
    ring_tail = Ring(kv_tail)
    ring_tail.advance()
    mixed_own, mixed_twin = attend(
        *pattern,
        [(lambda d: d, [(0, 0, rows)]), (lambda d: d ^ 1, [(0, rows, rows)])],
        [after(q_near, *ring_tail.latest)],
        [near],
    )
    out_twin = swap(mixed_twin, "doc", 1)
    ring_head.advance()
    ring_tail.advance(mixed_twin)
    ring_head.advance()
    ring_tail.advance()
    ring_tail.advance()
    mixed = attend(
        *pattern,
        [
            (lambda d: d ^ 2, [(0, 0, head), (1, 0, tail)]),
            (lambda d: d ^ 3, [(0, head, head), (1, tail, tail)]),
        ],
        [after(q_head, out_twin), q_tail],
        [ring_head, ring_tail],
    )
    return assemble(info, mixed_own, out_twin, swap(mixed[0], "doc", 2), swap(mixed[1], "doc", 3))


def solution(mesh):
    return jax.shard_map(
        local,
        mesh=mesh,
        in_specs=(
            P("doc", "seq", None),
            P(),
            P(None, "doc"),
            P(None, "doc"),
            P(None, "doc"),
            P(),
            P(),
        ),
        out_specs=P("doc", "seq", None),
        check_vma=False,
    )
```

profile of v0, /device:TPU:0, one launch (start us, length us, event | category | flops | bytes accessed | tf_op | source)
XLA Modules:
  0.0 74.5 jit_solution(9953937713068790257)
XLA Ops:
  0.5 1.2 %cut.1 = (bf16[96,4096]{1,0:T(8,128)(2,1)S(1)}, bf16[32,4096]{1,0:T(8,128)(2,1)S(1)}) custom-call(bf16[128,4096]{1,0:T(8,128)(2,1)} %bitcast.5), custom_call_target="tpu_custom_call" | custom-call | tf_op jit(solution)/shard_map/cut/pallas_call | solution.py:181
  1.7 2.6 %collective-permute-start.1 = (bf16[96,4096]{1,0:T(8,128)(2,1)S(1)}, bf16[96,4096]{1,0:T(8,128)(2,1)S(1)}, u32[]{:S(2)}, u32[]{:S(2)}) collective-permute-start(bf16[96,4096]{1,0:T(8,128)(2,1)S(1)} %get-tuple-element.30), channel_id=1, source_target_pairs={{0,2},{1,3},{2,0},{3,1},{4,6},{5,7},{6,4},{7,5},{8,10},{9,11},{10,... | collective-permute-start | bytes 2359304 | tf_op jit(solution)/shard_map/ppermute | solution.py:26
  4.8 5.2 %project.3 = (bf16[256,512]{1,0:T(8,128)(2,1)S(1)}, bf16[256,256]{1,0:T(8,128)(2,1)S(1)}, f32[1,4096]{1,0:T(1,128)S(1)}, bf16[4096,128]{1,0:T(8,128)(2,1)S(1)}, ...) custom-call(s32[2]{0:T(128)S(1)} %pad_add_fusion.info_ref, bf16[128,4096]{1,0:T(8,128)(2,1)} %bitcast.6, ...), custom_call_target="tpu_custom_call" | custom-call | flops 1610612736 | bytes 8388608 | tf_op jit(solution)/shard_map/project/pallas_call | solution.py:152
  10.0 1.6 %collective-permute-start.2 = (bf16[256,256]{1,0:T(8,128)(2,1)S(1)}, bf16[256,256]{1,0:T(8,128)(2,1)S(1)}, u32[]{:S(2)}, u32[]{:S(2)}) collective-permute-start(bf16[256,256]{1,0:T(8,128)(2,1)S(1)} %get-tuple-element.31.refs_1_), channel_id=1, source_target_pairs={{0,8},{8,16},{16,24},{24,28},{28,20},{20,12},{12,4},{4,0},{1,9},{9... | collective-permute-start | bytes 393224 | tf_op jit(solution)/shard_map/ppermute | solution.py:238
  12.0 3.6 %collective-permute-done.2.refs_2_ = bf16[256,256]{1,0:T(8,128)(2,1)S(1)} collective-permute-done((bf16[256,256]{1,0:T(8,128)(2,1)S(1)}, bf16[256,256]{1,0:T(8,128)(2,1)S(1)}, u32[]{:S(2)}, u32[]{:S(2)}) %collective-permute-start.2) | collective-permute-done | bytes 131104 | tf_op jit(solution)/shard_map/ppermute | solution.py:238
  15.6 1.6 %collective-permute-start.3 = (bf16[256,256]{1,0:T(8,128)(2,1)S(1)}, bf16[256,256]{1,0:T(8,128)(2,1)S(1)}, u32[]{:S(2)}, u32[]{:S(2)}) collective-permute-start(bf16[256,256]{1,0:T(8,128)(2,1)S(1)} %collective-permute-done.2.refs_2_), channel_id=1, source_target_pairs={{0,8},{8,16},{16,24},{24,28},{28,20},{20,12},{12,4},{4,0},{1,9},{9... | collective-permute-start | bytes 393224 | tf_op jit(solution)/shard_map/ppermute | solution.py:238
  17.7 4.8 %collective-permute-done.1.refs_0_ = bf16[96,4096]{1,0:T(8,128)(2,1)S(1)} collective-permute-done((bf16[96,4096]{1,0:T(8,128)(2,1)S(1)}, bf16[96,4096]{1,0:T(8,128)(2,1)S(1)}, u32[]{:S(2)}, u32[]{:S(2)}) %collective-permute-start.1) | collective-permute-done | bytes 786464 | tf_op jit(solution)/shard_map/ppermute | solution.py:26
  22.4 1.8 %collective-permute-start.6 = (bf16[32,4096]{1,0:T(8,128)(2,1)S(1)}, bf16[32,4096]{1,0:T(8,128)(2,1)S(1)}, u32[]{:S(2)}, u32[]{:S(2)}) collective-permute-start(bf16[32,4096]{1,0:T(8,128)(2,1)S(1)} %get-tuple-element.33), channel_id=1, source_target_pairs={{0,2},{1,3},{2,0},{3,1},{4,6},{5,7},{6,4},{7,5},{8,10},{9,11},{10,... | collective-permute-start | bytes 786440 | tf_op jit(solution)/shard_map/ppermute | solution.py:26
  24.3 1.6 %collective-permute-start.7 = (bf16[256,256]{1,0:T(8,128)(2,1)S(1)}, bf16[256,256]{1,0:T(8,128)(2,1)S(1)}, u32[]{:S(2)}, u32[]{:S(2)}) collective-permute-start(bf16[256,256]{1,0:T(8,128)(2,1)S(1)} %collective-permute-done.3.refs_4_), channel_id=1, source_target_pairs={{0,8},{8,16},{16,24},{24,28},{28,20},{20,12},{12,4},{4,0},{1,9},{9... | collective-permute-start | bytes 393224 | tf_op jit(solution)/shard_map/ppermute | solution.py:238
  26.3 3.2 %project.4 = (bf16[192,512]{1,0:T(8,128)(2,1)S(1)}, bf16[192,256]{1,0:T(8,128)(2,1)S(1)}) custom-call(s32[2]{0:T(128)S(1)} %pad_add_fusion.info_ref, bf16[96,4096]{1,0:T(8,128)(2,1)S(1)} %collective-permute-done.1.refs_0_, bf16[96,4096]{1,0:T(8,128)(2,1)S(1)} %collective-permute-done.9.refs_1_, f32[1,4096]{1,0:T(1,128)S(1)} %get-tuple-element.34.refs_2_, ...), custom_call_target="tpu_custom_call" | custom-call | flops 1207959552 | bytes 7864320 | tf_op jit(solution)/shard_map/project/pallas_call | solution.py:152
  29.5 1.6 %collective-permute-start.10 = (bf16[192,256]{1,0:T(8,128)(2,1)S(1)}, bf16[192,256]{1,0:T(8,128)(2,1)S(1)}, u32[]{:S(2)}, u32[]{:S(2)}) collective-permute-start(bf16[192,256]{1,0:T(8,128)(2,1)S(1)} %get-tuple-element.38.refs_2_), channel_id=1, source_target_pairs={{0,8},{8,16},{16,24},{24,28},{28,20},{20,12},{12,4},{4,0},{1,9},{9... | collective-permute-start | bytes 294920 | tf_op jit(solution)/shard_map/ppermute | solution.py:238
  31.6 2.6 %collective-permute-done.10.refs_3_ = bf16[192,256]{1,0:T(8,128)(2,1)S(1)} collective-permute-done((bf16[192,256]{1,0:T(8,128)(2,1)S(1)}, bf16[192,256]{1,0:T(8,128)(2,1)S(1)}, u32[]{:S(2)}, u32[]{:S(2)}) %collective-permute-start.10) | collective-permute-done | bytes 98336 | tf_op jit(solution)/shard_map/ppermute | solution.py:238
  34.2 1.6 %collective-permute-done.11.refs_4_ = bf16[192,256]{1,0:T(8,128)(2,1)S(1)} collective-permute-done((bf16[192,256]{1,0:T(8,128)(2,1)S(1)}, bf16[192,256]{1,0:T(8,128)(2,1)S(1)}, u32[]{:S(2)}, u32[]{:S(2)}) %collective-permute-start.11) | collective-permute-done | bytes 98336 | tf_op jit(solution)/shard_map/ppermute | solution.py:238
  35.8 1.6 %collective-permute-start.15 = (bf16[256,256]{1,0:T(8,128)(2,1)S(1)}, bf16[256,256]{1,0:T(8,128)(2,1)S(1)}, u32[]{:S(2)}, u32[]{:S(2)}) collective-permute-start(bf16[256,256]{1,0:T(8,128)(2,1)S(1)} %collective-permute-done.7.refs_6_), channel_id=1, source_target_pairs={{0,8},{8,16},{16,24},{24,28},{28,20},{20,12},{12,4},{4,0},{1,9},{9... | collective-permute-start | bytes 393224 | tf_op jit(solution)/shard_map/ppermute | solution.py:238
  37.3 1.6 %collective-permute-start.17 = (bf16[192,256]{1,0:T(8,128)(2,1)S(1)}, bf16[192,256]{1,0:T(8,128)(2,1)S(1)}, u32[]{:S(2)}, u32[]{:S(2)}) collective-permute-start(bf16[192,256]{1,0:T(8,128)(2,1)S(1)} %collective-permute-done.10.refs_3_), channel_id=1, source_target_pairs={{0,8},{8,16},{16,24},{24,28},{28,20},{20,12},{12,4},{4,0},{1,9},{9... | collective-permute-start | bytes 294920 | tf_op jit(solution)/shard_map/ppermute | solution.py:238
  38.9 2.0 %project.5 = (bf16[64,512]{1,0:T(8,128)(2,1)S(1)}, bf16[64,256]{1,0:T(8,128)(2,1)S(1)}) custom-call(s32[2]{0:T(128)S(1)} %pad_add_fusion.info_ref, bf16[32,4096]{1,0:T(8,128)(2,1)S(1)} %collective-permute-done.6.refs_0_, bf16[32,4096]{1,0:T(8,128)(2,1)S(1)} %collective-permute-done.12.refs_1_, f32[1,4096]{1,0:T(1,128)S(1)} %get-tuple-element.34.refs_2_, ...), custom_call_target="tpu_custom_call" | custom-call | flops 402653184 | bytes 6815744 | tf_op jit(solution)/shard_map/project/pallas_call | solution.py:152
  40.9 1.6 %collective-permute-start.13 = (bf16[64,256]{1,0:T(8,128)(2,1)S(1)}, bf16[64,256]{1,0:T(8,128)(2,1)S(1)}, u32[]{:S(2)}, u32[]{:S(2)}) collective-permute-start(bf16[64,256]{1,0:T(8,128)(2,1)S(1)} %get-tuple-element.40.refs_10_), channel_id=1, source_target_pairs={{0,8},{8,16},{16,24},{24,28},{28,20},{20,12},{12,4},{4,0},{1,9},{9... | collective-permute-start | bytes 98312 | tf_op jit(solution)/shard_map/ppermute | solution.py:238
  44.0 1.6 %collective-permute-start.19 = (bf16[192,256]{1,0:T(8,128)(2,1)S(1)}, bf16[192,256]{1,0:T(8,128)(2,1)S(1)}, u32[]{:S(2)}, u32[]{:S(2)}) collective-permute-start(bf16[192,256]{1,0:T(8,128)(2,1)S(1)} %collective-permute-done.17.refs_5_), channel_id=1, source_target_pairs={{0,8},{8,16},{16,24},{24,28},{28,20},{20,12},{12,4},{4,0},{1,9},{9... | collective-permute-start | bytes 294920 | tf_op jit(solution)/shard_map/ppermute | solution.py:238
  45.6 0.9 %collective-permute-done.14.refs_12_ = bf16[64,256]{1,0:T(8,128)(2,1)S(1)} collective-permute-done((bf16[64,256]{1,0:T(8,128)(2,1)S(1)}, bf16[64,256]{1,0:T(8,128)(2,1)S(1)}, u32[]{:S(2)}, u32[]{:S(2)}) %collective-permute-start.14) | collective-permute-done | bytes 32800 | tf_op jit(solution)/shard_map/ppermute | solution.py:238
  46.5 3.1 %attend.2 = (bf16[128,512]{1,0:T(8,128)(2,1)S(1)}, bf16[128,512]{1,0:T(8,128)(2,1)S(1)}) custom-call(s32[2]{0:T(128)S(1)} %pad_add_fusion.info_ref, s32[4,4,4]{2,1,0:T(4,128)S(1)} %copy-done, s32[4,4,4]{2,1,0:T(4,128)S(1)} %copy-done.1, bf16[256,512]{1,0:T(8,128)(2,1)S(1)} %get-tuple-element.41.refs_0_, bf16[256,256]{1,0:T(8,128)(2,1)S(1)} %get-tuple-element.31.refs_1_, ...), custom_call_target="tpu_custom_call" | custom-call | flops 536870912 | bytes 1572864 | tf_op jit(solution)/shard_map/attend/pallas_call | solution.py:356
  50.3 1.5 %collective-permute-start.21 = (bf16[192,256]{1,0:T(8,128)(2,1)S(1)}, bf16[192,256]{1,0:T(8,128)(2,1)S(1)}, u32[]{:S(2)}, u32[]{:S(2)}) collective-permute-start(bf16[192,256]{1,0:T(8,128)(2,1)S(1)} %collective-permute-done.19.refs_7_), channel_id=1, source_target_pairs={{0,8},{8,16},{16,24},{24,28},{28,20},{20,12},{12,4},{4,0},{1,9},{9... | collective-permute-start | bytes 294920 | tf_op jit(solution)/shard_map/ppermute | solution.py:238
  51.8 0.8 %collective-permute-start.22 = (bf16[64,256]{1,0:T(8,128)(2,1)S(1)}, bf16[64,256]{1,0:T(8,128)(2,1)S(1)}, u32[]{:S(2)}, u32[]{:S(2)}) collective-permute-start(bf16[64,256]{1,0:T(8,128)(2,1)S(1)} %collective-permute-done.13.refs_11_), channel_id=1, source_target_pairs={{0,8},{8,16},{16,24},{24,28},{28,20},{20,12},{12,4},{4,0},{1,9},{9... | collective-permute-start | bytes 98312 | tf_op jit(solution)/shard_map/ppermute | solution.py:238
  52.6 1.2 %collective-permute-start.23 = (bf16[64,256]{1,0:T(8,128)(2,1)S(1)}, bf16[64,256]{1,0:T(8,128)(2,1)S(1)}, u32[]{:S(2)}, u32[]{:S(2)}) collective-permute-start(bf16[64,256]{1,0:T(8,128)(2,1)S(1)} %collective-permute-done.14.refs_12_), channel_id=1, source_target_pairs={{0,4},{8,0},{16,8},{24,16},{28,24},{20,28},{12,20},{4,12},{1,5},{9... | collective-permute-start | bytes 98312 | tf_op jit(solution)/shard_map/ppermute | solution.py:238
  53.8 2.0 %collective-permute-done.22.refs_13_ = bf16[64,256]{1,0:T(8,128)(2,1)S(1)} collective-permute-done((bf16[64,256]{1,0:T(8,128)(2,1)S(1)}, bf16[64,256]{1,0:T(8,128)(2,1)S(1)}, u32[]{:S(2)}, u32[]{:S(2)}) %collective-permute-start.22) | collective-permute-done | bytes 32800 | tf_op jit(solution)/shard_map/ppermute | solution.py:238
  55.8 1.5 %collective-permute-start.24 = (bf16[64,256]{1,0:T(8,128)(2,1)S(1)}, bf16[64,256]{1,0:T(8,128)(2,1)S(1)}, u32[]{:S(2)}, u32[]{:S(2)}) collective-permute-start(bf16[64,256]{1,0:T(8,128)(2,1)S(1)} %collective-permute-done.22.refs_13_), channel_id=1, source_target_pairs={{0,8},{8,16},{16,24},{24,28},{28,20},{20,12},{12,4},{4,0},{1,9},{9... | collective-permute-start | bytes 98312 | tf_op jit(solution)/shard_map/ppermute | solution.py:238
  57.9 1.9 %collective-permute-done.24.refs_15_ = bf16[64,256]{1,0:T(8,128)(2,1)S(1)} collective-permute-done((bf16[64,256]{1,0:T(8,128)(2,1)S(1)}, bf16[64,256]{1,0:T(8,128)(2,1)S(1)}, u32[]{:S(2)}, u32[]{:S(2)}) %collective-permute-start.24) | collective-permute-done | bytes 32800 | tf_op jit(solution)/shard_map/ppermute | solution.py:238
  59.8 1.5 %collective-permute-start.26 = (bf16[64,256]{1,0:T(8,128)(2,1)S(1)}, bf16[64,256]{1,0:T(8,128)(2,1)S(1)}, u32[]{:S(2)}, u32[]{:S(2)}) collective-permute-start(bf16[64,256]{1,0:T(8,128)(2,1)S(1)} %collective-permute-done.24.refs_15_), channel_id=1, source_target_pairs={{0,8},{8,16},{16,24},{24,28},{28,20},{20,12},{12,4},{4,0},{1,9},{9... | collective-permute-start | bytes 98312 | tf_op jit(solution)/shard_map/ppermute | solution.py:238
  61.3 2.4 %collective-permute-done.26.refs_17_ = bf16[64,256]{1,0:T(8,128)(2,1)S(1)} collective-permute-done((bf16[64,256]{1,0:T(8,128)(2,1)S(1)}, bf16[64,256]{1,0:T(8,128)(2,1)S(1)}, u32[]{:S(2)}, u32[]{:S(2)}) %collective-permute-start.26) | collective-permute-done | bytes 32800 | tf_op jit(solution)/shard_map/ppermute | solution.py:238
  63.7 3.1 %attend.3 = (bf16[128,512]{1,0:T(8,128)(2,1)S(1)}, bf16[128,512]{1,0:T(8,128)(2,1)S(1)}) custom-call(s32[2]{0:T(128)S(1)} %pad_add_fusion.info_ref, s32[4,4,4]{2,1,0:T(4,128)S(1)} %copy-done, s32[4,4,4]{2,1,0:T(4,128)S(1)} %copy-done.1, bf16[192,512]{1,0:T(8,128)(2,1)S(1)} %get-tuple-element.45.refs_0_, bf16[64,512]{1,0:T(8,128)(2,1)S(1)} %get-tuple-element.46.refs_1_, ...), custom_call_target="tpu_custom_call" | custom-call | flops 536870912 | bytes 1572864 | tf_op jit(solution)/shard_map/attend/pallas_call | solution.py:356
  66.8 0.6 collective-permute-start.27
  67.3 5.8 %collective-permute-done.27.refs_2_ = bf16[128,512]{1,0:T(8,128)(2,1)S(1)} collective-permute-done((bf16[128,512]{1,0:T(8,128)(2,1)S(1)}, bf16[128,512]{1,0:T(8,128)(2,1)S(1)}, u32[]{:S(2)}, u32[]{:S(2)}) %collective-permute-start.27) | collective-permute-done | bytes 131104 | tf_op jit(solution)/shard_map/ppermute | solution.py:26
  73.1 1.4 %assemble.1 = bf16[1,128,2048]{2,1,0:T(8,128)(2,1)} custom-call(s32[2]{0:T(128)S(1)} %pad_add_fusion.info_ref, bf16[128,512]{1,0:T(8,128)(2,1)S(1)} %get-tuple-element.42.refs_0_, bf16[128,512]{1,0:T(8,128)(2,1)S(1)} %collective-permute-done.16.refs_1_, bf16[128,512]{1,0:T(8,128)(2,1)S(1)} %collective-permute-done.27.refs_2_, ...), custom_call_target="tpu_custom_call" | custom-call | tf_op jit(solution)/shard_map/assemble/pallas_call | solution.py:381
  (42 shorter events, 5.4 us)
Async XLA Ops:
  0.0 4.8 %collective-permute-start = (bf16[128,4096]{1,0:T(8,128)(2,1)}, bf16[128,4096]{1,0:T(8,128)(2,1)S(1)}, u32[]{:S(2)}, u32[]{:S(2)}) collective-permute-start(bf16[128,4096]{1,0:T(8,128)(2,1)} %bitcast.4), channel_id=1, source_target_pairs={{0,1},{1,0},{2,3},{3,2},{4,5},{5,4},{6,7},{7,6},{8,9},{9,8},{10,11... | collective-permute-start | bytes 3145736 | tf_op jit(solution)/shard_map/ppermute | solution.py:26
  1.7 20.8 %collective-permute-start.1 = (bf16[96,4096]{1,0:T(8,128)(2,1)S(1)}, bf16[96,4096]{1,0:T(8,128)(2,1)S(1)}, u32[]{:S(2)}, u32[]{:S(2)}) collective-permute-start(bf16[96,4096]{1,0:T(8,128)(2,1)S(1)} %get-tuple-element.30), channel_id=1, source_target_pairs={{0,2},{1,3},{2,0},{3,1},{4,6},{5,7},{6,4},{7,5},{8,10},{9,11},{10,... | collective-permute-start | bytes 2359304 | tf_op jit(solution)/shard_map/ppermute | solution.py:26
  10.0 5.7 %collective-permute-start.2 = (bf16[256,256]{1,0:T(8,128)(2,1)S(1)}, bf16[256,256]{1,0:T(8,128)(2,1)S(1)}, u32[]{:S(2)}, u32[]{:S(2)}) collective-permute-start(bf16[256,256]{1,0:T(8,128)(2,1)S(1)} %get-tuple-element.31.refs_1_), channel_id=1, source_target_pairs={{0,8},{8,16},{16,24},{24,28},{28,20},{20,12},{12,4},{4,0},{1,9},{9... | collective-permute-start | bytes 393224 | tf_op jit(solution)/shard_map/ppermute | solution.py:238
  11.6 5.6 %collective-permute-start.4 = (bf16[256,256]{1,0:T(8,128)(2,1)S(1)}, bf16[256,256]{1,0:T(8,128)(2,1)S(1)}, u32[]{:S(2)}, u32[]{:S(2)}) collective-permute-start(bf16[256,256]{1,0:T(8,128)(2,1)S(1)} %get-tuple-element.31.refs_1_), channel_id=1, source_target_pairs={{0,4},{8,0},{16,8},{24,16},{28,24},{20,28},{12,20},{4,12},{1,5},{9... | collective-permute-start | bytes 393224 | tf_op jit(solution)/shard_map/ppermute | solution.py:238
  15.6 6.8 %collective-permute-start.3 = (bf16[256,256]{1,0:T(8,128)(2,1)S(1)}, bf16[256,256]{1,0:T(8,128)(2,1)S(1)}, u32[]{:S(2)}, u32[]{:S(2)}) collective-permute-start(bf16[256,256]{1,0:T(8,128)(2,1)S(1)} %collective-permute-done.2.refs_2_), channel_id=1, source_target_pairs={{0,8},{8,16},{16,24},{24,28},{28,20},{20,12},{12,4},{4,0},{1,9},{9... | collective-permute-start | bytes 393224 | tf_op jit(solution)/shard_map/ppermute | solution.py:238
  17.2 5.2 %collective-permute-start.5 = (bf16[256,256]{1,0:T(8,128)(2,1)S(1)}, bf16[256,256]{1,0:T(8,128)(2,1)S(1)}, u32[]{:S(2)}, u32[]{:S(2)}) collective-permute-start(bf16[256,256]{1,0:T(8,128)(2,1)S(1)} %collective-permute-done.4.refs_3_), channel_id=1, source_target_pairs={{0,4},{8,0},{16,8},{24,16},{28,24},{20,28},{12,20},{4,12},{1,5},{9... | collective-permute-start | bytes 393224 | tf_op jit(solution)/shard_map/ppermute | solution.py:238
  22.4 3.8 %collective-permute-start.9 = (bf16[96,4096]{1,0:T(8,128)(2,1)S(1)}, bf16[96,4096]{1,0:T(8,128)(2,1)S(1)}, u32[]{:S(2)}, u32[]{:S(2)}) collective-permute-start(bf16[96,4096]{1,0:T(8,128)(2,1)S(1)} %collective-permute-done.1.refs_0_), channel_id=1, source_target_pairs={{0,1},{1,0},{2,3},{3,2},{4,5},{5,4},{6,7},{7,6},{8,9},{9,8},{10,11... | collective-permute-start | bytes 2359304 | tf_op jit(solution)/shard_map/ppermute | solution.py:26
  22.4 9.2 %collective-permute-start.6 = (bf16[32,4096]{1,0:T(8,128)(2,1)S(1)}, bf16[32,4096]{1,0:T(8,128)(2,1)S(1)}, u32[]{:S(2)}, u32[]{:S(2)}) collective-permute-start(bf16[32,4096]{1,0:T(8,128)(2,1)S(1)} %get-tuple-element.33), channel_id=1, source_target_pairs={{0,2},{1,3},{2,0},{3,1},{4,6},{5,7},{6,4},{7,5},{8,10},{9,11},{10,... | collective-permute-start | bytes 786440 | tf_op jit(solution)/shard_map/ppermute | solution.py:26
  24.3 7.3 %collective-permute-start.7 = (bf16[256,256]{1,0:T(8,128)(2,1)S(1)}, bf16[256,256]{1,0:T(8,128)(2,1)S(1)}, u32[]{:S(2)}, u32[]{:S(2)}) collective-permute-start(bf16[256,256]{1,0:T(8,128)(2,1)S(1)} %collective-permute-done.3.refs_4_), channel_id=1, source_target_pairs={{0,8},{8,16},{16,24},{24,28},{28,20},{20,12},{12,4},{4,0},{1,9},{9... | collective-permute-start | bytes 393224 | tf_op jit(solution)/shard_map/ppermute | solution.py:238
  25.8 5.8 %collective-permute-start.8 = (bf16[256,256]{1,0:T(8,128)(2,1)S(1)}, bf16[256,256]{1,0:T(8,128)(2,1)S(1)}, u32[]{:S(2)}, u32[]{:S(2)}) collective-permute-start(bf16[256,256]{1,0:T(8,128)(2,1)S(1)} %collective-permute-done.5.refs_5_), channel_id=1, source_target_pairs={{0,4},{8,0},{16,8},{24,16},{28,24},{20,28},{12,20},{4,12},{1,5},{9... | collective-permute-start | bytes 393224 | tf_op jit(solution)/shard_map/ppermute | solution.py:238
  29.5 17.0 %copy-start = (s32[4,4,4]{2,1,0:T(4,128)S(1)}, s32[4,4,4]{2,1,0:T(4,128)}, u32[]{:S(2)}) copy-start(s32[4,4,4]{2,1,0:T(4,128)} %vertical_ref.3) | copy-start | bytes 772
  29.5 17.0 %copy-start.1 = (s32[4,4,4]{2,1,0:T(4,128)S(1)}, s32[4,4,4]{2,1,0:T(4,128)}, u32[]{:S(2)}) copy-start(s32[4,4,4]{2,1,0:T(4,128)} %slash_ref.3) | copy-start | bytes 772
  29.5 4.7 %collective-permute-start.10 = (bf16[192,256]{1,0:T(8,128)(2,1)S(1)}, bf16[192,256]{1,0:T(8,128)(2,1)S(1)}, u32[]{:S(2)}, u32[]{:S(2)}) collective-permute-start(bf16[192,256]{1,0:T(8,128)(2,1)S(1)} %get-tuple-element.38.refs_2_), channel_id=1, source_target_pairs={{0,8},{8,16},{16,24},{24,28},{28,20},{20,12},{12,4},{4,0},{1,9},{9... | collective-permute-start | bytes 294920 | tf_op jit(solution)/shard_map/ppermute | solution.py:238
  31.2 4.6 %collective-permute-start.11 = (bf16[192,256]{1,0:T(8,128)(2,1)S(1)}, bf16[192,256]{1,0:T(8,128)(2,1)S(1)}, u32[]{:S(2)}, u32[]{:S(2)}) collective-permute-start(bf16[192,256]{1,0:T(8,128)(2,1)S(1)} %get-tuple-element.38.refs_2_), channel_id=1, source_target_pairs={{0,4},{8,0},{16,8},{24,16},{28,24},{20,28},{12,20},{4,12},{1,5},{9... | collective-permute-start | bytes 294920 | tf_op jit(solution)/shard_map/ppermute | solution.py:238
  35.8 3.1 %collective-permute-start.12 = (bf16[32,4096]{1,0:T(8,128)(2,1)S(1)}, bf16[32,4096]{1,0:T(8,128)(2,1)S(1)}, u32[]{:S(2)}, u32[]{:S(2)}) collective-permute-start(bf16[32,4096]{1,0:T(8,128)(2,1)S(1)} %collective-permute-done.6.refs_0_), channel_id=1, source_target_pairs={{0,1},{1,0},{2,3},{3,2},{4,5},{5,4},{6,7},{7,6},{8,9},{9,8},{10,11... | collective-permute-start | bytes 786440 | tf_op jit(solution)/shard_map/ppermute | solution.py:26
  35.8 10.8 %collective-permute-start.15 = (bf16[256,256]{1,0:T(8,128)(2,1)S(1)}, bf16[256,256]{1,0:T(8,128)(2,1)S(1)}, u32[]{:S(2)}, u32[]{:S(2)}) collective-permute-start(bf16[256,256]{1,0:T(8,128)(2,1)S(1)} %collective-permute-done.7.refs_6_), channel_id=1, source_target_pairs={{0,8},{8,16},{16,24},{24,28},{28,20},{20,12},{12,4},{4,0},{1,9},{9... | collective-permute-start | bytes 393224 | tf_op jit(solution)/shard_map/ppermute | solution.py:238
  37.3 6.6 %collective-permute-start.17 = (bf16[192,256]{1,0:T(8,128)(2,1)S(1)}, bf16[192,256]{1,0:T(8,128)(2,1)S(1)}, u32[]{:S(2)}, u32[]{:S(2)}) collective-permute-start(bf16[192,256]{1,0:T(8,128)(2,1)S(1)} %collective-permute-done.10.refs_3_), channel_id=1, source_target_pairs={{0,8},{8,16},{16,24},{24,28},{28,20},{20,12},{12,4},{4,0},{1,9},{9... | collective-permute-start | bytes 294920 | tf_op jit(solution)/shard_map/ppermute | solution.py:238
  40.9 4.7 %collective-permute-start.13 = (bf16[64,256]{1,0:T(8,128)(2,1)S(1)}, bf16[64,256]{1,0:T(8,128)(2,1)S(1)}, u32[]{:S(2)}, u32[]{:S(2)}) collective-permute-start(bf16[64,256]{1,0:T(8,128)(2,1)S(1)} %get-tuple-element.40.refs_10_), channel_id=1, source_target_pairs={{0,8},{8,16},{16,24},{24,28},{28,20},{20,12},{12,4},{4,0},{1,9},{9... | collective-permute-start | bytes 98312 | tf_op jit(solution)/shard_map/ppermute | solution.py:238
  42.5 4.0 %collective-permute-start.14 = (bf16[64,256]{1,0:T(8,128)(2,1)S(1)}, bf16[64,256]{1,0:T(8,128)(2,1)S(1)}, u32[]{:S(2)}, u32[]{:S(2)}) collective-permute-start(bf16[64,256]{1,0:T(8,128)(2,1)S(1)} %get-tuple-element.40.refs_10_), channel_id=1, source_target_pairs={{0,4},{8,0},{16,8},{24,16},{28,24},{20,28},{12,20},{4,12},{1,5},{9... | collective-permute-start | bytes 98312 | tf_op jit(solution)/shard_map/ppermute | solution.py:238
  43.0 6.7 %collective-permute-start.18 = (bf16[192,256]{1,0:T(8,128)(2,1)S(1)}, bf16[192,256]{1,0:T(8,128)(2,1)S(1)}, u32[]{:S(2)}, u32[]{:S(2)}) collective-permute-start(bf16[192,256]{1,0:T(8,128)(2,1)S(1)} %collective-permute-done.11.refs_4_), channel_id=1, source_target_pairs={{0,4},{8,0},{16,8},{24,16},{28,24},{20,28},{12,20},{4,12},{1,5},{9... | collective-permute-start | bytes 294920 | tf_op jit(solution)/shard_map/ppermute | solution.py:238
  44.0 6.3 %collective-permute-start.19 = (bf16[192,256]{1,0:T(8,128)(2,1)S(1)}, bf16[192,256]{1,0:T(8,128)(2,1)S(1)}, u32[]{:S(2)}, u32[]{:S(2)}) collective-permute-start(bf16[192,256]{1,0:T(8,128)(2,1)S(1)} %collective-permute-done.17.refs_5_), channel_id=1, source_target_pairs={{0,8},{8,16},{16,24},{24,28},{28,20},{20,12},{12,4},{4,0},{1,9},{9... | collective-permute-start | bytes 294920 | tf_op jit(solution)/shard_map/ppermute | solution.py:238
  49.6 11.7 %collective-permute-start.16 = (bf16[128,512]{1,0:T(8,128)(2,1)S(1)}, bf16[128,512]{1,0:T(8,128)(2,1)S(1)}, u32[]{:S(2)}, u32[]{:S(2)}) collective-permute-start(bf16[128,512]{1,0:T(8,128)(2,1)S(1)} %get-tuple-element.43), channel_id=1, source_target_pairs={{0,1},{1,0},{2,3},{3,2},{4,5},{5,4},{6,7},{7,6},{8,9},{9,8},{10,11... | collective-permute-start | bytes 393224 | tf_op jit(solution)/shard_map/ppermute | solution.py:26
  49.7 11.6 %collective-permute-start.20 = (bf16[192,256]{1,0:T(8,128)(2,1)S(1)}, bf16[192,256]{1,0:T(8,128)(2,1)S(1)}, u32[]{:S(2)}, u32[]{:S(2)}) collective-permute-start(bf16[192,256]{1,0:T(8,128)(2,1)S(1)} %collective-permute-done.18.refs_6_), channel_id=1, source_target_pairs={{0,4},{8,0},{16,8},{24,16},{28,24},{20,28},{12,20},{4,12},{1,5},{9... | collective-permute-start | bytes 294920 | tf_op jit(solution)/shard_map/ppermute | solution.py:238
  50.3 11.0 %collective-permute-start.21 = (bf16[192,256]{1,0:T(8,128)(2,1)S(1)}, bf16[192,256]{1,0:T(8,128)(2,1)S(1)}, u32[]{:S(2)}, u32[]{:S(2)}) collective-permute-start(bf16[192,256]{1,0:T(8,128)(2,1)S(1)} %collective-permute-done.19.refs_7_), channel_id=1, source_target_pairs={{0,8},{8,16},{16,24},{24,28},{28,20},{20,12},{12,4},{4,0},{1,9},{9... | collective-permute-start | bytes 294920 | tf_op jit(solution)/shard_map/ppermute | solution.py:238
  51.8 4.0 %collective-permute-start.22 = (bf16[64,256]{1,0:T(8,128)(2,1)S(1)}, bf16[64,256]{1,0:T(8,128)(2,1)S(1)}, u32[]{:S(2)}, u32[]{:S(2)}) collective-permute-start(bf16[64,256]{1,0:T(8,128)(2,1)S(1)} %collective-permute-done.13.refs_11_), channel_id=1, source_target_pairs={{0,8},{8,16},{16,24},{24,28},{28,20},{20,12},{12,4},{4,0},{1,9},{9... | collective-permute-start | bytes 98312 | tf_op jit(solution)/shard_map/ppermute | solution.py:238
  52.6 4.8 %collective-permute-start.23 = (bf16[64,256]{1,0:T(8,128)(2,1)S(1)}, bf16[64,256]{1,0:T(8,128)(2,1)S(1)}, u32[]{:S(2)}, u32[]{:S(2)}) collective-permute-start(bf16[64,256]{1,0:T(8,128)(2,1)S(1)} %collective-permute-done.14.refs_12_), channel_id=1, source_target_pairs={{0,4},{8,0},{16,8},{24,16},{28,24},{20,28},{12,20},{4,12},{1,5},{9... | collective-permute-start | bytes 98312 | tf_op jit(solution)/shard_map/ppermute | solution.py:238
  55.8 3.9 %collective-permute-start.24 = (bf16[64,256]{1,0:T(8,128)(2,1)S(1)}, bf16[64,256]{1,0:T(8,128)(2,1)S(1)}, u32[]{:S(2)}, u32[]{:S(2)}) collective-permute-start(bf16[64,256]{1,0:T(8,128)(2,1)S(1)} %collective-permute-done.22.refs_13_), channel_id=1, source_target_pairs={{0,8},{8,16},{16,24},{24,28},{28,20},{20,12},{12,4},{4,0},{1,9},{9... | collective-permute-start | bytes 98312 | tf_op jit(solution)/shard_map/ppermute | solution.py:238
  57.4 3.9 %collective-permute-start.25 = (bf16[64,256]{1,0:T(8,128)(2,1)S(1)}, bf16[64,256]{1,0:T(8,128)(2,1)S(1)}, u32[]{:S(2)}, u32[]{:S(2)}) collective-permute-start(bf16[64,256]{1,0:T(8,128)(2,1)S(1)} %collective-permute-done.23.refs_14_), channel_id=1, source_target_pairs={{0,4},{8,0},{16,8},{24,16},{28,24},{20,28},{12,20},{4,12},{1,5},{9... | collective-permute-start | bytes 98312 | tf_op jit(solution)/shard_map/ppermute | solution.py:238
  59.8 3.9 %collective-permute-start.26 = (bf16[64,256]{1,0:T(8,128)(2,1)S(1)}, bf16[64,256]{1,0:T(8,128)(2,1)S(1)}, u32[]{:S(2)}, u32[]{:S(2)}) collective-permute-start(bf16[64,256]{1,0:T(8,128)(2,1)S(1)} %collective-permute-done.24.refs_15_), channel_id=1, source_target_pairs={{0,8},{8,16},{16,24},{24,28},{28,20},{20,12},{12,4},{4,0},{1,9},{9... | collective-permute-start | bytes 98312 | tf_op jit(solution)/shard_map/ppermute | solution.py:238
  66.8 6.4 %collective-permute-start.27 = (bf16[128,512]{1,0:T(8,128)(2,1)S(1)}, bf16[128,512]{1,0:T(8,128)(2,1)S(1)}, u32[]{:S(2)}, u32[]{:S(2)}) collective-permute-start(bf16[128,512]{1,0:T(8,128)(2,1)S(1)} %get-tuple-element.49), channel_id=1, source_target_pairs={{0,2},{1,3},{2,0},{3,1},{4,6},{5,7},{6,4},{7,5},{8,10},{9,11},{10,... | collective-permute-start | bytes 393224 | tf_op jit(solution)/shard_map/ppermute | solution.py:26
  67.3 5.8 %collective-permute-start.28 = (bf16[128,512]{1,0:T(8,128)(2,1)S(1)}, bf16[128,512]{1,0:T(8,128)(2,1)S(1)}, u32[]{:S(2)}, u32[]{:S(2)}) collective-permute-start(bf16[128,512]{1,0:T(8,128)(2,1)S(1)} %get-tuple-element.50), channel_id=1, source_target_pairs={{0,3},{1,2},{2,1},{3,0},{4,7},{5,6},{6,5},{7,4},{8,11},{9,10},{10,... | collective-permute-start | bytes 393224 | tf_op jit(solution)/shard_map/ppermute | solution.py:26
where the time goes:
time: 75.5 us; the launch traced here: 74.5 us
  starting transfers between devices  28.6 us (38%)
  waiting for transfers between devices  26.1 us (35%)
  Pallas kernels  19.1 us (25%)
    ppermute x21, starting transfers between devices, advance(): self.front[way] = lax.ppermute(value, 'seq', pairs)  23.1 us
    ppermute x21, waiting for transfers between devices, advance(): self.front[way] = lax.ppermute(value, 'seq', pairs)  15.5 us
    ppermute x8, waiting for transfers between devices, swap(): lax.ppermute(value, axis, [(source, source ^ mask) for source in range(co...  10.6 us
    pallas_call x3, Pallas kernels, project(): pl.pallas_call(functools.partial(project_kernel, places, table_rows, earl...  10.4 us
    pallas_call x2, Pallas kernels, attend(): pl.pallas_call(functools.partial(attend_kernel, lanes, layout, len(querie...  6.16 us
    ppermute x8, starting transfers between devices, swap(): lax.ppermute(value, axis, [(source, source ^ mask) for source in range(co...  5.47 us
  transfers between devices with their start and end apart: 29, of which 10 were waited for; matrix products, arithmetic and copies ran while one was open for 1% of the time, Pallas kernels for 20%

commit v1 on v0

--- a/solution.py
+++ b/solution.py
@@ -189,48 +189,64 @@
     )(in_hbm(array))
 
 
-class Ring:
+def ring_order(count):
+    return list(range(0, count, 2)) + list(range(count - 1, 0, -2))
+
+
+def ring_place(place, count):
+    return jnp.where(place % 2 == 0, place // 2, count - 1 - place // 2)
+
+
+def ring_block(at, count):
+    at = (at + count) % count
+    return jnp.where(at < count // 2, 2 * at, 2 * (count - 1 - at) + 1)
+
+
+class Gathered:
     def __init__(self, kv):
         count = lax.axis_size("seq")
         total = kv.shape[0]
-        self.count, self.chunks, self.stage = count, 1, 0
+        chunk = 8 if count % 8 == 0 else 1
+        self.chunks, self.latest = count // chunk, ()
+        self.arrays = [lax.all_gather(kv, "seq", axis=0, tiled=True)]
+        self.slots = [
+            lambda place, index, j=j: (
+                0,
+                pl.multiple_of((index * chunk + j) * total, BAND),
+                index * chunk + j,
+            )
+            for j in range(chunk)
+        ]
+
+    def advance(self, *others):
+        pass
+
+
+class Ring:
+    def __init__(self, kv):
+        self.count, self.chunks, self.stage = lax.axis_size("seq"), 1, 0
+        self.order = ring_order(self.count)
         self.arrays, self.slots, self.latest = [], [], ()
-        if count > 8 or count % 2:
-            chunk = 8 if count % 8 == 0 else 1
-            self.chunks = count // chunk
-            self.arrays.append(lax.all_gather(kv, "seq", axis=0, tiled=True))
-            for j in range(chunk):
-                self.slots.append(
-                    lambda place, index, j=j: (
-                        0,
-                        pl.multiple_of((index * chunk + j) * total, BAND),
-                        index * chunk + j,
-                    )
-                )
-        else:
-            self.order = list(range(0, count, 2)) + list(range(count - 1, 0, -2))
-            self.front = {1: kv, -1: kv}
-            self.hold(kv, 0)
+        self.front = {1: kv, -1: kv}
+        self.hold(kv, 0)
 
     def hold(self, array, steps):
-        count, half = self.count, self.count // 2
-
-        def slot(place, index, r=len(self.arrays)):
-            z, y = place // 2, place % 2
-            at = jnp.where(y == 0, z, count - 1 - z) + count - steps
-            at = at % count
-            return r, 0, jnp.where(at < half, 2 * at, 2 * (count - 1 - at) + 1)
-
-        self.slots.append(slot)
+        count = self.count
+        self.slots.append(
+            lambda place, index, r=len(self.arrays): (
+                r,
+                0,
+                ring_block(ring_place(place, count) - steps, count),
+            )
+        )
         self.arrays.append(array)
 
     def advance(self, *others):
-        if self.chunks > 1 or self.stage >= self.count // 2:
+        if self.stage >= self.count // 2:
             return
         self.stage += 1
-        ways = (1, -1) if 2 * self.stage < self.count else (1,)
         fresh = []
-        for way in ways:
+        for way in (1, -1) if 2 * self.stage < self.count else (1,):
             value = after(self.front[way], *others) if others else self.front[way]
             pairs = [
                 (source, self.order[(at + way) % self.count]) for at, source in enumerate(self.order)
@@ -241,23 +257,55 @@
         self.latest = tuple(fresh)
 
 
-def attend_kernel(lanes, spreads, q_count, info_ref, vertical_ref, slash_ref, *refs):
-    q_refs = refs[:q_count]
-    kv_refs, at = [], q_count
-    for arrays, _, _ in spreads:
-        kv_refs.append(refs[at:at + arrays])
-        at += arrays
-    out_refs = refs[at:]
-    slots, chunks = spreads[0][1], spreads[0][2]
-    heads = kv_refs[0][0].shape[1] // (2 * HEAD_WIDTH)
-    rows = out_refs[0].shape[0]
+class Pairs:
+    def __init__(self, kv):
+        self.count, self.chunks, self.step = lax.axis_size("seq"), 1, 0
+        self.order = ring_order(self.count)
+        self.total, self.front, self.latest = kv.shape[0], kv, ()
+        self.arrays, self.slots = [kv], []
+        self.hold(0, 0, lambda at: at)
+
+    def hold(self, r, first, block_at):
+        count = self.count
+        self.slots.append(
+            lambda place, index: (r, first, ring_block(block_at(ring_place(place, count)), count))
+        )
+
+    def beside(self, at, step):
+        up = 1 - 2 * (at % 2)
+        return (at + (up if step % 2 == 1 else -up) + self.count) % self.count
+
+    def source(self, at, step):
+        for back in range(step, 1, -1):
+            at = self.beside(at, back)
+        return at if step > 1 else self.beside(at, 1)
+
+    def advance(self, *others):
+        if self.step >= self.count // 2:
+            return
+        self.step += 1
+        step = self.step
+        value = after(self.front, *others) if others else self.front
+        pairs = [(source, self.order[self.beside(at, step)]) for at, source in enumerate(self.order)]
+        got = lax.ppermute(value, "seq", pairs)
+        r = len(self.arrays)
+        self.arrays.append(got)
+        self.hold(r, 0, lambda at: self.source(at, step))
+        if step == 1:
+            self.front = jnp.concatenate([self.front, got], axis=0)
+        else:
+            self.front = got
+            self.hold(r, self.total, lambda at: self.beside(self.source(at, step), 1))
+        self.latest = (got,)
+
+
+def attend_kernel(lanes, slots, chunks, q_count, kv_count, begin, end, info_ref, vertical_ref, slash_ref, *refs):
+    q_refs, kv_refs, refs = refs[:q_count], refs[q_count:q_count + kv_count], refs[q_count + kv_count:]
+    state_refs = refs[:0 if begin else 3 * len(lanes)]
+    out_refs = refs[len(state_refs):]
+    heads = kv_refs[0].shape[1] // (2 * HEAD_WIDTH)
     place = info_ref[0]
-    group_place = info_ref[1]
-    rank = QUERY_GROUP * rows
-    span = len(slots) * rows
     factor = HEAD_WIDTH ** (-0.5)
-    query_at = place * rows + lax.broadcasted_iota(jnp.int32, (rows, rows), 0)
-    key_at = lax.broadcasted_iota(jnp.int32, (rows, rows), 1)
 
     def block_allowed(doc, group, block):
         found = (block == place) | (block == place - 1)
@@ -267,10 +315,15 @@
             found = found | ((block == vertical_ref[doc, group, s]) & (block < place - 1))
         return found & (block >= 0)
 
-    for lane, (doc_of, segments) in enumerate(lanes):
+    for lane, (doc_of, segments, (kv_first, keys_in, base)) in enumerate(lanes):
         doc = doc_of(info_ref[1])
+        rows = sum(count for _, _, count in segments)
+        rank = QUERY_GROUP * rows
+        span = len(slots) * keys_in
+        query_at = place * rows + lax.broadcasted_iota(jnp.int32, (rows, span), 0)
+        column_at = lax.broadcasted_iota(jnp.int32, (1, span), 1)
         for head in range(heads):
-            group = group_place * heads + head
+            group = info_ref[1] * heads + head
             queries = jnp.concatenate(
                 [
                     q_refs[source][
@@ -283,62 +336,76 @@
                 axis=0,
             )
 
-            def column(index, at):
-                cols = slice(at * HEAD_WIDTH, (at + 1) * HEAD_WIDTH)
-                parts = []
-                for number in range(len(slots)):
-                    for source, start, count in segments:
-                        r, first, _ = spreads[source][1][number](place, index)
+            def step(index, carry):
+                found = [slot(place, index) for slot in slots]
+
+                def column(at):
+                    cols = slice(at * HEAD_WIDTH, (at + 1) * HEAD_WIDTH)
+                    parts = []
+                    for r, first, _ in found:
                         if isinstance(first, int):
-                            where = slice(first + start, first + start + count)
+                            where = slice(first + kv_first, first + kv_first + keys_in)
                         else:
-                            where = pl.ds(pl.multiple_of(first + start, BAND), count)
-                        parts.append(kv_refs[source][r][where, cols])
-                return jnp.concatenate(parts, axis=0)
-
-            def step(index, carry):
-                highest, total, mixed = carry
-                keys, values = column(index, 2 * head), column(index, 2 * head + 1)
+                            where = pl.ds(pl.multiple_of(first + kv_first, BAND), keys_in)
+                        parts.append(kv_refs[r][where, cols])
+                    return jnp.concatenate(parts, axis=0)
+
+                keys, values = column(2 * head), column(2 * head + 1)
                 scores = lax.dot_general(
                     queries, keys, (((1,), (1,)), ((), ())), preferred_element_type=jnp.float32
                 ) * factor
-                bias = []
-                for slot in slots:
-                    block = slot(place, index)[2]
-                    bias.append(
-                        jnp.where(
-                            (key_at + block * rows <= query_at) & block_allowed(doc, group, block),
-                            jnp.float32(0),
-                            -jnp.inf,
-                        )
+                key_at = jnp.zeros((1, span), jnp.int32)
+                for j, (_, _, block) in enumerate(found):
+                    shift = jnp.where(
+                        block_allowed(doc, group, block), block * rows + base - j * keys_in, 1 << 30
                     )
-                bias = jnp.concatenate(bias, axis=1)
+                    inside = (column_at >= j * keys_in) & (column_at < (j + 1) * keys_in)
+                    key_at = jnp.where(inside, column_at + shift, key_at)
+                bias = jnp.where(key_at <= query_at, jnp.float32(0), -jnp.inf)
                 scores = (scores.reshape(QUERY_GROUP, rows, span) + bias[None]).reshape(rank, span)
                 top = jnp.max(scores, axis=1, keepdims=True)
-                if chunks > 1:
-                    fresh = jnp.maximum(highest, top)
-                    safe = jnp.where(fresh == -jnp.inf, jnp.float32(0), fresh)
-                    fade = jnp.exp(highest - safe)
-                else:
-                    fresh = safe = top
+                if carry is None:
+                    raised = jnp.exp(scores - top)
+                    return (
+                        top,
+                        jnp.sum(raised, axis=1, keepdims=True),
+                        jnp.dot(
+                            raised.astype(jnp.bfloat16), values, preferred_element_type=jnp.float32
+                        ),
+                    )
+                highest, total, mixed = carry
+                fresh = jnp.maximum(highest, top)
+                safe = jnp.where(fresh == -jnp.inf, jnp.float32(0), fresh)
+                fade = jnp.exp(highest - safe)
                 raised = jnp.exp(scores - safe)
                 part = jnp.sum(raised, axis=1, keepdims=True)
                 product = jnp.dot(
                     raised.astype(jnp.bfloat16), values, preferred_element_type=jnp.float32
                 )
-                if chunks > 1:
-                    return fresh, total * fade + part, mixed * fade + product
-                return fresh, part, product
-
-            initial = (
-                jnp.full((rank, 1), -jnp.inf, jnp.float32),
-                jnp.zeros((rank, 1), jnp.float32),
-                jnp.zeros((rank, HEAD_WIDTH), jnp.float32),
-            )
+                return fresh, total * fade + part, mixed * fade + product
+
+            band = slice(head * rank, (head + 1) * rank)
+            carry = None
+            if not begin:
+                top_ref, total_ref, mixed_ref = state_refs[3 * lane:3 * lane + 3]
+                carry = (top_ref[band, :1], total_ref[band, :1], mixed_ref[band, :])
+            elif chunks > 1:
+                carry = (
+                    jnp.full((rank, 1), -jnp.inf, jnp.float32),
+                    jnp.zeros((rank, 1), jnp.float32),
+                    jnp.zeros((rank, HEAD_WIDTH), jnp.float32),
+                )
             if chunks > 1:
-                _, total, mixed = lax.fori_loop(0, chunks, step, initial)
+                carry = lax.fori_loop(0, chunks, step, carry)
             else:
-                _, total, mixed = step(0, initial)
+                carry = step(0, carry)
+            top, total, mixed = carry
+            if not end:
+                top_ref, total_ref, mixed_ref = out_refs[3 * lane:3 * lane + 3]
+                top_ref[band, :] = jnp.broadcast_to(top, (rank, HEAD_WIDTH))
+                total_ref[band, :] = jnp.broadcast_to(total, (rank, HEAD_WIDTH))
+                mixed_ref[band, :] = mixed
+                continue
             result = (mixed / total).astype(jnp.bfloat16)
             for h in range(QUERY_GROUP):
                 cols = slice(
@@ -347,17 +414,25 @@
                 out_refs[lane][:, cols] = result[h * rows:(h + 1) * rows]
 
 
-def attend(info, vertical, slash, lanes, queries, spreads):
+def attend(info, vertical, slash, lanes, queries, spread, states=None, end=True):
     q_cols = queries[0].shape[1]
     rows = sum(count for _, _, count in lanes[0][1])
-    span = len(spreads[0].slots) * spreads[0].chunks * rows
-    arrays = [array for spread in spreads for array in spread.arrays]
-    layout = [(len(spread.arrays), spread.slots, spread.chunks) for spread in spreads]
+    span = len(spread.slots) * spread.chunks * lanes[0][2][1]
+    arrays = spread.arrays
+    held = [array for state in states for array in state] if states else []
+    if end:
+        shapes = [jax.ShapeDtypeStruct((rows, q_cols), jnp.bfloat16)] * len(lanes)
+    else:
+        shape = (rows * q_cols // HEAD_WIDTH, HEAD_WIDTH)
+        shapes = [jax.ShapeDtypeStruct(shape, jnp.float32)] * (3 * len(lanes))
+    kernel = functools.partial(
+        attend_kernel, lanes, spread.slots, spread.chunks, len(queries), len(arrays), not states, end
+    )
     return pl.pallas_call(
-        functools.partial(attend_kernel, lanes, layout, len(queries)),
-        in_specs=[SMEM] * 3 + [VMEM] * (len(queries) + len(arrays)),
-        out_specs=[VMEM] * len(lanes),
-        out_shape=[jax.ShapeDtypeStruct((rows, q_cols), jnp.bfloat16)] * len(lanes),
+        kernel,
+        in_specs=[SMEM] * 3 + [VMEM] * (len(queries) + len(arrays) + len(held)),
+        out_specs=[VMEM] * len(shapes),
+        out_shape=shapes,
         compiler_params=pltpu.CompilerParams(vmem_limit_bytes=28 * MIB),
         cost_estimate=pl.CostEstimate(
             flops=4 * len(lanes) * rows * q_cols * span,
@@ -365,27 +440,34 @@
             transcendentals=len(lanes) * rows * span * q_cols // HEAD_WIDTH,
         ),
         name="attend",
-    )(info, vertical, slash, *queries, *arrays)
-
-
-def assemble_kernel(info_ref, *refs):
-    out_ref = refs[-1]
-    cols = refs[0].shape[1]
-    for mask, ref in enumerate(refs[:-1]):
-        at = pl.multiple_of((info_ref[1] ^ mask) * cols, cols)
-        out_ref[0, :, pl.ds(at, cols)] = ref[...]
-
-
-def assemble(info, *pieces):
+    )(info, vertical, slash, *queries, *arrays, *held)
+
+
+def deliver_kernel(masks, info_ref, *refs):
+    pieces, (out_ref, sems) = refs[:len(masks)], refs[-2:]
+    cols = pieces[0].shape[1]
+    copies = []
+    for at, (mask, piece) in enumerate(zip(masks, pieces)):
+        where = pl.ds(pl.multiple_of((info_ref[1] ^ mask) * cols, cols), cols)
+        copies.append(pltpu.make_async_copy(piece, out_ref.at[0, :, where], sems.at[at]))
+        copies[-1].start()
+    for copy in copies:
+        copy.wait()
+
+
+def deliver(info, masks, pieces, count, before=None):
     rows, cols = pieces[0].shape
+    begun = () if before is None else (before,)
     return pl.pallas_call(
-        assemble_kernel,
-        in_specs=[SMEM] + [VMEM] * len(pieces),
-        out_specs=VMEM,
-        out_shape=jax.ShapeDtypeStruct((1, rows, len(pieces) * cols), jnp.bfloat16),
+        functools.partial(deliver_kernel, masks),
+        in_specs=[SMEM] + [VMEM] * len(pieces) + [HBM] * len(begun),
+        out_specs=HBM,
+        out_shape=jax.ShapeDtypeStruct((1, rows, count * cols), jnp.bfloat16),
+        input_output_aliases={1 + len(pieces): 0} if begun else {},
+        scratch_shapes=[pltpu.SemaphoreType.DMA((len(pieces),))],
         compiler_params=pltpu.CompilerParams(vmem_limit_bytes=16 * MIB),
-        name="assemble",
-    )(info, *pieces)
+        name="deliver",
+    )(info, *pieces, *begun)
 
 
 def local(tokens, norm_gain, w_query, key_weight, value_weight, vertical_blocks, slash_offsets):
@@ -417,7 +499,9 @@
         early=True,
     )
     params = (gain_in, wq_in, wk_in, wv_in, table)
-    near = Ring(kv_near)
+    long = lax.axis_size("seq") > 8 or lax.axis_size("seq") % 2 == 1
+    ring, pairs = (Gathered, Gathered) if long else (Ring, Pairs)
+    near = ring(kv_near)
     near.advance()
     near.advance()
     got_head = after(got_head, *near.latest)
@@ -432,13 +516,13 @@
         [(0, head), (0, head)],
         *params,
     )
-    ring_head = Ring(kv_head)
-    ring_head.advance()
-
-    got_tail = after(got_tail, *near.latest, *ring_head.latest)
+    early = ring(kv_head)
+    early.advance()
+
+    got_tail = after(got_tail, *near.latest, *early.latest)
     near.advance()
     tail_twin = swap(got_tail, "doc", 1)
-    ring_head.advance()
+    early.advance()
     q_tail, kv_tail = project(
         info,
         [got_tail, tail_twin],
@@ -446,30 +530,45 @@
         [(head, tail), (head, tail)],
         *params,
     )
-    ring_tail = Ring(kv_tail)
-    ring_tail.advance()
+    late = pairs(kv_tail)
+    late.advance()
     mixed_own, mixed_twin = attend(
         *pattern,
-        [(lambda d: d, [(0, 0, rows)]), (lambda d: d ^ 1, [(0, rows, rows)])],
-        [after(q_near, *ring_tail.latest)],
-        [near],
+        [
+            (lambda d: d, [(0, 0, rows)], (0, rows, 0)),
+            (lambda d: d ^ 1, [(0, rows, rows)], (rows, rows, 0)),
+        ],
+        [after(q_near, kv_tail)],
+        near,
     )
     out_twin = swap(mixed_twin, "doc", 1)
-    ring_head.advance()
-    ring_tail.advance(mixed_twin)
-    ring_head.advance()
-    ring_tail.advance()
-    ring_tail.advance()
-    mixed = attend(
+    early.advance()
+    late.advance(mixed_twin)
+    early.advance()
+    late.advance()
+    late.advance()
+    remote = [
+        (lambda d: d ^ 2, [(0, 0, head), (1, 0, tail)]),
+        (lambda d: d ^ 3, [(0, head, head), (1, tail, tail)]),
+    ]
+    queries = [after(q_head, out_twin), q_tail]
+    states = attend(
         *pattern,
-        [
-            (lambda d: d ^ 2, [(0, 0, head), (1, 0, tail)]),
-            (lambda d: d ^ 3, [(0, head, head), (1, tail, tail)]),
-        ],
-        [after(q_head, out_twin), q_tail],
-        [ring_head, ring_tail],
-    )
-    return assemble(info, mixed_own, out_twin, swap(mixed[0], "doc", 2), swap(mixed[1], "doc", 3))
+        [lane + ((at * head, head, 0),) for at, lane in enumerate(remote)],
+        queries,
+        early,
+        end=False,
+    )
+    home = []
+    for at, lane in enumerate(remote):
+        state = states[3 * at:3 * at + 3]
+        (mixed,) = attend(
+            *pattern, [lane + ((at * tail, tail, head),)], queries, late, states=[state]
+        )
+        home.append(swap(mixed, "doc", 2 + at))
+    count = lax.axis_size("doc")
+    result = deliver(info, (0, 1), [mixed_own, out_twin], count)
+    return deliver(info, (2, 3), home, count, before=result)
 
 
 def solution(mesh):

time: 75.5 us -> 75.5 us (level)
  Pallas kernels: 19.1 us -> 24.8 us
  starting transfers between devices: 28.6 us -> 24.2 us
    ppermute x21 -> x14, starting transfers between devices: 23.1 us -> 15.8 us  [advance(): self.front[way] = lax.ppermute(value, 'seq', pairs)]
    ppermute x0 -> x4, waiting for transfers between devices: none -> 6.62 us  [advance(): got = lax.ppermute(value, 'seq', pairs)]
    ppermute x21 -> x14, waiting for transfers between devices: 15.5 us -> 9.76 us  [advance(): self.front[way] = lax.ppermute(value, 'seq', pairs)]
    pallas_call x3 -> x6, Pallas kernels: 7.54 us -> 13.2 us  [the longest x4 10.7 us: attend(): pl.pallas_call(kernel, in_specs=[SMEM] * 3 + [VMEM] * (len(queries) + len...]
    ppermute x0 -> x4, starting transfers between devices: none -> 2.8 us  [advance(): got = lax.ppermute(value, 'seq', pairs)]
    ppermute x8, waiting for transfers between devices: 10.6 us -> 9.01 us  [swap(): lax.ppermute(value, axis, [(source, source ^ mask) for source in range(co...]
  transfers between devices with their start and end apart: 29 -> 26, of which waited for: 10 -> 10; matrix products, arithmetic and copies ran while one was open for 1% -> 1% of each run, Pallas kernels for 20% -> 28%
where the time goes in v1:
time: 75.5 us; the launch traced here: 75.2 us
  waiting for transfers between devices  25.4 us (34%)
  Pallas kernels  24.8 us (33%)
  starting transfers between devices  24.2 us (32%)
    ppermute x14, starting transfers between devices, advance(): self.front[way] = lax.ppermute(value, 'seq', pairs)  15.8 us
    pallas_call x4, Pallas kernels, attend(): pl.pallas_call(kernel, in_specs=[SMEM] * 3 + [VMEM] * (len(queries) + len...  10.7 us
    pallas_call x3, Pallas kernels, project(): pl.pallas_call(functools.partial(project_kernel, places, table_rows, earl...  10.4 us
    ppermute x14, waiting for transfers between devices, advance(): self.front[way] = lax.ppermute(value, 'seq', pairs)  9.76 us
    ppermute x8, waiting for transfers between devices, swap(): lax.ppermute(value, axis, [(source, source ^ mask) for source in range(co...  9.01 us
    ppermute x4, waiting for transfers between devices, advance(): got = lax.ppermute(value, 'seq', pairs)  6.62 us
    ppermute x8, starting transfers between devices, swap(): lax.ppermute(value, axis, [(source, source ^ mask) for source in range(co...  5.53 us
    ppermute x4, starting transfers between devices, advance(): got = lax.ppermute(value, 'seq', pairs)  2.8 us
  transfers between devices with their start and end apart: 26, of which 10 were waited for; matrix products, arithmetic and copies ran while one was open for 1% of the time, Pallas kernels for 28%

profile of v1, /device:TPU:0, one launch (start us, length us, event | category | flops | bytes accessed | tf_op | source)
XLA Modules:
  0.0 75.2 jit_solution(7869591010772397359)
XLA Ops:
  0.5 1.2 %cut.1 = (bf16[96,4096]{1,0:T(8,128)(2,1)S(1)}, bf16[32,4096]{1,0:T(8,128)(2,1)S(1)}) custom-call(bf16[128,4096]{1,0:T(8,128)(2,1)} %bitcast.5), custom_call_target="tpu_custom_call" | custom-call | tf_op jit(solution)/shard_map/cut/pallas_call | solution.py:181
  1.7 2.6 %collective-permute-start = (bf16[96,4096]{1,0:T(8,128)(2,1)S(1)}, bf16[96,4096]{1,0:T(8,128)(2,1)S(1)}, u32[]{:S(2)}, u32[]{:S(2)}) collective-permute-start(bf16[96,4096]{1,0:T(8,128)(2,1)S(1)} %get-tuple-element.31), channel_id=1, source_target_pairs={{0,2},{1,3},{2,0},{3,1},{4,6},{5,7},{6,4},{7,5},{8,10},{9,11},{10,... | collective-permute-start | bytes 2359304 | tf_op jit(solution)/shard_map/ppermute | solution.py:26
  4.8 5.2 %project.3 = (bf16[256,512]{1,0:T(8,128)(2,1)S(1)}, bf16[256,256]{1,0:T(8,128)(2,1)S(1)}, f32[1,4096]{1,0:T(1,128)S(1)}, bf16[4096,128]{1,0:T(8,128)(2,1)S(1)}, ...) custom-call(s32[2]{0:T(128)S(1)} %pad_add_fusion.info_ref, bf16[128,4096]{1,0:T(8,128)(2,1)} %bitcast.6, ...), custom_call_target="tpu_custom_call" | custom-call | flops 1610612736 | bytes 8388608 | tf_op jit(solution)/shard_map/project/pallas_call | solution.py:152
  10.0 1.6 %collective-permute-start.2 = (bf16[256,256]{1,0:T(8,128)(2,1)S(1)}, bf16[256,256]{1,0:T(8,128)(2,1)S(1)}, u32[]{:S(2)}, u32[]{:S(2)}) collective-permute-start(bf16[256,256]{1,0:T(8,128)(2,1)S(1)} %get-tuple-element.32.refs_1_), channel_id=1, source_target_pairs={{0,8},{8,16},{16,24},{24,28},{28,20},{20,12},{12,4},{4,0},{1,9},{9... | collective-permute-start | bytes 393224 | tf_op jit(solution)/shard_map/ppermute | solution.py:254
  12.0 3.6 %collective-permute-done.2.refs_2_ = bf16[256,256]{1,0:T(8,128)(2,1)S(1)} collective-permute-done((bf16[256,256]{1,0:T(8,128)(2,1)S(1)}, bf16[256,256]{1,0:T(8,128)(2,1)S(1)}, u32[]{:S(2)}, u32[]{:S(2)}) %collective-permute-start.2) | collective-permute-done | bytes 131104 | tf_op jit(solution)/shard_map/ppermute | solution.py:254
  15.6 1.6 %collective-permute-start.3 = (bf16[256,256]{1,0:T(8,128)(2,1)S(1)}, bf16[256,256]{1,0:T(8,128)(2,1)S(1)}, u32[]{:S(2)}, u32[]{:S(2)}) collective-permute-start(bf16[256,256]{1,0:T(8,128)(2,1)S(1)} %collective-permute-done.2.refs_2_), channel_id=1, source_target_pairs={{0,8},{8,16},{16,24},{24,28},{28,20},{20,12},{12,4},{4,0},{1,9},{9... | collective-permute-start | bytes 393224 | tf_op jit(solution)/shard_map/ppermute | solution.py:254
  17.7 4.8 %collective-permute-done.refs_0_ = bf16[96,4096]{1,0:T(8,128)(2,1)S(1)} collective-permute-done((bf16[96,4096]{1,0:T(8,128)(2,1)S(1)}, bf16[96,4096]{1,0:T(8,128)(2,1)S(1)}, u32[]{:S(2)}, u32[]{:S(2)}) %collective-permute-start) | collective-permute-done | bytes 786464 | tf_op jit(solution)/shard_map/ppermute | solution.py:26
  22.4 1.8 %collective-permute-start.7 = (bf16[32,4096]{1,0:T(8,128)(2,1)S(1)}, bf16[32,4096]{1,0:T(8,128)(2,1)S(1)}, u32[]{:S(2)}, u32[]{:S(2)}) collective-permute-start(bf16[32,4096]{1,0:T(8,128)(2,1)S(1)} %get-tuple-element.41), channel_id=1, source_target_pairs={{0,2},{1,3},{2,0},{3,1},{4,6},{5,7},{6,4},{7,5},{8,10},{9,11},{10,... | collective-permute-start | bytes 786440 | tf_op jit(solution)/shard_map/ppermute | solution.py:26
  24.3 1.6 %collective-permute-start.8 = (bf16[256,256]{1,0:T(8,128)(2,1)S(1)}, bf16[256,256]{1,0:T(8,128)(2,1)S(1)}, u32[]{:S(2)}, u32[]{:S(2)}) collective-permute-start(bf16[256,256]{1,0:T(8,128)(2,1)S(1)} %collective-permute-done.3.refs_4_), channel_id=1, source_target_pairs={{0,8},{8,16},{16,24},{24,28},{28,20},{20,12},{12,4},{4,0},{1,9},{9... | collective-permute-start | bytes 393224 | tf_op jit(solution)/shard_map/ppermute | solution.py:254
  26.3 3.2 %project.4 = (bf16[192,512]{1,0:T(8,128)(2,1)S(1)}, bf16[192,256]{1,0:T(8,128)(2,1)S(1)}) custom-call(s32[2]{0:T(128)S(1)} %pad_add_fusion.info_ref, bf16[96,4096]{1,0:T(8,128)(2,1)S(1)} %collective-permute-done.refs_0_, bf16[96,4096]{1,0:T(8,128)(2,1)S(1)} %collective-permute-done.6.refs_1_, f32[1,4096]{1,0:T(1,128)S(1)} %get-tuple-element.34.refs_2_, ...), custom_call_target="tpu_custom_call" | custom-call | flops 1207959552 | bytes 7864320 | tf_op jit(solution)/shard_map/project/pallas_call | solution.py:152
  29.5 1.6 %collective-permute-start.10 = (bf16[192,256]{1,0:T(8,128)(2,1)S(1)}, bf16[192,256]{1,0:T(8,128)(2,1)S(1)}, u32[]{:S(2)}, u32[]{:S(2)}) collective-permute-start(bf16[192,256]{1,0:T(8,128)(2,1)S(1)} %get-tuple-element.42.refs_2_), channel_id=1, source_target_pairs={{0,8},{8,16},{16,24},{24,28},{28,20},{20,12},{12,4},{4,0},{1,9},{9... | collective-permute-start | bytes 294920 | tf_op jit(solution)/shard_map/ppermute | solution.py:254
  31.6 2.6 %collective-permute-done.10.refs_3_ = bf16[192,256]{1,0:T(8,128)(2,1)S(1)} collective-permute-done((bf16[192,256]{1,0:T(8,128)(2,1)S(1)}, bf16[192,256]{1,0:T(8,128)(2,1)S(1)}, u32[]{:S(2)}, u32[]{:S(2)}) %collective-permute-start.10) | collective-permute-done | bytes 98336 | tf_op jit(solution)/shard_map/ppermute | solution.py:254
  34.2 1.6 %collective-permute-done.11.refs_4_ = bf16[192,256]{1,0:T(8,128)(2,1)S(1)} collective-permute-done((bf16[192,256]{1,0:T(8,128)(2,1)S(1)}, bf16[192,256]{1,0:T(8,128)(2,1)S(1)}, u32[]{:S(2)}, u32[]{:S(2)}) %collective-permute-start.11) | collective-permute-done | bytes 98336 | tf_op jit(solution)/shard_map/ppermute | solution.py:254
  35.8 1.6 %collective-permute-start.19 = (bf16[192,256]{1,0:T(8,128)(2,1)S(1)}, bf16[192,256]{1,0:T(8,128)(2,1)S(1)}, u32[]{:S(2)}, u32[]{:S(2)}) collective-permute-start(bf16[192,256]{1,0:T(8,128)(2,1)S(1)} %collective-permute-done.10.refs_3_), channel_id=1, source_target_pairs={{0,8},{8,16},{16,24},{24,28},{28,20},{20,12},{12,4},{4,0},{1,9},{9... | collective-permute-start | bytes 294920 | tf_op jit(solution)/shard_map/ppermute | solution.py:254
  37.4 1.6 %collective-permute-start.13 = (bf16[256,256]{1,0:T(8,128)(2,1)S(1)}, bf16[256,256]{1,0:T(8,128)(2,1)S(1)}, u32[]{:S(2)}, u32[]{:S(2)}) collective-permute-start(bf16[256,256]{1,0:T(8,128)(2,1)S(1)} %collective-permute-done.8.refs_6_), channel_id=1, source_target_pairs={{0,8},{8,16},{16,24},{24,28},{28,20},{20,12},{12,4},{4,0},{1,9},{9... | collective-permute-start | bytes 393224 | tf_op jit(solution)/shard_map/ppermute | solution.py:254
  39.4 2.0 %collective-permute-done.19.refs_5_ = bf16[192,256]{1,0:T(8,128)(2,1)S(1)} collective-permute-done((bf16[192,256]{1,0:T(8,128)(2,1)S(1)}, bf16[192,256]{1,0:T(8,128)(2,1)S(1)}, u32[]{:S(2)}, u32[]{:S(2)}) %collective-permute-start.19) | collective-permute-done | bytes 98336 | tf_op jit(solution)/shard_map/ppermute | solution.py:254
  41.4 1.6 %collective-permute-start.21 = (bf16[192,256]{1,0:T(8,128)(2,1)S(1)}, bf16[192,256]{1,0:T(8,128)(2,1)S(1)}, u32[]{:S(2)}, u32[]{:S(2)}) collective-permute-start(bf16[192,256]{1,0:T(8,128)(2,1)S(1)} %collective-permute-done.19.refs_5_), channel_id=1, source_target_pairs={{0,8},{8,16},{16,24},{24,28},{28,20},{20,12},{12,4},{4,0},{1,9},{9... | collective-permute-start | bytes 294920 | tf_op jit(solution)/shard_map/ppermute | solution.py:254
  42.9 2.0 %project.5 = (bf16[64,512]{1,0:T(8,128)(2,1)S(1)}, bf16[64,256]{1,0:T(8,128)(2,1)S(1)}) custom-call(s32[2]{0:T(128)S(1)} %pad_add_fusion.info_ref, bf16[32,4096]{1,0:T(8,128)(2,1)S(1)} %collective-permute-done.7.refs_0_, bf16[32,4096]{1,0:T(8,128)(2,1)S(1)} %collective-permute-done.12.refs_1_, f32[1,4096]{1,0:T(1,128)S(1)} %get-tuple-element.34.refs_2_, ...), custom_call_target="tpu_custom_call" | custom-call | flops 402653184 | bytes 6815744 | tf_op jit(solution)/shard_map/project/pallas_call | solution.py:152
  45.0 1.6 %collective-permute-start.15 = (bf16[64,256]{1,0:T(8,128)(2,1)S(1)}, bf16[64,256]{1,0:T(8,128)(2,1)S(1)}, u32[]{:S(2)}, u32[]{:S(2)}) collective-permute-start(bf16[64,256]{1,0:T(8,128)(2,1)S(1)} %get-tuple-element.44.refs_2_), channel_id=1, source_target_pairs={{0,8},{8,0},{16,24},{24,16},{28,20},{20,28},{12,4},{4,12},{1,9},{9... | collective-permute-start | bytes 98312 | tf_op jit(solution)/shard_map/ppermute | solution.py:290
  46.6 3.1 %attend.4 = (bf16[128,512]{1,0:T(8,128)(2,1)S(1)}, bf16[128,512]{1,0:T(8,128)(2,1)S(1)}) custom-call(s32[2]{0:T(128)S(1)} %pad_add_fusion.info_ref, s32[4,4,4]{2,1,0:T(4,128)S(1)} %copy-done, s32[4,4,4]{2,1,0:T(4,128)S(1)} %copy-done.1, bf16[256,512]{1,0:T(8,128)(2,1)S(1)} %get-tuple-element.45.refs_0_, bf16[256,256]{1,0:T(8,128)(2,1)S(1)} %get-tuple-element.32.refs_1_, ...), custom_call_target="tpu_custom_call" | custom-call | flops 536870912 | bytes 1572864 | tf_op jit(solution)/shard_map/attend/pallas_call | solution.py:431
  49.9 1.9 %collective-permute-start.22 = (bf16[192,256]{1,0:T(8,128)(2,1)S(1)}, bf16[192,256]{1,0:T(8,128)(2,1)S(1)}, u32[]{:S(2)}, u32[]{:S(2)}) collective-permute-start(bf16[192,256]{1,0:T(8,128)(2,1)S(1)} %collective-permute-done.20.refs_6_), channel_id=1, source_target_pairs={{0,4},{8,0},{16,8},{24,16},{28,24},{20,28},{12,20},{4,12},{1,5},{9... | collective-permute-start | bytes 294920 | tf_op jit(solution)/shard_map/ppermute | solution.py:254
  52.3 1.7 %collective-permute-done.16.refs_4_ = bf16[128,256]{1,0:T(8,128)(2,1)S(1)} collective-permute-done((bf16[128,256]{1,0:T(8,128)(2,1)S(1)}, bf16[128,256]{1,0:T(8,128)(2,1)S(1)}, u32[]{:S(2)}, u32[]{:S(2)}) %collective-permute-start.16) | collective-permute-done | bytes 65568 | tf_op jit(solution)/shard_map/ppermute | solution.py:290
  54.0 0.7 collective-permute-start.17
  54.8 3.5 %collective-permute-done.17.refs_5_ = bf16[128,256]{1,0:T(8,128)(2,1)S(1)} collective-permute-done((bf16[128,256]{1,0:T(8,128)(2,1)S(1)}, bf16[128,256]{1,0:T(8,128)(2,1)S(1)}, u32[]{:S(2)}, u32[]{:S(2)}) %collective-permute-start.17) | collective-permute-done | bytes 65568 | tf_op jit(solution)/shard_map/ppermute | solution.py:290
  58.7 2.5 %attend.5 = (f32[512,128]{1,0:T(8,128)S(1)}, f32[512,128]{1,0:T(8,128)S(1)}, f32[512,128]{1,0:T(8,128)S(1)}, f32[512,128]{1,0:T(8,128)S(1)}, f32[512,128]{1,0:T(8,128)S(1)}, /*index=5*/f32[512,128]{1,0:T(8,128)S(1)}) custom-call(s32[2]{0:T(128)S(1)} %pad_add_fusion.info_ref, s32[4,4,4]{2,1,0:T(4,128)S(1)} %copy-done, s32[4,4,4]{2,1,0:T(4,128)S(1)} %copy-done.1, ...), custom_call_target="tpu_custom_call" | custom-call | flops 402653184 | bytes 1310720 | tf_op jit(solution)/shard_map/attend/pallas_call | solution.py:431
  61.2 1.4 %collective-permute-done.18.refs_6_ = bf16[128,256]{1,0:T(8,128)(2,1)S(1)} collective-permute-done((bf16[128,256]{1,0:T(8,128)(2,1)S(1)}, bf16[128,256]{1,0:T(8,128)(2,1)S(1)}, u32[]{:S(2)}, u32[]{:S(2)}) %collective-permute-start.18) | collective-permute-done | bytes 65568 | tf_op jit(solution)/shard_map/ppermute | solution.py:290
  62.6 2.5 %attend.7 = bf16[128,512]{1,0:T(8,128)(2,1)S(1)} custom-call(s32[2]{0:T(128)S(1)} %pad_add_fusion.info_ref, s32[4,4,4]{2,1,0:T(4,128)S(1)} %copy-done, s32[4,4,4]{2,1,0:T(4,128)S(1)} %copy-done.1, bf16[192,512]{1,0:T(8,128)(2,1)S(1)} %get-tuple-element.47.refs_0_, bf16[64,512]{1,0:T(8,128)(2,1)S(1)} %get-tuple-element.48.refs_1_, ...), custom_call_target="tpu_custom_call" | custom-call | flops 67108864 | bytes 524288 | tf_op jit(solution)/shard_map/attend/pallas_call | solution.py:431
  65.2 2.6 %attend.6 = bf16[128,512]{1,0:T(8,128)(2,1)S(1)} custom-call(s32[2]{0:T(128)S(1)} %pad_add_fusion.info_ref, s32[4,4,4]{2,1,0:T(4,128)S(1)} %copy-done, s32[4,4,4]{2,1,0:T(4,128)S(1)} %copy-done.1, bf16[192,512]{1,0:T(8,128)(2,1)S(1)} %get-tuple-element.47.refs_0_, bf16[64,512]{1,0:T(8,128)(2,1)S(1)} %get-tuple-element.48.refs_1_, ...), custom_call_target="tpu_custom_call" | custom-call | flops 67108864 | bytes 524288 | tf_op jit(solution)/shard_map/attend/pallas_call | solution.py:431
  67.7 0.6 collective-permute-start.24
  68.3 1.3 %deliver.2.refs_2_ = bf16[1,128,2048]{2,1,0:T(8,128)(2,1)} custom-call(s32[2]{0:T(128)S(1)} %pad_add_fusion.info_ref, bf16[128,512]{1,0:T(8,128)(2,1)S(1)} %get-tuple-element.56.refs_0_, bf16[128,512]{1,0:T(8,128)(2,1)S(1)} %collective-permute-done.14.refs_1_), custom_call_target="tpu_custom_call" | custom-call | tf_op jit(solution)/shard_map/deliver/pallas_call | solution.py:461
  70.1 3.8 %collective-permute-done.24.refs_0_ = bf16[128,512]{1,0:T(8,128)(2,1)S(1)} collective-permute-done((bf16[128,512]{1,0:T(8,128)(2,1)S(1)}, bf16[128,512]{1,0:T(8,128)(2,1)S(1)}, u32[]{:S(2)}, u32[]{:S(2)}) %collective-permute-start.24) | collective-permute-done | bytes 131104 | tf_op jit(solution)/shard_map/ppermute | solution.py:26
  73.8 1.3 %deliver.3 = bf16[1,128,2048]{2,1,0:T(8,128)(2,1)} custom-call(s32[2]{0:T(128)S(1)} %pad_add_fusion.info_ref, bf16[128,512]{1,0:T(8,128)(2,1)S(1)} %collective-permute-done.24.refs_0_, bf16[128,512]{1,0:T(8,128)(2,1)S(1)} %collective-permute-done.25.refs_1_, bf16[1,128,2048]{2,1,0:T(8,128)(2,1)} %deliver.2.refs_2_), custom_call_target="tpu_custom_call", output_to_operand_aliasing={{}: (3, {})} | custom-call | tf_op jit(solution)/shard_map/deliver/pallas_call | solution.py:461
  (40 shorter events, 4.8 us)
Async XLA Ops:
  0.0 4.8 %collective-permute-start.1 = (bf16[128,4096]{1,0:T(8,128)(2,1)}, bf16[128,4096]{1,0:T(8,128)(2,1)S(1)}, u32[]{:S(2)}, u32[]{:S(2)}) collective-permute-start(bf16[128,4096]{1,0:T(8,128)(2,1)} %bitcast.4), channel_id=1, source_target_pairs={{0,1},{1,0},{2,3},{3,2},{4,5},{5,4},{6,7},{7,6},{8,9},{9,8},{10,11... | collective-permute-start | bytes 3145736 | tf_op jit(solution)/shard_map/ppermute | solution.py:26
  1.7 20.8 %collective-permute-start = (bf16[96,4096]{1,0:T(8,128)(2,1)S(1)}, bf16[96,4096]{1,0:T(8,128)(2,1)S(1)}, u32[]{:S(2)}, u32[]{:S(2)}) collective-permute-start(bf16[96,4096]{1,0:T(8,128)(2,1)S(1)} %get-tuple-element.31), channel_id=1, source_target_pairs={{0,2},{1,3},{2,0},{3,1},{4,6},{5,7},{6,4},{7,5},{8,10},{9,11},{10,... | collective-permute-start | bytes 2359304 | tf_op jit(solution)/shard_map/ppermute | solution.py:26
  10.0 5.7 %collective-permute-start.2 = (bf16[256,256]{1,0:T(8,128)(2,1)S(1)}, bf16[256,256]{1,0:T(8,128)(2,1)S(1)}, u32[]{:S(2)}, u32[]{:S(2)}) collective-permute-start(bf16[256,256]{1,0:T(8,128)(2,1)S(1)} %get-tuple-element.32.refs_1_), channel_id=1, source_target_pairs={{0,8},{8,16},{16,24},{24,28},{28,20},{20,12},{12,4},{4,0},{1,9},{9... | collective-permute-start | bytes 393224 | tf_op jit(solution)/shard_map/ppermute | solution.py:254
  11.6 5.6 %collective-permute-start.4 = (bf16[256,256]{1,0:T(8,128)(2,1)S(1)}, bf16[256,256]{1,0:T(8,128)(2,1)S(1)}, u32[]{:S(2)}, u32[]{:S(2)}) collective-permute-start(bf16[256,256]{1,0:T(8,128)(2,1)S(1)} %get-tuple-element.32.refs_1_), channel_id=1, source_target_pairs={{0,4},{8,0},{16,8},{24,16},{28,24},{20,28},{12,20},{4,12},{1,5},{9... | collective-permute-start | bytes 393224 | tf_op jit(solution)/shard_map/ppermute | solution.py:254
  15.6 6.8 %collective-permute-start.3 = (bf16[256,256]{1,0:T(8,128)(2,1)S(1)}, bf16[256,256]{1,0:T(8,128)(2,1)S(1)}, u32[]{:S(2)}, u32[]{:S(2)}) collective-permute-start(bf16[256,256]{1,0:T(8,128)(2,1)S(1)} %collective-permute-done.2.refs_2_), channel_id=1, source_target_pairs={{0,8},{8,16},{16,24},{24,28},{28,20},{20,12},{12,4},{4,0},{1,9},{9... | collective-permute-start | bytes 393224 | tf_op jit(solution)/shard_map/ppermute | solution.py:254
  17.2 5.2 %collective-permute-start.5 = (bf16[256,256]{1,0:T(8,128)(2,1)S(1)}, bf16[256,256]{1,0:T(8,128)(2,1)S(1)}, u32[]{:S(2)}, u32[]{:S(2)}) collective-permute-start(bf16[256,256]{1,0:T(8,128)(2,1)S(1)} %collective-permute-done.4.refs_3_), channel_id=1, source_target_pairs={{0,4},{8,0},{16,8},{24,16},{28,24},{20,28},{12,20},{4,12},{1,5},{9... | collective-permute-start | bytes 393224 | tf_op jit(solution)/shard_map/ppermute | solution.py:254
  22.4 3.8 %collective-permute-start.6 = (bf16[96,4096]{1,0:T(8,128)(2,1)S(1)}, bf16[96,4096]{1,0:T(8,128)(2,1)S(1)}, u32[]{:S(2)}, u32[]{:S(2)}) collective-permute-start(bf16[96,4096]{1,0:T(8,128)(2,1)S(1)} %collective-permute-done.refs_0_), channel_id=1, source_target_pairs={{0,1},{1,0},{2,3},{3,2},{4,5},{5,4},{6,7},{7,6},{8,9},{9,8},{10,11... | collective-permute-start | bytes 2359304 | tf_op jit(solution)/shard_map/ppermute | solution.py:26
  22.4 9.1 %collective-permute-start.7 = (bf16[32,4096]{1,0:T(8,128)(2,1)S(1)}, bf16[32,4096]{1,0:T(8,128)(2,1)S(1)}, u32[]{:S(2)}, u32[]{:S(2)}) collective-permute-start(bf16[32,4096]{1,0:T(8,128)(2,1)S(1)} %get-tuple-element.41), channel_id=1, source_target_pairs={{0,2},{1,3},{2,0},{3,1},{4,6},{5,7},{6,4},{7,5},{8,10},{9,11},{10,... | collective-permute-start | bytes 786440 | tf_op jit(solution)/shard_map/ppermute | solution.py:26
  24.3 7.3 %collective-permute-start.8 = (bf16[256,256]{1,0:T(8,128)(2,1)S(1)}, bf16[256,256]{1,0:T(8,128)(2,1)S(1)}, u32[]{:S(2)}, u32[]{:S(2)}) collective-permute-start(bf16[256,256]{1,0:T(8,128)(2,1)S(1)} %collective-permute-done.3.refs_4_), channel_id=1, source_target_pairs={{0,8},{8,16},{16,24},{24,28},{28,20},{20,12},{12,4},{4,0},{1,9},{9... | collective-permute-start | bytes 393224 | tf_op jit(solution)/shard_map/ppermute | solution.py:254
  25.8 5.8 %collective-permute-start.9 = (bf16[256,256]{1,0:T(8,128)(2,1)S(1)}, bf16[256,256]{1,0:T(8,128)(2,1)S(1)}, u32[]{:S(2)}, u32[]{:S(2)}) collective-permute-start(bf16[256,256]{1,0:T(8,128)(2,1)S(1)} %collective-permute-done.5.refs_5_), channel_id=1, source_target_pairs={{0,4},{8,0},{16,8},{24,16},{28,24},{20,28},{12,20},{4,12},{1,5},{9... | collective-permute-start | bytes 393224 | tf_op jit(solution)/shard_map/ppermute | solution.py:254
  29.5 17.1 %copy-start = (s32[4,4,4]{2,1,0:T(4,128)S(1)}, s32[4,4,4]{2,1,0:T(4,128)}, u32[]{:S(2)}) copy-start(s32[4,4,4]{2,1,0:T(4,128)} %vertical_ref.7) | copy-start | bytes 772
  29.5 17.1 %copy-start.1 = (s32[4,4,4]{2,1,0:T(4,128)S(1)}, s32[4,4,4]{2,1,0:T(4,128)}, u32[]{:S(2)}) copy-start(s32[4,4,4]{2,1,0:T(4,128)} %slash_ref.7) | copy-start | bytes 772
  29.5 4.7 %collective-permute-start.10 = (bf16[192,256]{1,0:T(8,128)(2,1)S(1)}, bf16[192,256]{1,0:T(8,128)(2,1)S(1)}, u32[]{:S(2)}, u32[]{:S(2)}) collective-permute-start(bf16[192,256]{1,0:T(8,128)(2,1)S(1)} %get-tuple-element.42.refs_2_), channel_id=1, source_target_pairs={{0,8},{8,16},{16,24},{24,28},{28,20},{20,12},{12,4},{4,0},{1,9},{9... | collective-permute-start | bytes 294920 | tf_op jit(solution)/shard_map/ppermute | solution.py:254
  31.1 4.6 %collective-permute-start.11 = (bf16[192,256]{1,0:T(8,128)(2,1)S(1)}, bf16[192,256]{1,0:T(8,128)(2,1)S(1)}, u32[]{:S(2)}, u32[]{:S(2)}) collective-permute-start(bf16[192,256]{1,0:T(8,128)(2,1)S(1)} %get-tuple-element.42.refs_2_), channel_id=1, source_target_pairs={{0,4},{8,0},{16,8},{24,16},{28,24},{20,28},{12,20},{4,12},{1,5},{9... | collective-permute-start | bytes 294920 | tf_op jit(solution)/shard_map/ppermute | solution.py:254
  35.8 7.2 %collective-permute-start.12 = (bf16[32,4096]{1,0:T(8,128)(2,1)S(1)}, bf16[32,4096]{1,0:T(8,128)(2,1)S(1)}, u32[]{:S(2)}, u32[]{:S(2)}) collective-permute-start(bf16[32,4096]{1,0:T(8,128)(2,1)S(1)} %collective-permute-done.7.refs_0_), channel_id=1, source_target_pairs={{0,1},{1,0},{2,3},{3,2},{4,5},{5,4},{6,7},{7,6},{8,9},{9,8},{10,11... | collective-permute-start | bytes 786440 | tf_op jit(solution)/shard_map/ppermute | solution.py:26
  35.8 5.6 %collective-permute-start.19 = (bf16[192,256]{1,0:T(8,128)(2,1)S(1)}, bf16[192,256]{1,0:T(8,128)(2,1)S(1)}, u32[]{:S(2)}, u32[]{:S(2)}) collective-permute-start(bf16[192,256]{1,0:T(8,128)(2,1)S(1)} %collective-permute-done.10.refs_3_), channel_id=1, source_target_pairs={{0,8},{8,16},{16,24},{24,28},{28,20},{20,12},{12,4},{4,0},{1,9},{9... | collective-permute-start | bytes 294920 | tf_op jit(solution)/shard_map/ppermute | solution.py:254
  37.4 9.2 %collective-permute-start.13 = (bf16[256,256]{1,0:T(8,128)(2,1)S(1)}, bf16[256,256]{1,0:T(8,128)(2,1)S(1)}, u32[]{:S(2)}, u32[]{:S(2)}) collective-permute-start(bf16[256,256]{1,0:T(8,128)(2,1)S(1)} %collective-permute-done.8.refs_6_), channel_id=1, source_target_pairs={{0,8},{8,16},{16,24},{24,28},{28,20},{20,12},{12,4},{4,0},{1,9},{9... | collective-permute-start | bytes 393224 | tf_op jit(solution)/shard_map/ppermute | solution.py:254
  38.9 10.9 %collective-permute-start.20 = (bf16[192,256]{1,0:T(8,128)(2,1)S(1)}, bf16[192,256]{1,0:T(8,128)(2,1)S(1)}, u32[]{:S(2)}, u32[]{:S(2)}) collective-permute-start(bf16[192,256]{1,0:T(8,128)(2,1)S(1)} %collective-permute-done.11.refs_4_), channel_id=1, source_target_pairs={{0,4},{8,0},{16,8},{24,16},{28,24},{20,28},{12,20},{4,12},{1,5},{9... | collective-permute-start | bytes 294920 | tf_op jit(solution)/shard_map/ppermute | solution.py:254
  41.4 10.5 %collective-permute-start.21 = (bf16[192,256]{1,0:T(8,128)(2,1)S(1)}, bf16[192,256]{1,0:T(8,128)(2,1)S(1)}, u32[]{:S(2)}, u32[]{:S(2)}) collective-permute-start(bf16[192,256]{1,0:T(8,128)(2,1)S(1)} %collective-permute-done.19.refs_5_), channel_id=1, source_target_pairs={{0,8},{8,16},{16,24},{24,28},{28,20},{20,12},{12,4},{4,0},{1,9},{9... | collective-permute-start | bytes 294920 | tf_op jit(solution)/shard_map/ppermute | solution.py:254
  45.0 4.7 %collective-permute-start.15 = (bf16[64,256]{1,0:T(8,128)(2,1)S(1)}, bf16[64,256]{1,0:T(8,128)(2,1)S(1)}, u32[]{:S(2)}, u32[]{:S(2)}) collective-permute-start(bf16[64,256]{1,0:T(8,128)(2,1)S(1)} %get-tuple-element.44.refs_2_), channel_id=1, source_target_pairs={{0,8},{8,0},{16,24},{24,16},{28,20},{20,28},{12,4},{4,12},{1,9},{9... | collective-permute-start | bytes 98312 | tf_op jit(solution)/shard_map/ppermute | solution.py:290
  49.7 4.3 %collective-permute-start.16 = (bf16[128,256]{1,0:T(8,128)(2,1)S(1)}, bf16[128,256]{1,0:T(8,128)(2,1)S(1)}, u32[]{:S(2)}, u32[]{:S(2)}) collective-permute-start(bf16[128,256]{1,0:T(8,128)(2,1)S(1)} %pad_maximum_fusion.1), channel_id=1, source_target_pairs={{0,4},{8,16},{16,8},{24,28},{28,24},{20,12},{12,20},{4,0},{1,5},{9... | collective-permute-start | bytes 196616 | tf_op jit(solution)/shard_map/ppermute | solution.py:290
  49.8 8.9 %collective-permute-start.14 = (bf16[128,512]{1,0:T(8,128)(2,1)S(1)}, bf16[128,512]{1,0:T(8,128)(2,1)S(1)}, u32[]{:S(2)}, u32[]{:S(2)}) collective-permute-start(bf16[128,512]{1,0:T(8,128)(2,1)S(1)} %get-tuple-element.46), channel_id=1, source_target_pairs={{0,1},{1,0},{2,3},{3,2},{4,5},{5,4},{6,7},{7,6},{8,9},{9,8},{10,11... | collective-permute-start | bytes 393224 | tf_op jit(solution)/shard_map/ppermute | solution.py:26
  49.9 8.8 %collective-permute-start.22 = (bf16[192,256]{1,0:T(8,128)(2,1)S(1)}, bf16[192,256]{1,0:T(8,128)(2,1)S(1)}, u32[]{:S(2)}, u32[]{:S(2)}) collective-permute-start(bf16[192,256]{1,0:T(8,128)(2,1)S(1)} %collective-permute-done.20.refs_6_), channel_id=1, source_target_pairs={{0,4},{8,0},{16,8},{24,16},{28,24},{20,28},{12,20},{4,12},{1,5},{9... | collective-permute-start | bytes 294920 | tf_op jit(solution)/shard_map/ppermute | solution.py:254
  51.8 6.9 %collective-permute-start.23 = (bf16[192,256]{1,0:T(8,128)(2,1)S(1)}, bf16[192,256]{1,0:T(8,128)(2,1)S(1)}, u32[]{:S(2)}, u32[]{:S(2)}) collective-permute-start(bf16[192,256]{1,0:T(8,128)(2,1)S(1)} %collective-permute-done.21.refs_7_), channel_id=1, source_target_pairs={{0,8},{8,16},{16,24},{24,28},{28,20},{20,12},{12,4},{4,0},{1,9},{9... | collective-permute-start | bytes 294920 | tf_op jit(solution)/shard_map/ppermute | solution.py:254
  54.0 4.3 %collective-permute-start.17 = (bf16[128,256]{1,0:T(8,128)(2,1)S(1)}, bf16[128,256]{1,0:T(8,128)(2,1)S(1)}, u32[]{:S(2)}, u32[]{:S(2)}) collective-permute-start(bf16[128,256]{1,0:T(8,128)(2,1)S(1)} %collective-permute-done.16.refs_4_), channel_id=1, source_target_pairs={{0,8},{8,0},{16,24},{24,16},{28,20},{20,28},{12,4},{4,12},{1,9},{9... | collective-permute-start | bytes 196616 | tf_op jit(solution)/shard_map/ppermute | solution.py:290
  58.3 4.3 %collective-permute-start.18 = (bf16[128,256]{1,0:T(8,128)(2,1)S(1)}, bf16[128,256]{1,0:T(8,128)(2,1)S(1)}, u32[]{:S(2)}, u32[]{:S(2)}) collective-permute-start(bf16[128,256]{1,0:T(8,128)(2,1)S(1)} %collective-permute-done.17.refs_5_), channel_id=1, source_target_pairs={{0,4},{8,16},{16,8},{24,28},{28,24},{20,12},{12,20},{4,0},{1,5},{9... | collective-permute-start | bytes 196616 | tf_op jit(solution)/shard_map/ppermute | solution.py:290
  65.1 4.9 %collective-permute-start.25 = (bf16[128,512]{1,0:T(8,128)(2,1)S(1)}, bf16[128,512]{1,0:T(8,128)(2,1)S(1)}, u32[]{:S(2)}, u32[]{:S(2)}) collective-permute-start(bf16[128,512]{1,0:T(8,128)(2,1)S(1)} %attend.7), channel_id=1, source_target_pairs={{0,3},{1,2},{2,1},{3,0},{4,7},{5,6},{6,5},{7,4},{8,11},{9,10},{10,... | collective-permute-start | bytes 393224 | tf_op jit(solution)/shard_map/ppermute | solution.py:26
  67.7 6.1 %collective-permute-start.24 = (bf16[128,512]{1,0:T(8,128)(2,1)S(1)}, bf16[128,512]{1,0:T(8,128)(2,1)S(1)}, u32[]{:S(2)}, u32[]{:S(2)}) collective-permute-start(bf16[128,512]{1,0:T(8,128)(2,1)S(1)} %attend.6), channel_id=1, source_target_pairs={{0,2},{1,3},{2,0},{3,1},{4,6},{5,7},{6,4},{7,5},{8,10},{9,11},{10,... | collective-permute-start | bytes 393224 | tf_op jit(solution)/shard_map/ppermute | solution.py:26

commit v2 on v1

--- a/solution.py
+++ b/solution.py
@@ -14,6 +14,7 @@
 EPSILON = 1e-05
 BAND = 16
 MIB = 1024 * 1024
+OUT_OF_REACH = 1 << 30
 
 SMEM = pl.BlockSpec(memory_space=pltpu.SMEM)
 VMEM = pl.BlockSpec(memory_space=pltpu.VMEM)
@@ -193,16 +194,9 @@
     return list(range(0, count, 2)) + list(range(count - 1, 0, -2))
 
 
-def ring_place(place, count):
-    return jnp.where(place % 2 == 0, place // 2, count - 1 - place // 2)
-
-
-def ring_block(at, count):
-    at = (at + count) % count
-    return jnp.where(at < count // 2, 2 * at, 2 * (count - 1 - at) + 1)
-
-
 class Gathered:
+    kind = 0
+
     def __init__(self, kv):
         count = lax.axis_size("seq")
         total = kv.shape[0]
@@ -210,11 +204,7 @@
         self.chunks, self.latest = count // chunk, ()
         self.arrays = [lax.all_gather(kv, "seq", axis=0, tiled=True)]
         self.slots = [
-            lambda place, index, j=j: (
-                0,
-                pl.multiple_of((index * chunk + j) * total, BAND),
-                index * chunk + j,
-            )
+            lambda index, j=j: (0, pl.multiple_of((index * chunk + j) * total, BAND))
             for j in range(chunk)
         ]
 
@@ -223,22 +213,24 @@
 
 
 class Ring:
+    kind = 0
+
     def __init__(self, kv):
         self.count, self.chunks, self.stage = lax.axis_size("seq"), 1, 0
         self.order = ring_order(self.count)
         self.arrays, self.slots, self.latest = [], [], ()
         self.front = {1: kv, -1: kv}
-        self.hold(kv, 0)
-
-    def hold(self, array, steps):
-        count = self.count
-        self.slots.append(
-            lambda place, index, r=len(self.arrays): (
-                r,
-                0,
-                ring_block(ring_place(place, count) - steps, count),
-            )
-        )
+        self.hold(kv)
+
+    @staticmethod
+    def sources(at, count):
+        steps = [0]
+        for stage in range(1, count // 2 + 1):
+            steps += [stage, -stage] if 2 * stage < count else [stage]
+        return [(at - step) % count for step in steps]
+
+    def hold(self, array):
+        self.slots.append(lambda index, r=len(self.arrays): (r, 0))
         self.arrays.append(array)
 
     def advance(self, *others):
@@ -253,32 +245,36 @@
             ]
             self.front[way] = lax.ppermute(value, "seq", pairs)
             fresh.append(self.front[way])
-            self.hold(self.front[way], way * self.stage)
+            self.hold(self.front[way])
         self.latest = tuple(fresh)
 
 
 class Pairs:
+    kind = 1
+
     def __init__(self, kv):
         self.count, self.chunks, self.step = lax.axis_size("seq"), 1, 0
         self.order = ring_order(self.count)
         self.total, self.front, self.latest = kv.shape[0], kv, ()
-        self.arrays, self.slots = [kv], []
-        self.hold(0, 0, lambda at: at)
-
-    def hold(self, r, first, block_at):
-        count = self.count
-        self.slots.append(
-            lambda place, index: (r, first, ring_block(block_at(ring_place(place, count)), count))
-        )
-
-    def beside(self, at, step):
-        up = 1 - 2 * (at % 2)
-        return (at + (up if step % 2 == 1 else -up) + self.count) % self.count
-
-    def source(self, at, step):
-        for back in range(step, 1, -1):
-            at = self.beside(at, back)
-        return at if step > 1 else self.beside(at, 1)
+        self.arrays, self.slots = [kv], [lambda index: (0, 0)]
+
+    @staticmethod
+    def beside(at, step, count):
+        return (at + (1 if (at + step) % 2 == 1 else -1)) % count
+
+    @staticmethod
+    def sources(at, count):
+        def first(at, step):
+            if step == 1:
+                return Pairs.beside(at, 1, count)
+            for back in range(step, 1, -1):
+                at = Pairs.beside(at, back, count)
+            return at
+
+        found = [at, first(at, 1)]
+        for step in range(2, count // 2 + 1):
+            found += [first(at, step), Pairs.beside(first(at, step), 1, count)]
+        return found
 
     def advance(self, *others):
         if self.step >= self.count // 2:
@@ -286,44 +282,87 @@
         self.step += 1
         step = self.step
         value = after(self.front, *others) if others else self.front
-        pairs = [(source, self.order[self.beside(at, step)]) for at, source in enumerate(self.order)]
+        pairs = [
+            (source, self.order[self.beside(at, step, self.count)])
+            for at, source in enumerate(self.order)
+        ]
         got = lax.ppermute(value, "seq", pairs)
         r = len(self.arrays)
         self.arrays.append(got)
-        self.hold(r, 0, lambda at: self.source(at, step))
+        self.slots.append(lambda index: (r, 0))
         if step == 1:
             self.front = jnp.concatenate([self.front, got], axis=0)
         else:
             self.front = got
-            self.hold(r, self.total, lambda at: self.beside(self.source(at, step), 1))
+            self.slots.append(lambda index: (r, self.total))
         self.latest = (got,)
 
 
-def attend_kernel(lanes, slots, chunks, q_count, kv_count, begin, end, info_ref, vertical_ref, slash_ref, *refs):
+def plan_kernel(kinds, lanes, heads, count, rows, info_ref, vertical_ref, slash_ref, plan_ref):
+    place, me = info_ref[0], info_ref[1]
+    plan_ref[0] = place
+
+    def enter(number, kind, block):
+        for lane in range(lanes):
+            doc = me ^ lane
+            for head in range(heads):
+                group = me * heads + head
+                found = (block == place) | (block == place - 1)
+                for s in range(slash_ref.shape[2]):
+                    found = found | (block == place - slash_ref[doc, group, s])
+                for s in range(vertical_ref.shape[2]):
+                    found = found | ((block == vertical_ref[doc, group, s]) & (block < place - 1))
+                at = 1 + ((kind * lanes + lane) * heads + head) * count + number
+                plan_ref[at] = jnp.where(found & (block >= 0), block * rows, OUT_OF_REACH)
+
+    if kinds:
+        order = ring_order(count)
+        for kind, maker in enumerate(kinds):
+            lists = {order[at]: [order[r] for r in maker.sources(at, count)] for at in range(count)}
+            for number in range(count):
+                block = jnp.int32(0)
+                for here, blocks in lists.items():
+                    block = jnp.where(place == here, blocks[number], block)
+                enter(number, kind, block)
+    else:
+
+        def one(number, carry):
+            enter(number, 0, number)
+            return carry
+
+        lax.fori_loop(0, count, one, 0)
+
+
+def plan(info, vertical, slash, kinds, rows):
+    count, lanes = lax.axis_size("seq"), lax.axis_size("doc")
+    heads = vertical.shape[1] // lanes
+    length = 1 + max(len(kinds), 1) * lanes * heads * count
+    return pl.pallas_call(
+        functools.partial(plan_kernel, kinds, lanes, heads, count, rows),
+        in_specs=[SMEM] * 3,
+        out_specs=SMEM,
+        out_shape=jax.ShapeDtypeStruct((length,), jnp.int32),
+        compiler_params=pltpu.CompilerParams(vmem_limit_bytes=16 * MIB),
+        name="plan",
+    )(info, vertical, slash)
+
+
+def attend_kernel(lanes, documents, kind, slots, chunks, q_count, kv_count, begin, end, plan_ref, *refs):
     q_refs, kv_refs, refs = refs[:q_count], refs[q_count:q_count + kv_count], refs[q_count + kv_count:]
     state_refs = refs[:0 if begin else 3 * len(lanes)]
     out_refs = refs[len(state_refs):]
     heads = kv_refs[0].shape[1] // (2 * HEAD_WIDTH)
-    place = info_ref[0]
+    place = plan_ref[0]
     factor = HEAD_WIDTH ** (-0.5)
 
-    def block_allowed(doc, group, block):
-        found = (block == place) | (block == place - 1)
-        for s in range(slash_ref.shape[2]):
-            found = found | (block == place - slash_ref[doc, group, s])
-        for s in range(vertical_ref.shape[2]):
-            found = found | ((block == vertical_ref[doc, group, s]) & (block < place - 1))
-        return found & (block >= 0)
-
-    for lane, (doc_of, segments, (kv_first, keys_in, base)) in enumerate(lanes):
-        doc = doc_of(info_ref[1])
+    for lane, (mask, segments, (kv_first, keys_in, base)) in enumerate(lanes):
         rows = sum(count for _, _, count in segments)
         rank = QUERY_GROUP * rows
         span = len(slots) * keys_in
         query_at = place * rows + lax.broadcasted_iota(jnp.int32, (rows, span), 0)
         column_at = lax.broadcasted_iota(jnp.int32, (1, span), 1)
         for head in range(heads):
-            group = info_ref[1] * heads + head
+            table = 1 + ((kind * documents + mask) * heads + head) * len(slots) * chunks
             queries = jnp.concatenate(
                 [
                     q_refs[source][
@@ -337,12 +376,12 @@
             )
 
             def step(index, carry):
-                found = [slot(place, index) for slot in slots]
+                found = [slot(index) for slot in slots]
 
                 def column(at):
                     cols = slice(at * HEAD_WIDTH, (at + 1) * HEAD_WIDTH)
                     parts = []
-                    for r, first, _ in found:
+                    for r, first in found:
                         if isinstance(first, int):
                             where = slice(first + kv_first, first + kv_first + keys_in)
                         else:
@@ -355,10 +394,8 @@
                     queries, keys, (((1,), (1,)), ((), ())), preferred_element_type=jnp.float32
                 ) * factor
                 key_at = jnp.zeros((1, span), jnp.int32)
-                for j, (_, _, block) in enumerate(found):
-                    shift = jnp.where(
-                        block_allowed(doc, group, block), block * rows + base - j * keys_in, 1 << 30
-                    )
+                for j in range(len(slots)):
+                    shift = plan_ref[table + index * len(slots) + j] + (base - j * keys_in)
                     inside = (column_at >= j * keys_in) & (column_at < (j + 1) * keys_in)
                     key_at = jnp.where(inside, column_at + shift, key_at)
                 bias = jnp.where(key_at <= query_at, jnp.float32(0), -jnp.inf)
@@ -414,7 +451,7 @@
                 out_refs[lane][:, cols] = result[h * rows:(h + 1) * rows]
 
 
-def attend(info, vertical, slash, lanes, queries, spread, states=None, end=True):
+def attend(table, lanes, queries, spread, states=None, end=True):
     q_cols = queries[0].shape[1]
     rows = sum(count for _, _, count in lanes[0][1])
     span = len(spread.slots) * spread.chunks * lanes[0][2][1]
@@ -426,11 +463,20 @@
         shape = (rows * q_cols // HEAD_WIDTH, HEAD_WIDTH)
         shapes = [jax.ShapeDtypeStruct(shape, jnp.float32)] * (3 * len(lanes))
     kernel = functools.partial(
-        attend_kernel, lanes, spread.slots, spread.chunks, len(queries), len(arrays), not states, end
+        attend_kernel,
+        lanes,
+        lax.axis_size("doc"),
+        spread.kind,
+        spread.slots,
+        spread.chunks,
+        len(queries),
+        len(arrays),
+        not states,
+        end,
     )
     return pl.pallas_call(
         kernel,
-        in_specs=[SMEM] * 3 + [VMEM] * (len(queries) + len(arrays) + len(held)),
+        in_specs=[SMEM] + [VMEM] * (len(queries) + len(arrays) + len(held)),
         out_specs=[VMEM] * len(shapes),
         out_shape=shapes,
         compiler_params=pltpu.CompilerParams(vmem_limit_bytes=28 * MIB),
@@ -440,7 +486,7 @@
             transcendentals=len(lanes) * rows * span * q_cols // HEAD_WIDTH,
         ),
         name="attend",
-    )(info, vertical, slash, *queries, *arrays, *held)
+    )(table, *queries, *arrays, *held)
 
 
 def deliver_kernel(masks, info_ref, *refs):
@@ -481,7 +527,9 @@
     own = tokens[0]
     gain = norm_gain.reshape(1, width)
     weights = (w_query, key_weight, value_weight)
-    pattern = (info, vertical_blocks, slash_offsets)
+    long = lax.axis_size("seq") > 8 or lax.axis_size("seq") % 2 == 1
+    ring, pairs = (Gathered, Gathered) if long else (Ring, Pairs)
+    pattern = plan(info, vertical_blocks, slash_offsets, () if long else (Ring, Pairs), rows)
     head = rows * 3 // 4 // BAND * BAND
     tail = rows - head
 
@@ -499,11 +547,9 @@
         early=True,
     )
     params = (gain_in, wq_in, wk_in, wv_in, table)
-    long = lax.axis_size("seq") > 8 or lax.axis_size("seq") % 2 == 1
-    ring, pairs = (Gathered, Gathered) if long else (Ring, Pairs)
     near = ring(kv_near)
     near.advance()
-    near.advance()
+    near.advance(pattern)
     got_head = after(got_head, *near.latest)
 
     got_tail = swap(after(send_tail, got_head), "doc", 2)
@@ -533,27 +579,24 @@
     late = pairs(kv_tail)
     late.advance()
     mixed_own, mixed_twin = attend(
-        *pattern,
-        [
-            (lambda d: d, [(0, 0, rows)], (0, rows, 0)),
-            (lambda d: d ^ 1, [(0, rows, rows)], (rows, rows, 0)),
-        ],
+        pattern,
+        [(0, [(0, 0, rows)], (0, rows, 0)), (1, [(0, rows, rows)], (rows, rows, 0))],
         [after(q_near, kv_tail)],
         near,
     )
     out_twin = swap(mixed_twin, "doc", 1)
-    early.advance()
+    early.advance(kv_tail)
     late.advance(mixed_twin)
     early.advance()
     late.advance()
     late.advance()
     remote = [
-        (lambda d: d ^ 2, [(0, 0, head), (1, 0, tail)]),
-        (lambda d: d ^ 3, [(0, head, head), (1, tail, tail)]),
+        (2, [(0, 0, head), (1, 0, tail)]),
+        (3, [(0, head, head), (1, tail, tail)]),
     ]
     queries = [after(q_head, out_twin), q_tail]
     states = attend(
-        *pattern,
+        pattern,
         [lane + ((at * head, head, 0),) for at, lane in enumerate(remote)],
         queries,
         early,
@@ -563,7 +606,7 @@
     for at, lane in enumerate(remote):
         state = states[3 * at:3 * at + 3]
         (mixed,) = attend(
-            *pattern, [lane + ((at * tail, tail, head),)], queries, late, states=[state]
+            pattern, [lane + ((at * tail, tail, head),)], queries, late, states=[state]
         )
         home.append(swap(mixed, "doc", 2 + at))
     count = lax.axis_size("doc")

time: 75.5 us -> 73.2 us (0.970)
  waiting for transfers between devices: 25.4 us -> 20.2 us
  starting transfers between devices: 24.2 us -> 26.2 us
  Pallas kernels: 24.8 us -> 25.8 us
    ppermute x14, waiting for transfers between devices: 9.76 us -> 6.32 us  [advance(): self.front[way] = lax.ppermute(value, 'seq', pairs)]
    ppermute x4, waiting for transfers between devices: 6.62 us -> 4.86 us  [advance(): got = lax.ppermute(value, 'seq', pairs)]
    ppermute x4, starting transfers between devices: 2.8 us -> 4.09 us  [advance(): got = lax.ppermute(value, 'seq', pairs)]
    pallas_call x4 -> x5, Pallas kernels: 10.7 us -> 11.7 us  [the longest x4 9.5 us: attend(): pl.pallas_call(kernel, in_specs=[SMEM] + [VMEM] * (len(queries) + len(arr...]
    ppermute x14, starting transfers between devices: 15.8 us -> 16.7 us  [advance(): self.front[way] = lax.ppermute(value, 'seq', pairs)]
  transfers between devices with their start and end apart: 26 -> 26, of which waited for: 10 -> 10; matrix products, arithmetic and copies ran while one was open for 1% -> 1% of each run, Pallas kernels for 28% -> 31%
where the time goes in v2:
time: 73.2 us; the launch traced here: 73.1 us
  starting transfers between devices  26.2 us (36%)
  Pallas kernels  25.8 us (35%)
  waiting for transfers between devices  20.2 us (28%)
    ppermute x14, starting transfers between devices, advance(): self.front[way] = lax.ppermute(value, 'seq', pairs)  16.7 us
    pallas_call x3, Pallas kernels, project(): pl.pallas_call(functools.partial(project_kernel, places, table_rows, earl...  10.4 us
    pallas_call x4, Pallas kernels, attend(): pl.pallas_call(kernel, in_specs=[SMEM] + [VMEM] * (len(queries) + len(arr...  9.5 us
    ppermute x8, waiting for transfers between devices, swap(): lax.ppermute(value, axis, [(source, source ^ mask) for source in range(co...  8.99 us
    ppermute x14, waiting for transfers between devices, advance(): self.front[way] = lax.ppermute(value, 'seq', pairs)  6.32 us
    ppermute x8, starting transfers between devices, swap(): lax.ppermute(value, axis, [(source, source ^ mask) for source in range(co...  5.44 us
    ppermute x4, waiting for transfers between devices, advance(): got = lax.ppermute(value, 'seq', pairs)  4.86 us
    ppermute x4, starting transfers between devices, advance(): got = lax.ppermute(value, 'seq', pairs)  4.09 us
  transfers between devices with their start and end apart: 26, of which 10 were waited for; matrix products, arithmetic and copies ran while one was open for 1% of the time, Pallas kernels for 31%

profile of v2, /device:TPU:0, one launch (start us, length us, event | category | flops | bytes accessed | tf_op | source)
XLA Modules:
  0.0 73.1 jit_solution(15683683799189147390)
XLA Ops:
  0.5 1.2 %cut.1 = (bf16[96,4096]{1,0:T(8,128)(2,1)S(1)}, bf16[32,4096]{1,0:T(8,128)(2,1)S(1)}) custom-call(bf16[128,4096]{1,0:T(8,128)(2,1)} %bitcast.5), custom_call_target="tpu_custom_call" | custom-call | tf_op jit(solution)/shard_map/cut/pallas_call | solution.py:182
  1.7 2.6 %collective-permute-start = (bf16[96,4096]{1,0:T(8,128)(2,1)S(1)}, bf16[96,4096]{1,0:T(8,128)(2,1)S(1)}, u32[]{:S(2)}, u32[]{:S(2)}) collective-permute-start(bf16[96,4096]{1,0:T(8,128)(2,1)S(1)} %get-tuple-element.35), channel_id=1, source_target_pairs={{0,2},{1,3},{2,0},{3,1},{4,6},{5,7},{6,4},{7,5},{8,10},{9,11},{10,... | collective-permute-start | bytes 2359304 | tf_op jit(solution)/shard_map/ppermute | solution.py:27
  4.8 5.2 %project.3 = (bf16[256,512]{1,0:T(8,128)(2,1)S(1)}, bf16[256,256]{1,0:T(8,128)(2,1)S(1)}, f32[1,4096]{1,0:T(1,128)S(1)}, bf16[4096,128]{1,0:T(8,128)(2,1)S(1)}, ...) custom-call(s32[2]{0:T(128)S(1)} %pad_add_fusion.info_ref, bf16[128,4096]{1,0:T(8,128)(2,1)} %bitcast.6, ...), custom_call_target="tpu_custom_call" | custom-call | flops 1610612736 | bytes 8388608 | tf_op jit(solution)/shard_map/project/pallas_call | solution.py:153
  10.0 1.6 %collective-permute-start.2 = (bf16[256,256]{1,0:T(8,128)(2,1)S(1)}, bf16[256,256]{1,0:T(8,128)(2,1)S(1)}, u32[]{:S(2)}, u32[]{:S(2)}) collective-permute-start(bf16[256,256]{1,0:T(8,128)(2,1)S(1)} %get-tuple-element.36.refs_1_), channel_id=1, source_target_pairs={{0,8},{8,16},{16,24},{24,28},{28,20},{20,12},{12,4},{4,0},{1,9},{9... | collective-permute-start | bytes 393224 | tf_op jit(solution)/shard_map/ppermute | solution.py:246
  12.1 2.2 %plan.1.plan_ref = s32[65]{0:T(128)S(1)} custom-call(s32[2]{0:T(128)S(1)} %pad_add_fusion.info_ref, s32[4,4,4]{2,1,0:T(4,128)S(1)} %copy-done, s32[4,4,4]{2,1,0:T(4,128)S(1)} %copy-done.1), custom_call_target="tpu_custom_call" | custom-call | tf_op jit(solution)/shard_map/plan/pallas_call | solution.py:340
  14.3 1.4 %collective-permute-done.2.refs_2_ = bf16[256,256]{1,0:T(8,128)(2,1)S(1)} collective-permute-done((bf16[256,256]{1,0:T(8,128)(2,1)S(1)}, bf16[256,256]{1,0:T(8,128)(2,1)S(1)}, u32[]{:S(2)}, u32[]{:S(2)}) %collective-permute-start.2) | collective-permute-done | bytes 131104 | tf_op jit(solution)/shard_map/ppermute | solution.py:246
  15.7 1.6 %collective-permute-start.3 = (bf16[256,256]{1,0:T(8,128)(2,1)S(1)}, bf16[256,256]{1,0:T(8,128)(2,1)S(1)}, u32[]{:S(2)}, u32[]{:S(2)}) collective-permute-start(bf16[256,256]{1,0:T(8,128)(2,1)S(1)} %collective-permute-done.2.refs_2_), channel_id=1, source_target_pairs={{0,8},{8,16},{16,24},{24,28},{28,20},{20,12},{12,4},{4,0},{1,9},{9... | collective-permute-start | bytes 393224 | tf_op jit(solution)/shard_map/ppermute | solution.py:246
  17.7 4.7 %collective-permute-done.refs_0_ = bf16[96,4096]{1,0:T(8,128)(2,1)S(1)} collective-permute-done((bf16[96,4096]{1,0:T(8,128)(2,1)S(1)}, bf16[96,4096]{1,0:T(8,128)(2,1)S(1)}, u32[]{:S(2)}, u32[]{:S(2)}) %collective-permute-start) | collective-permute-done | bytes 786464 | tf_op jit(solution)/shard_map/ppermute | solution.py:27
  22.4 1.8 %collective-permute-start.7 = (bf16[32,4096]{1,0:T(8,128)(2,1)S(1)}, bf16[32,4096]{1,0:T(8,128)(2,1)S(1)}, u32[]{:S(2)}, u32[]{:S(2)}) collective-permute-start(bf16[32,4096]{1,0:T(8,128)(2,1)S(1)} %get-tuple-element.47), channel_id=1, source_target_pairs={{0,2},{1,3},{2,0},{3,1},{4,6},{5,7},{6,4},{7,5},{8,10},{9,11},{10,... | collective-permute-start | bytes 786440 | tf_op jit(solution)/shard_map/ppermute | solution.py:27
  24.3 1.6 %collective-permute-start.8 = (bf16[256,256]{1,0:T(8,128)(2,1)S(1)}, bf16[256,256]{1,0:T(8,128)(2,1)S(1)}, u32[]{:S(2)}, u32[]{:S(2)}) collective-permute-start(bf16[256,256]{1,0:T(8,128)(2,1)S(1)} %collective-permute-done.3.refs_4_), channel_id=1, source_target_pairs={{0,8},{8,16},{16,24},{24,28},{28,20},{20,12},{12,4},{4,0},{1,9},{9... | collective-permute-start | bytes 393224 | tf_op jit(solution)/shard_map/ppermute | solution.py:246
  26.3 3.2 %project.4 = (bf16[192,512]{1,0:T(8,128)(2,1)S(1)}, bf16[192,256]{1,0:T(8,128)(2,1)S(1)}) custom-call(s32[2]{0:T(128)S(1)} %pad_add_fusion.info_ref, bf16[96,4096]{1,0:T(8,128)(2,1)S(1)} %collective-permute-done.refs_0_, bf16[96,4096]{1,0:T(8,128)(2,1)S(1)} %collective-permute-done.6.refs_1_, f32[1,4096]{1,0:T(1,128)S(1)} %get-tuple-element.40.refs_2_, ...), custom_call_target="tpu_custom_call" | custom-call | flops 1207959552 | bytes 7864320 | tf_op jit(solution)/shard_map/project/pallas_call | solution.py:153
  29.5 1.6 %collective-permute-start.10 = (bf16[192,256]{1,0:T(8,128)(2,1)S(1)}, bf16[192,256]{1,0:T(8,128)(2,1)S(1)}, u32[]{:S(2)}, u32[]{:S(2)}) collective-permute-start(bf16[192,256]{1,0:T(8,128)(2,1)S(1)} %get-tuple-element.48.refs_2_), channel_id=1, source_target_pairs={{0,8},{8,16},{16,24},{24,28},{28,20},{20,12},{12,4},{4,0},{1,9},{9... | collective-permute-start | bytes 294920 | tf_op jit(solution)/shard_map/ppermute | solution.py:246
  31.6 2.6 %collective-permute-done.10.refs_3_ = bf16[192,256]{1,0:T(8,128)(2,1)S(1)} collective-permute-done((bf16[192,256]{1,0:T(8,128)(2,1)S(1)}, bf16[192,256]{1,0:T(8,128)(2,1)S(1)}, u32[]{:S(2)}, u32[]{:S(2)}) %collective-permute-start.10) | collective-permute-done | bytes 98336 | tf_op jit(solution)/shard_map/ppermute | solution.py:246
  34.1 1.6 %collective-permute-done.11.refs_4_ = bf16[192,256]{1,0:T(8,128)(2,1)S(1)} collective-permute-done((bf16[192,256]{1,0:T(8,128)(2,1)S(1)}, bf16[192,256]{1,0:T(8,128)(2,1)S(1)}, u32[]{:S(2)}, u32[]{:S(2)}) %collective-permute-start.11) | collective-permute-done | bytes 98336 | tf_op jit(solution)/shard_map/ppermute | solution.py:246
  35.7 1.6 %collective-permute-start.13 = (bf16[256,256]{1,0:T(8,128)(2,1)S(1)}, bf16[256,256]{1,0:T(8,128)(2,1)S(1)}, u32[]{:S(2)}, u32[]{:S(2)}) collective-permute-start(bf16[256,256]{1,0:T(8,128)(2,1)S(1)} %collective-permute-done.8.refs_6_), channel_id=1, source_target_pairs={{0,8},{8,16},{16,24},{24,28},{28,20},{20,12},{12,4},{4,0},{1,9},{9... | collective-permute-start | bytes 393224 | tf_op jit(solution)/shard_map/ppermute | solution.py:246
  37.3 1.6 %collective-permute-start.19 = (bf16[192,256]{1,0:T(8,128)(2,1)S(1)}, bf16[192,256]{1,0:T(8,128)(2,1)S(1)}, u32[]{:S(2)}, u32[]{:S(2)}) collective-permute-start(bf16[192,256]{1,0:T(8,128)(2,1)S(1)} %collective-permute-done.10.refs_3_), channel_id=1, source_target_pairs={{0,8},{8,16},{16,24},{24,28},{28,20},{20,12},{12,4},{4,0},{1,9},{9... | collective-permute-start | bytes 294920 | tf_op jit(solution)/shard_map/ppermute | solution.py:246
  39.4 2.0 %project.5 = (bf16[64,512]{1,0:T(8,128)(2,1)S(1)}, bf16[64,256]{1,0:T(8,128)(2,1)S(1)}) custom-call(s32[2]{0:T(128)S(1)} %pad_add_fusion.info_ref, bf16[32,4096]{1,0:T(8,128)(2,1)S(1)} %collective-permute-done.7.refs_0_, bf16[32,4096]{1,0:T(8,128)(2,1)S(1)} %collective-permute-done.12.refs_1_, f32[1,4096]{1,0:T(1,128)S(1)} %get-tuple-element.40.refs_2_, ...), custom_call_target="tpu_custom_call" | custom-call | flops 402653184 | bytes 6815744 | tf_op jit(solution)/shard_map/project/pallas_call | solution.py:153
  41.4 1.6 %collective-permute-start.15 = (bf16[64,256]{1,0:T(8,128)(2,1)S(1)}, bf16[64,256]{1,0:T(8,128)(2,1)S(1)}, u32[]{:S(2)}, u32[]{:S(2)}) collective-permute-start(bf16[64,256]{1,0:T(8,128)(2,1)S(1)} %get-tuple-element.50.refs_2_), channel_id=1, source_target_pairs={{0,8},{8,0},{16,24},{24,16},{28,20},{20,28},{12,4},{4,12},{1,9},{9... | collective-permute-start | bytes 98312 | tf_op jit(solution)/shard_map/ppermute | solution.py:289
  43.8 1.6 %collective-permute-start.21 = (bf16[192,256]{1,0:T(8,128)(2,1)S(1)}, bf16[192,256]{1,0:T(8,128)(2,1)S(1)}, u32[]{:S(2)}, u32[]{:S(2)}) collective-permute-start(bf16[192,256]{1,0:T(8,128)(2,1)S(1)} %collective-permute-done.19.refs_5_), channel_id=1, source_target_pairs={{0,8},{8,16},{16,24},{24,28},{28,20},{20,12},{12,4},{4,0},{1,9},{9... | collective-permute-start | bytes 294920 | tf_op jit(solution)/shard_map/ppermute | solution.py:246
  45.4 2.8 %attend.4 = (bf16[128,512]{1,0:T(8,128)(2,1)S(1)}, bf16[128,512]{1,0:T(8,128)(2,1)S(1)}) custom-call(s32[65]{0:T(128)S(1)} %plan.1.plan_ref, bf16[256,512]{1,0:T(8,128)(2,1)S(1)} %get-tuple-element.51.refs_0_, bf16[256,256]{1,0:T(8,128)(2,1)S(1)} %get-tuple-element.36.refs_1_, bf16[256,256]{1,0:T(8,128)(2,1)S(1)} %collective-permute-done.2.refs_2_, ...), custom_call_target="tpu_custom_call" | custom-call | flops 536870912 | bytes 1572864 | tf_op jit(solution)/shard_map/attend/pallas_call | solution.py:477
  48.7 1.6 %collective-permute-start.22 = (bf16[192,256]{1,0:T(8,128)(2,1)S(1)}, bf16[192,256]{1,0:T(8,128)(2,1)S(1)}, u32[]{:S(2)}, u32[]{:S(2)}) collective-permute-start(bf16[192,256]{1,0:T(8,128)(2,1)S(1)} %collective-permute-done.20.refs_6_), channel_id=1, source_target_pairs={{0,4},{8,0},{16,8},{24,16},{28,24},{20,28},{12,20},{4,12},{1,5},{9... | collective-permute-start | bytes 294920 | tf_op jit(solution)/shard_map/ppermute | solution.py:246
  50.3 1.7 %collective-permute-start.23 = (bf16[192,256]{1,0:T(8,128)(2,1)S(1)}, bf16[192,256]{1,0:T(8,128)(2,1)S(1)}, u32[]{:S(2)}, u32[]{:S(2)}) collective-permute-start(bf16[192,256]{1,0:T(8,128)(2,1)S(1)} %collective-permute-done.21.refs_7_), channel_id=1, source_target_pairs={{0,8},{8,16},{16,24},{24,28},{28,20},{20,12},{12,4},{4,0},{1,9},{9... | collective-permute-start | bytes 294920 | tf_op jit(solution)/shard_map/ppermute | solution.py:246
  52.5 1.6 %collective-permute-start.17 = (bf16[128,256]{1,0:T(8,128)(2,1)S(1)}, bf16[128,256]{1,0:T(8,128)(2,1)S(1)}, u32[]{:S(2)}, u32[]{:S(2)}) collective-permute-start(bf16[128,256]{1,0:T(8,128)(2,1)S(1)} %collective-permute-done.16.refs_4_), channel_id=1, source_target_pairs={{0,8},{8,0},{16,24},{24,16},{28,20},{20,28},{12,4},{4,12},{1,9},{9... | collective-permute-start | bytes 196616 | tf_op jit(solution)/shard_map/ppermute | solution.py:289
  54.1 2.7 %collective-permute-done.17.refs_5_ = bf16[128,256]{1,0:T(8,128)(2,1)S(1)} collective-permute-done((bf16[128,256]{1,0:T(8,128)(2,1)S(1)}, bf16[128,256]{1,0:T(8,128)(2,1)S(1)}, u32[]{:S(2)}, u32[]{:S(2)}) %collective-permute-start.17) | collective-permute-done | bytes 65568 | tf_op jit(solution)/shard_map/ppermute | solution.py:289
  57.2 2.2 %attend.5 = (f32[512,128]{1,0:T(8,128)S(1)}, f32[512,128]{1,0:T(8,128)S(1)}, f32[512,128]{1,0:T(8,128)S(1)}, f32[512,128]{1,0:T(8,128)S(1)}, f32[512,128]{1,0:T(8,128)S(1)}, /*index=5*/f32[512,128]{1,0:T(8,128)S(1)}) custom-call(s32[65]{0:T(128)S(1)} %plan.1.plan_ref, bf16[192,512]{1,0:T(8,128)(2,1)S(1)} %get-tuple-element.53.refs_0_, ...), custom_call_target="tpu_custom_call" | custom-call | flops 402653184 | bytes 1310720 | tf_op jit(solution)/shard_map/attend/pallas_call | solution.py:477
  59.5 1.6 %collective-permute-done.18.refs_6_ = bf16[128,256]{1,0:T(8,128)(2,1)S(1)} collective-permute-done((bf16[128,256]{1,0:T(8,128)(2,1)S(1)}, bf16[128,256]{1,0:T(8,128)(2,1)S(1)}, u32[]{:S(2)}, u32[]{:S(2)}) %collective-permute-start.18) | collective-permute-done | bytes 65568 | tf_op jit(solution)/shard_map/ppermute | solution.py:289
  61.0 2.2 %attend.7 = bf16[128,512]{1,0:T(8,128)(2,1)S(1)} custom-call(s32[65]{0:T(128)S(1)} %plan.1.plan_ref, bf16[192,512]{1,0:T(8,128)(2,1)S(1)} %get-tuple-element.53.refs_0_, bf16[64,512]{1,0:T(8,128)(2,1)S(1)} %get-tuple-element.54.refs_1_, bf16[64,256]{1,0:T(8,128)(2,1)S(1)} %get-tuple-element.50.refs_2_, bf16[64,256]{1,0:T(8,128)(2,1)S(1)} %collective-permute-done.15.refs_3_, ...), custom_call_target="tpu_custom_call" | custom-call | flops 67108864 | bytes 524288 | tf_op jit(solution)/shard_map/attend/pallas_call | solution.py:477
  63.3 2.2 %attend.6 = bf16[128,512]{1,0:T(8,128)(2,1)S(1)} custom-call(s32[65]{0:T(128)S(1)} %plan.1.plan_ref, bf16[192,512]{1,0:T(8,128)(2,1)S(1)} %get-tuple-element.53.refs_0_, bf16[64,512]{1,0:T(8,128)(2,1)S(1)} %get-tuple-element.54.refs_1_, bf16[64,256]{1,0:T(8,128)(2,1)S(1)} %get-tuple-element.50.refs_2_, bf16[64,256]{1,0:T(8,128)(2,1)S(1)} %collective-permute-done.15.refs_3_, ...), custom_call_target="tpu_custom_call" | custom-call | flops 67108864 | bytes 524288 | tf_op jit(solution)/shard_map/attend/pallas_call | solution.py:477
  66.1 1.3 %deliver.2.refs_2_ = bf16[1,128,2048]{2,1,0:T(8,128)(2,1)} custom-call(s32[2]{0:T(128)S(1)} %pad_add_fusion.info_ref, bf16[128,512]{1,0:T(8,128)(2,1)S(1)} %get-tuple-element.64.refs_0_, bf16[128,512]{1,0:T(8,128)(2,1)S(1)} %collective-permute-done.14.refs_1_), custom_call_target="tpu_custom_call" | custom-call | tf_op jit(solution)/shard_map/deliver/pallas_call | solution.py:507
  67.4 0.8 %collective-permute-done.25.refs_1_ = bf16[128,512]{1,0:T(8,128)(2,1)S(1)} collective-permute-done((bf16[128,512]{1,0:T(8,128)(2,1)S(1)}, bf16[128,512]{1,0:T(8,128)(2,1)S(1)}, u32[]{:S(2)}, u32[]{:S(2)}) %collective-permute-start.25) | collective-permute-done | bytes 131104 | tf_op jit(solution)/shard_map/ppermute | solution.py:27
  68.2 3.5 %collective-permute-done.24.refs_0_ = bf16[128,512]{1,0:T(8,128)(2,1)S(1)} collective-permute-done((bf16[128,512]{1,0:T(8,128)(2,1)S(1)}, bf16[128,512]{1,0:T(8,128)(2,1)S(1)}, u32[]{:S(2)}, u32[]{:S(2)}) %collective-permute-start.24) | collective-permute-done | bytes 131104 | tf_op jit(solution)/shard_map/ppermute | solution.py:27
  71.6 1.3 %deliver.3 = bf16[1,128,2048]{2,1,0:T(8,128)(2,1)} custom-call(s32[2]{0:T(128)S(1)} %pad_add_fusion.info_ref, bf16[128,512]{1,0:T(8,128)(2,1)S(1)} %collective-permute-done.24.refs_0_, bf16[128,512]{1,0:T(8,128)(2,1)S(1)} %collective-permute-done.25.refs_1_, bf16[1,128,2048]{2,1,0:T(8,128)(2,1)} %deliver.2.refs_2_), custom_call_target="tpu_custom_call", output_to_operand_aliasing={{}: (3, {})} | custom-call | tf_op jit(solution)/shard_map/deliver/pallas_call | solution.py:507
  (41 shorter events, 6.1 us)
Async XLA Ops:
  0.0 4.8 %collective-permute-start.1 = (bf16[128,4096]{1,0:T(8,128)(2,1)}, bf16[128,4096]{1,0:T(8,128)(2,1)S(1)}, u32[]{:S(2)}, u32[]{:S(2)}) collective-permute-start(bf16[128,4096]{1,0:T(8,128)(2,1)} %bitcast.4), channel_id=1, source_target_pairs={{0,1},{1,0},{2,3},{3,2},{4,5},{5,4},{6,7},{7,6},{8,9},{9,8},{10,11... | collective-permute-start | bytes 3145736 | tf_op jit(solution)/shard_map/ppermute | solution.py:27
  1.7 20.8 %collective-permute-start = (bf16[96,4096]{1,0:T(8,128)(2,1)S(1)}, bf16[96,4096]{1,0:T(8,128)(2,1)S(1)}, u32[]{:S(2)}, u32[]{:S(2)}) collective-permute-start(bf16[96,4096]{1,0:T(8,128)(2,1)S(1)} %get-tuple-element.35), channel_id=1, source_target_pairs={{0,2},{1,3},{2,0},{3,1},{4,6},{5,7},{6,4},{7,5},{8,10},{9,11},{10,... | collective-permute-start | bytes 2359304 | tf_op jit(solution)/shard_map/ppermute | solution.py:27
  4.8 7.3 %copy-start = (s32[4,4,4]{2,1,0:T(4,128)S(1)}, s32[4,4,4]{2,1,0:T(4,128)}, u32[]{:S(2)}) copy-start(s32[4,4,4]{2,1,0:T(4,128)} %vertical_ref.1) | copy-start | bytes 772
  4.8 7.3 %copy-start.1 = (s32[4,4,4]{2,1,0:T(4,128)S(1)}, s32[4,4,4]{2,1,0:T(4,128)}, u32[]{:S(2)}) copy-start(s32[4,4,4]{2,1,0:T(4,128)} %slash_ref.1) | copy-start | bytes 772
  10.0 5.7 %collective-permute-start.2 = (bf16[256,256]{1,0:T(8,128)(2,1)S(1)}, bf16[256,256]{1,0:T(8,128)(2,1)S(1)}, u32[]{:S(2)}, u32[]{:S(2)}) collective-permute-start(bf16[256,256]{1,0:T(8,128)(2,1)S(1)} %get-tuple-element.36.refs_1_), channel_id=1, source_target_pairs={{0,8},{8,16},{16,24},{24,28},{28,20},{20,12},{12,4},{4,0},{1,9},{9... | collective-permute-start | bytes 393224 | tf_op jit(solution)/shard_map/ppermute | solution.py:246
  11.6 5.6 %collective-permute-start.4 = (bf16[256,256]{1,0:T(8,128)(2,1)S(1)}, bf16[256,256]{1,0:T(8,128)(2,1)S(1)}, u32[]{:S(2)}, u32[]{:S(2)}) collective-permute-start(bf16[256,256]{1,0:T(8,128)(2,1)S(1)} %get-tuple-element.36.refs_1_), channel_id=1, source_target_pairs={{0,4},{8,0},{16,8},{24,16},{28,24},{20,28},{12,20},{4,12},{1,5},{9... | collective-permute-start | bytes 393224 | tf_op jit(solution)/shard_map/ppermute | solution.py:246
  15.7 6.8 %collective-permute-start.3 = (bf16[256,256]{1,0:T(8,128)(2,1)S(1)}, bf16[256,256]{1,0:T(8,128)(2,1)S(1)}, u32[]{:S(2)}, u32[]{:S(2)}) collective-permute-start(bf16[256,256]{1,0:T(8,128)(2,1)S(1)} %collective-permute-done.2.refs_2_), channel_id=1, source_target_pairs={{0,8},{8,16},{16,24},{24,28},{28,20},{20,12},{12,4},{4,0},{1,9},{9... | collective-permute-start | bytes 393224 | tf_op jit(solution)/shard_map/ppermute | solution.py:246
  17.2 5.2 %collective-permute-start.5 = (bf16[256,256]{1,0:T(8,128)(2,1)S(1)}, bf16[256,256]{1,0:T(8,128)(2,1)S(1)}, u32[]{:S(2)}, u32[]{:S(2)}) collective-permute-start(bf16[256,256]{1,0:T(8,128)(2,1)S(1)} %collective-permute-done.4.refs_3_), channel_id=1, source_target_pairs={{0,4},{8,0},{16,8},{24,16},{28,24},{20,28},{12,20},{4,12},{1,5},{9... | collective-permute-start | bytes 393224 | tf_op jit(solution)/shard_map/ppermute | solution.py:246
  22.4 3.8 %collective-permute-start.6 = (bf16[96,4096]{1,0:T(8,128)(2,1)S(1)}, bf16[96,4096]{1,0:T(8,128)(2,1)S(1)}, u32[]{:S(2)}, u32[]{:S(2)}) collective-permute-start(bf16[96,4096]{1,0:T(8,128)(2,1)S(1)} %collective-permute-done.refs_0_), channel_id=1, source_target_pairs={{0,1},{1,0},{2,3},{3,2},{4,5},{5,4},{6,7},{7,6},{8,9},{9,8},{10,11... | collective-permute-start | bytes 2359304 | tf_op jit(solution)/shard_map/ppermute | solution.py:27
  22.4 9.1 %collective-permute-start.7 = (bf16[32,4096]{1,0:T(8,128)(2,1)S(1)}, bf16[32,4096]{1,0:T(8,128)(2,1)S(1)}, u32[]{:S(2)}, u32[]{:S(2)}) collective-permute-start(bf16[32,4096]{1,0:T(8,128)(2,1)S(1)} %get-tuple-element.47), channel_id=1, source_target_pairs={{0,2},{1,3},{2,0},{3,1},{4,6},{5,7},{6,4},{7,5},{8,10},{9,11},{10,... | collective-permute-start | bytes 786440 | tf_op jit(solution)/shard_map/ppermute | solution.py:27
  24.3 7.3 %collective-permute-start.8 = (bf16[256,256]{1,0:T(8,128)(2,1)S(1)}, bf16[256,256]{1,0:T(8,128)(2,1)S(1)}, u32[]{:S(2)}, u32[]{:S(2)}) collective-permute-start(bf16[256,256]{1,0:T(8,128)(2,1)S(1)} %collective-permute-done.3.refs_4_), channel_id=1, source_target_pairs={{0,8},{8,16},{16,24},{24,28},{28,20},{20,12},{12,4},{4,0},{1,9},{9... | collective-permute-start | bytes 393224 | tf_op jit(solution)/shard_map/ppermute | solution.py:246
  25.8 5.7 %collective-permute-start.9 = (bf16[256,256]{1,0:T(8,128)(2,1)S(1)}, bf16[256,256]{1,0:T(8,128)(2,1)S(1)}, u32[]{:S(2)}, u32[]{:S(2)}) collective-permute-start(bf16[256,256]{1,0:T(8,128)(2,1)S(1)} %collective-permute-done.5.refs_5_), channel_id=1, source_target_pairs={{0,4},{8,0},{16,8},{24,16},{28,24},{20,28},{12,20},{4,12},{1,5},{9... | collective-permute-start | bytes 393224 | tf_op jit(solution)/shard_map/ppermute | solution.py:246
  29.5 4.7 %collective-permute-start.10 = (bf16[192,256]{1,0:T(8,128)(2,1)S(1)}, bf16[192,256]{1,0:T(8,128)(2,1)S(1)}, u32[]{:S(2)}, u32[]{:S(2)}) collective-permute-start(bf16[192,256]{1,0:T(8,128)(2,1)S(1)} %get-tuple-element.48.refs_2_), channel_id=1, source_target_pairs={{0,8},{8,16},{16,24},{24,28},{28,20},{20,12},{12,4},{4,0},{1,9},{9... | collective-permute-start | bytes 294920 | tf_op jit(solution)/shard_map/ppermute | solution.py:246
  31.1 4.6 %collective-permute-start.11 = (bf16[192,256]{1,0:T(8,128)(2,1)S(1)}, bf16[192,256]{1,0:T(8,128)(2,1)S(1)}, u32[]{:S(2)}, u32[]{:S(2)}) collective-permute-start(bf16[192,256]{1,0:T(8,128)(2,1)S(1)} %get-tuple-element.48.refs_2_), channel_id=1, source_target_pairs={{0,4},{8,0},{16,8},{24,16},{28,24},{20,28},{12,20},{4,12},{1,5},{9... | collective-permute-start | bytes 294920 | tf_op jit(solution)/shard_map/ppermute | solution.py:246
  35.7 3.6 %collective-permute-start.12 = (bf16[32,4096]{1,0:T(8,128)(2,1)S(1)}, bf16[32,4096]{1,0:T(8,128)(2,1)S(1)}, u32[]{:S(2)}, u32[]{:S(2)}) collective-permute-start(bf16[32,4096]{1,0:T(8,128)(2,1)S(1)} %collective-permute-done.7.refs_0_), channel_id=1, source_target_pairs={{0,1},{1,0},{2,3},{3,2},{4,5},{5,4},{6,7},{7,6},{8,9},{9,8},{10,11... | collective-permute-start | bytes 786440 | tf_op jit(solution)/shard_map/ppermute | solution.py:27
  35.7 9.6 %collective-permute-start.13 = (bf16[256,256]{1,0:T(8,128)(2,1)S(1)}, bf16[256,256]{1,0:T(8,128)(2,1)S(1)}, u32[]{:S(2)}, u32[]{:S(2)}) collective-permute-start(bf16[256,256]{1,0:T(8,128)(2,1)S(1)} %collective-permute-done.8.refs_6_), channel_id=1, source_target_pairs={{0,8},{8,16},{16,24},{24,28},{28,20},{20,12},{12,4},{4,0},{1,9},{9... | collective-permute-start | bytes 393224 | tf_op jit(solution)/shard_map/ppermute | solution.py:246
  37.3 6.4 %collective-permute-start.19 = (bf16[192,256]{1,0:T(8,128)(2,1)S(1)}, bf16[192,256]{1,0:T(8,128)(2,1)S(1)}, u32[]{:S(2)}, u32[]{:S(2)}) collective-permute-start(bf16[192,256]{1,0:T(8,128)(2,1)S(1)} %collective-permute-done.10.refs_3_), channel_id=1, source_target_pairs={{0,8},{8,16},{16,24},{24,28},{28,20},{20,12},{12,4},{4,0},{1,9},{9... | collective-permute-start | bytes 294920 | tf_op jit(solution)/shard_map/ppermute | solution.py:246
  38.9 9.8 %collective-permute-start.20 = (bf16[192,256]{1,0:T(8,128)(2,1)S(1)}, bf16[192,256]{1,0:T(8,128)(2,1)S(1)}, u32[]{:S(2)}, u32[]{:S(2)}) collective-permute-start(bf16[192,256]{1,0:T(8,128)(2,1)S(1)} %collective-permute-done.11.refs_4_), channel_id=1, source_target_pairs={{0,4},{8,0},{16,8},{24,16},{28,24},{20,28},{12,20},{4,12},{1,5},{9... | collective-permute-start | bytes 294920 | tf_op jit(solution)/shard_map/ppermute | solution.py:246
  41.4 6.8 %collective-permute-start.15 = (bf16[64,256]{1,0:T(8,128)(2,1)S(1)}, bf16[64,256]{1,0:T(8,128)(2,1)S(1)}, u32[]{:S(2)}, u32[]{:S(2)}) collective-permute-start(bf16[64,256]{1,0:T(8,128)(2,1)S(1)} %get-tuple-element.50.refs_2_), channel_id=1, source_target_pairs={{0,8},{8,0},{16,24},{24,16},{28,20},{20,28},{12,4},{4,12},{1,9},{9... | collective-permute-start | bytes 98312 | tf_op jit(solution)/shard_map/ppermute | solution.py:289
  43.8 6.5 %collective-permute-start.21 = (bf16[192,256]{1,0:T(8,128)(2,1)S(1)}, bf16[192,256]{1,0:T(8,128)(2,1)S(1)}, u32[]{:S(2)}, u32[]{:S(2)}) collective-permute-start(bf16[192,256]{1,0:T(8,128)(2,1)S(1)} %collective-permute-done.19.refs_5_), channel_id=1, source_target_pairs={{0,8},{8,16},{16,24},{24,28},{28,20},{20,12},{12,4},{4,0},{1,9},{9... | collective-permute-start | bytes 294920 | tf_op jit(solution)/shard_map/ppermute | solution.py:246
  48.2 4.3 %collective-permute-start.16 = (bf16[128,256]{1,0:T(8,128)(2,1)S(1)}, bf16[128,256]{1,0:T(8,128)(2,1)S(1)}, u32[]{:S(2)}, u32[]{:S(2)}) collective-permute-start(bf16[128,256]{1,0:T(8,128)(2,1)S(1)} %pad_maximum_fusion.1), channel_id=1, source_target_pairs={{0,4},{8,16},{16,8},{24,28},{28,24},{20,12},{12,20},{4,0},{1,5},{9... | collective-permute-start | bytes 196616 | tf_op jit(solution)/shard_map/ppermute | solution.py:289
  48.7 8.5 %collective-permute-start.14 = (bf16[128,512]{1,0:T(8,128)(2,1)S(1)}, bf16[128,512]{1,0:T(8,128)(2,1)S(1)}, u32[]{:S(2)}, u32[]{:S(2)}) collective-permute-start(bf16[128,512]{1,0:T(8,128)(2,1)S(1)} %get-tuple-element.52), channel_id=1, source_target_pairs={{0,1},{1,0},{2,3},{3,2},{4,5},{5,4},{6,7},{7,6},{8,9},{9,8},{10,11... | collective-permute-start | bytes 393224 | tf_op jit(solution)/shard_map/ppermute | solution.py:27
  48.7 8.5 %collective-permute-start.22 = (bf16[192,256]{1,0:T(8,128)(2,1)S(1)}, bf16[192,256]{1,0:T(8,128)(2,1)S(1)}, u32[]{:S(2)}, u32[]{:S(2)}) collective-permute-start(bf16[192,256]{1,0:T(8,128)(2,1)S(1)} %collective-permute-done.20.refs_6_), channel_id=1, source_target_pairs={{0,4},{8,0},{16,8},{24,16},{28,24},{20,28},{12,20},{4,12},{1,5},{9... | collective-permute-start | bytes 294920 | tf_op jit(solution)/shard_map/ppermute | solution.py:246
  50.3 6.9 %collective-permute-start.23 = (bf16[192,256]{1,0:T(8,128)(2,1)S(1)}, bf16[192,256]{1,0:T(8,128)(2,1)S(1)}, u32[]{:S(2)}, u32[]{:S(2)}) collective-permute-start(bf16[192,256]{1,0:T(8,128)(2,1)S(1)} %collective-permute-done.21.refs_7_), channel_id=1, source_target_pairs={{0,8},{8,16},{16,24},{24,28},{28,20},{20,12},{12,4},{4,0},{1,9},{9... | collective-permute-start | bytes 294920 | tf_op jit(solution)/shard_map/ppermute | solution.py:246
  52.5 4.3 %collective-permute-start.17 = (bf16[128,256]{1,0:T(8,128)(2,1)S(1)}, bf16[128,256]{1,0:T(8,128)(2,1)S(1)}, u32[]{:S(2)}, u32[]{:S(2)}) collective-permute-start(bf16[128,256]{1,0:T(8,128)(2,1)S(1)} %collective-permute-done.16.refs_4_), channel_id=1, source_target_pairs={{0,8},{8,0},{16,24},{24,16},{28,20},{20,28},{12,4},{4,12},{1,9},{9... | collective-permute-start | bytes 196616 | tf_op jit(solution)/shard_map/ppermute | solution.py:289
  56.8 4.3 %collective-permute-start.18 = (bf16[128,256]{1,0:T(8,128)(2,1)S(1)}, bf16[128,256]{1,0:T(8,128)(2,1)S(1)}, u32[]{:S(2)}, u32[]{:S(2)}) collective-permute-start(bf16[128,256]{1,0:T(8,128)(2,1)S(1)} %collective-permute-done.17.refs_5_), channel_id=1, source_target_pairs={{0,4},{8,16},{16,8},{24,28},{28,24},{20,12},{12,20},{4,0},{1,5},{9... | collective-permute-start | bytes 196616 | tf_op jit(solution)/shard_map/ppermute | solution.py:289
  63.3 4.9 %collective-permute-start.25 = (bf16[128,512]{1,0:T(8,128)(2,1)S(1)}, bf16[128,512]{1,0:T(8,128)(2,1)S(1)}, u32[]{:S(2)}, u32[]{:S(2)}) collective-permute-start(bf16[128,512]{1,0:T(8,128)(2,1)S(1)} %attend.7), channel_id=1, source_target_pairs={{0,3},{1,2},{2,1},{3,0},{4,7},{5,6},{6,5},{7,4},{8,11},{9,10},{10,... | collective-permute-start | bytes 393224 | tf_op jit(solution)/shard_map/ppermute | solution.py:27
  65.6 6.1 %collective-permute-start.24 = (bf16[128,512]{1,0:T(8,128)(2,1)S(1)}, bf16[128,512]{1,0:T(8,128)(2,1)S(1)}, u32[]{:S(2)}, u32[]{:S(2)}) collective-permute-start(bf16[128,512]{1,0:T(8,128)(2,1)S(1)} %attend.6), channel_id=1, source_target_pairs={{0,2},{1,3},{2,0},{3,1},{4,6},{5,7},{6,4},{7,5},{8,10},{9,11},{10,... | collective-permute-start | bytes 393224 | tf_op jit(solution)/shard_map/ppermute | solution.py:27

commit v3 on v2

--- a/solution.py
+++ b/solution.py
@@ -1,4 +1,5 @@
 import functools
+import math
 
 import jax
 import jax.numpy as jnp
@@ -41,7 +42,7 @@
     return (jnp.cos(angles), jnp.sin(angles))
 
 
-def project_kernel(places, table_rows, early, info_ref, *refs):
+def project_kernel(places, table_rows, early, ready, info_ref, *refs):
     token_refs = list(refs[:len(places)])
     refs = list(refs[len(places):])
     gain_ref, wq_ref, wk_ref, wv_ref, table_ref, q_ref, kv_ref = refs[:7]
@@ -50,6 +51,7 @@
     copies = []
     if early:
         sources = (gain_ref, token_refs[0], wk_ref, wv_ref, wq_ref)
+        send_ref, refs = refs[0], refs[1:]
         held, refs = refs[:1] + refs[5:6] + refs[1:4], refs[4:5] + refs[6:]
         sems = refs[1]
         gain_ref, token_refs[0], wk_ref, wv_ref, wq_ref = held
@@ -67,6 +69,9 @@
             copies[1].wait()
         first = place(core)
         ref = token_refs[piece]
+        if ready:
+            normed[pl.ds(pl.multiple_of(first, BAND), ref.shape[0]), :] = ref[...]
+            continue
 
         def norm_band(index, carry, ref=ref, first=first):
             at = pl.ds(pl.multiple_of(index * BAND, BAND), BAND)
@@ -79,6 +84,8 @@
 
         lax.fori_loop(0, ref.shape[0] // BAND, norm_band, 0, unroll=2)
 
+    if early:
+        send_ref[...] = normed[early:token_refs[0].shape[0], :]
     half = HEAD_WIDTH // 2
 
     def rotate(value, rows):
@@ -129,7 +136,7 @@
             row += count
 
 
-def project(info, pieces, places, table_rows, gain, w_query, key_weight, value_weight, table, early=False):
+def project(info, pieces, places, table_rows, gain, w_query, key_weight, value_weight, table, early=0, ready=False):
     width = gain.shape[1]
     q_cols, k_cols = w_query.shape[1], key_weight.shape[1]
     total = sum(count for _, count in table_rows)
@@ -144,6 +151,7 @@
         scratch.append(pltpu.VMEM(pieces[0].shape, pieces[0].dtype))
         scratch.append(pltpu.SemaphoreType.DMA((5,)))
         params = tuple(in_hbm(array) for array in params)
+        shapes.append(jax.ShapeDtypeStruct((pieces[0].shape[0] - early, width), jnp.bfloat16))
         shapes += [
             jax.ShapeDtypeStruct(array.shape, array.dtype)
             for array in (gain, key_weight, value_weight, w_query)
@@ -151,7 +159,7 @@
         pieces = [in_hbm(pieces[0])] + list(pieces[1:])
         kind = [HBM] + [VMEM] * (len(pieces) - 1) + [HBM] * len(params)
     return pl.pallas_call(
-        functools.partial(project_kernel, places, table_rows, early),
+        functools.partial(project_kernel, places, table_rows, early, ready),
         in_specs=[SMEM] + kind + [VMEM],
         out_specs=[VMEM] * len(shapes),
         out_shape=shapes,
@@ -166,25 +174,19 @@
     )(info, *pieces, *params, table)
 
 
-def cut_kernel(source, *refs):
-    sems = refs[-1]
-    copies, first = [], 0
-    for at, target in enumerate(refs[:-1]):
-        count = target.shape[0]
-        copies.append(pltpu.make_async_copy(source.at[pl.ds(first, count)], target, sems.at[at]))
-        copies[-1].start()
-        first += count
-    for copy in copies:
-        copy.wait()
-
-
-def cut(array, counts):
+def cut_kernel(source, target, sem):
+    copy = pltpu.make_async_copy(source.at[pl.ds(0, target.shape[0])], target, sem)
+    copy.start()
+    copy.wait()
+
+
+def cut(array, rows):
     return pl.pallas_call(
         cut_kernel,
         in_specs=[HBM],
-        out_specs=[VMEM] * len(counts),
-        out_shape=[jax.ShapeDtypeStruct((rows,) + array.shape[1:], array.dtype) for rows in counts],
-        scratch_shapes=[pltpu.SemaphoreType.DMA((len(counts),))],
+        out_specs=VMEM,
+        out_shape=jax.ShapeDtypeStruct((rows,) + array.shape[1:], array.dtype),
+        scratch_shapes=[pltpu.SemaphoreType.DMA],
         compiler_params=pltpu.CompilerParams(vmem_limit_bytes=16 * MIB),
         name="cut",
     )(in_hbm(array))
@@ -353,14 +355,14 @@
     out_refs = refs[len(state_refs):]
     heads = kv_refs[0].shape[1] // (2 * HEAD_WIDTH)
     place = plan_ref[0]
-    factor = HEAD_WIDTH ** (-0.5)
+    factor = HEAD_WIDTH ** (-0.5) * math.log2(math.e)
 
     for lane, (mask, segments, (kv_first, keys_in, base)) in enumerate(lanes):
         rows = sum(count for _, _, count in segments)
         rank = QUERY_GROUP * rows
-        span = len(slots) * keys_in
-        query_at = place * rows + lax.broadcasted_iota(jnp.int32, (rows, span), 0)
-        column_at = lax.broadcasted_iota(jnp.int32, (1, span), 1)
+        row_at = place * rows + lax.broadcasted_iota(jnp.int32, (1, rows), 1)
+        query_at = jnp.concatenate([row_at] * QUERY_GROUP, axis=1)
+        key_at = base + lax.broadcasted_iota(jnp.int32, (keys_in, rank), 0)
         for head in range(heads):
             table = 1 + ((kind * documents + mask) * heads + head) * len(slots) * chunks
             queries = jnp.concatenate(
@@ -391,64 +393,61 @@
 
                 keys, values = column(2 * head), column(2 * head + 1)
                 scores = lax.dot_general(
-                    queries, keys, (((1,), (1,)), ((), ())), preferred_element_type=jnp.float32
-                ) * factor
-                key_at = jnp.zeros((1, span), jnp.int32)
+                    keys, queries, (((1,), (1,)), ((), ())), preferred_element_type=jnp.float32
+                )
+                parts = []
                 for j in range(len(slots)):
-                    shift = plan_ref[table + index * len(slots) + j] + (base - j * keys_in)
-                    inside = (column_at >= j * keys_in) & (column_at < (j + 1) * keys_in)
-                    key_at = jnp.where(inside, column_at + shift, key_at)
-                bias = jnp.where(key_at <= query_at, jnp.float32(0), -jnp.inf)
-                scores = (scores.reshape(QUERY_GROUP, rows, span) + bias[None]).reshape(rank, span)
-                top = jnp.max(scores, axis=1, keepdims=True)
+                    shift = plan_ref[table + index * len(slots) + j]
+                    parts.append(
+                        jnp.where(
+                            key_at <= query_at - shift,
+                            scores[j * keys_in:(j + 1) * keys_in],
+                            -jnp.inf,
+                        )
+                    )
+                scores = jnp.concatenate(parts, axis=0)
+                top = jnp.max(scores, axis=0, keepdims=True)
                 if carry is None:
-                    raised = jnp.exp(scores - top)
-                    return (
-                        top,
-                        jnp.sum(raised, axis=1, keepdims=True),
-                        jnp.dot(
-                            raised.astype(jnp.bfloat16), values, preferred_element_type=jnp.float32
-                        ),
-                    )
-                highest, total, mixed = carry
-                fresh = jnp.maximum(highest, top)
-                safe = jnp.where(fresh == -jnp.inf, jnp.float32(0), fresh)
-                fade = jnp.exp(highest - safe)
-                raised = jnp.exp(scores - safe)
-                part = jnp.sum(raised, axis=1, keepdims=True)
-                product = jnp.dot(
-                    raised.astype(jnp.bfloat16), values, preferred_element_type=jnp.float32
+                    fresh = safe = top
+                else:
+                    fresh = jnp.maximum(carry[0], top)
+                    safe = jnp.where(fresh == -jnp.inf, jnp.float32(0), fresh)
+                raised = jnp.exp2((scores - safe) * factor)
+                total = jnp.sum(raised, axis=0, keepdims=True)
+                mixed = lax.dot_general(
+                    values,
+                    raised.astype(jnp.bfloat16),
+                    (((0,), (0,)), ((), ())),
+                    preferred_element_type=jnp.float32,
                 )
-                return fresh, total * fade + part, mixed * fade + product
-
-            band = slice(head * rank, (head + 1) * rank)
+                if carry is not None:
+                    fade = jnp.exp2((carry[0] - safe) * factor)
+                    total, mixed = carry[1] * fade + total, carry[2] * fade + mixed
+                return fresh, total, mixed
+
             carry = None
             if not begin:
-                top_ref, total_ref, mixed_ref = state_refs[3 * lane:3 * lane + 3]
-                carry = (top_ref[band, :1], total_ref[band, :1], mixed_ref[band, :])
+                carry = tuple(ref[head] for ref in state_refs[3 * lane:3 * lane + 3])
             elif chunks > 1:
                 carry = (
-                    jnp.full((rank, 1), -jnp.inf, jnp.float32),
-                    jnp.zeros((rank, 1), jnp.float32),
-                    jnp.zeros((rank, HEAD_WIDTH), jnp.float32),
+                    jnp.full((1, rank), -jnp.inf, jnp.float32),
+                    jnp.zeros((1, rank), jnp.float32),
+                    jnp.zeros((HEAD_WIDTH, rank), jnp.float32),
                 )
             if chunks > 1:
                 carry = lax.fori_loop(0, chunks, step, carry)
             else:
                 carry = step(0, carry)
-            top, total, mixed = carry
             if not end:
-                top_ref, total_ref, mixed_ref = out_refs[3 * lane:3 * lane + 3]
-                top_ref[band, :] = jnp.broadcast_to(top, (rank, HEAD_WIDTH))
-                total_ref[band, :] = jnp.broadcast_to(total, (rank, HEAD_WIDTH))
-                mixed_ref[band, :] = mixed
+                for ref, value in zip(out_refs[3 * lane:3 * lane + 3], carry):
+                    ref[head] = value
                 continue
-            result = (mixed / total).astype(jnp.bfloat16)
+            result = carry[2] / carry[1]
             for h in range(QUERY_GROUP):
                 cols = slice(
                     (head * QUERY_GROUP + h) * HEAD_WIDTH, (head * QUERY_GROUP + h + 1) * HEAD_WIDTH
                 )
-                out_refs[lane][:, cols] = result[h * rows:(h + 1) * rows]
+                out_refs[lane][:, cols] = result[:, h * rows:(h + 1) * rows].T.astype(jnp.bfloat16)
 
 
 def attend(table, lanes, queries, spread, states=None, end=True):
@@ -460,8 +459,11 @@
     if end:
         shapes = [jax.ShapeDtypeStruct((rows, q_cols), jnp.bfloat16)] * len(lanes)
     else:
-        shape = (rows * q_cols // HEAD_WIDTH, HEAD_WIDTH)
-        shapes = [jax.ShapeDtypeStruct(shape, jnp.float32)] * (3 * len(lanes))
+        heads = q_cols // (QUERY_GROUP * HEAD_WIDTH)
+        shapes = [
+            jax.ShapeDtypeStruct((heads, deep, QUERY_GROUP * rows), jnp.float32)
+            for deep in (1, 1, HEAD_WIDTH)
+        ] * len(lanes)
     kernel = functools.partial(
         attend_kernel,
         lanes,
@@ -534,9 +536,8 @@
     tail = rows - head
 
     twin = swap(own, "doc", 1)
-    send_head, send_tail = cut(own, (head, tail))
-    got_head = swap(send_head, "doc", 2)
-    q_near, kv_near, gain_in, wk_in, wv_in, wq_in = project(
+    got_head = swap(cut(own, head), "doc", 2)
+    q_near, kv_near, send_tail, gain_in, wk_in, wv_in, wq_in = project(
         info,
         [own, twin],
         [lambda c: 0, lambda c: rows],
@@ -544,7 +545,7 @@
         gain,
         *weights,
         table,
-        early=True,
+        early=head,
     )
     params = (gain_in, wq_in, wk_in, wv_in, table)
     near = ring(kv_near)
@@ -575,6 +576,7 @@
         [lambda c: 0, lambda c: tail],
         [(head, tail), (head, tail)],
         *params,
+        ready=True,
     )
     late = pairs(kv_tail)
     late.advance()
@@ -585,7 +587,7 @@
         near,
     )
     out_twin = swap(mixed_twin, "doc", 1)
-    early.advance(kv_tail)
+    early.advance(mixed_twin)
     late.advance(mixed_twin)
     early.advance()
     late.advance()

time: 73.2 us -> 69.5 us (0.949)
  Pallas kernels: 25.8 us -> 22.8 us
    pallas_call x4, Pallas kernels: 9.5 us -> 6.79 us  [attend(): pl.pallas_call(kernel, in_specs=[SMEM] + [VMEM] * (len(queries) + len(arr...]
    ppermute x14, starting transfers between devices: 16.7 us -> 14.1 us  [advance(): self.front[way] = lax.ppermute(value, 'seq', pairs)]
    ppermute x4, starting transfers between devices: 4.09 us -> 6.17 us  [advance(): got = lax.ppermute(value, 'seq', pairs)]
    ppermute x4, waiting for transfers between devices: 4.86 us -> 3.29 us  [advance(): got = lax.ppermute(value, 'seq', pairs)]
    ppermute x14, waiting for transfers between devices: 6.32 us -> 7.43 us  [advance(): self.front[way] = lax.ppermute(value, 'seq', pairs)]
  transfers between devices with their start and end apart: 26 -> 26, of which waited for: 10 -> 10; matrix products, arithmetic and copies ran while one was open for 1% -> 1% of each run, Pallas kernels for 31% -> 30%
where the time goes in v3:
time: 69.5 us; the launch traced here: 69.4 us
  starting transfers between devices  25.7 us (37%)
  Pallas kernels  22.8 us (33%)
  waiting for transfers between devices  20.1 us (29%)
    ppermute x14, starting transfers between devices, advance(): self.front[way] = lax.ppermute(value, 'seq', pairs)  14.1 us
    pallas_call x3, Pallas kernels, project(): pl.pallas_call(functools.partial(project_kernel, places, table_rows, earl...  10.2 us
    ppermute x8, waiting for transfers between devices, swap(): lax.ppermute(value, axis, [(source, source ^ mask) for source in range(co...  9.38 us
    ppermute x14, waiting for transfers between devices, advance(): self.front[way] = lax.ppermute(value, 'seq', pairs)  7.43 us
    pallas_call x4, Pallas kernels, attend(): pl.pallas_call(kernel, in_specs=[SMEM] + [VMEM] * (len(queries) + len(arr...  6.79 us
    ppermute x4, starting transfers between devices, advance(): got = lax.ppermute(value, 'seq', pairs)  6.17 us
    ppermute x8, starting transfers between devices, swap(): lax.ppermute(value, axis, [(source, source ^ mask) for source in range(co...  5.49 us
    ppermute x4, waiting for transfers between devices, advance(): got = lax.ppermute(value, 'seq', pairs)  3.29 us
  transfers between devices with their start and end apart: 26, of which 10 were waited for; matrix products, arithmetic and copies ran while one was open for 1% of the time, Pallas kernels for 30%

profile of v3, /device:TPU:0, one launch (start us, length us, event | category | flops | bytes accessed | tf_op | source)
XLA Modules:
  0.0 69.4 jit_solution(1137546107561193005)
XLA Ops:
  0.5 1.1 %cut.1 = bf16[96,4096]{1,0:T(8,128)(2,1)S(1)} custom-call(bf16[128,4096]{1,0:T(8,128)(2,1)} %bitcast.5), custom_call_target="tpu_custom_call" | custom-call | tf_op jit(solution)/shard_map/cut/pallas_call | solution.py:184
  1.6 2.6 %collective-permute-start = (bf16[96,4096]{1,0:T(8,128)(2,1)S(1)}, bf16[96,4096]{1,0:T(8,128)(2,1)S(1)}, u32[]{:S(2)}, u32[]{:S(2)}) collective-permute-start(bf16[96,4096]{1,0:T(8,128)(2,1)S(1)} %cut.1), channel_id=1, source_target_pairs={{0,2},{1,3},{2,0},{3,1},{4,6},{5,7},{6,4},{7,5},{8,10},{9,11},{10,... | collective-permute-start | bytes 2359304 | tf_op jit(solution)/shard_map/ppermute | solution.py:28
  4.7 5.2 %project.3 = (bf16[256,512]{1,0:T(8,128)(2,1)S(1)}, bf16[256,256]{1,0:T(8,128)(2,1)S(1)}, bf16[32,4096]{1,0:T(8,128)(2,1)S(1)}, f32[1,4096]{1,0:T(1,128)S(1)}, b...) custom-call(s32[2]{0:T(128)S(1)} %pad_add_fusion.info_ref, ...), custom_call_target="tpu_custom_call" | custom-call | flops 1610612736 | bytes 8388608 | tf_op jit(solution)/shard_map/project/pallas_call | solution.py:161
  9.9 1.6 %collective-permute-start.2 = (bf16[256,256]{1,0:T(8,128)(2,1)S(1)}, bf16[256,256]{1,0:T(8,128)(2,1)S(1)}, u32[]{:S(2)}, u32[]{:S(2)}) collective-permute-start(bf16[256,256]{1,0:T(8,128)(2,1)S(1)} %get-tuple-element.34.refs_1_), channel_id=1, source_target_pairs={{0,8},{8,16},{16,24},{24,28},{28,20},{20,12},{12,4},{4,0},{1,9},{9... | collective-permute-start | bytes 393224 | tf_op jit(solution)/shard_map/ppermute | solution.py:248
  12.0 2.2 %plan.1.plan_ref = s32[65]{0:T(128)S(1)} custom-call(s32[2]{0:T(128)S(1)} %pad_add_fusion.info_ref, s32[4,4,4]{2,1,0:T(4,128)S(1)} %copy-done, s32[4,4,4]{2,1,0:T(4,128)S(1)} %copy-done.1), custom_call_target="tpu_custom_call" | custom-call | tf_op jit(solution)/shard_map/plan/pallas_call | solution.py:342
  14.2 1.4 %collective-permute-done.2.refs_2_ = bf16[256,256]{1,0:T(8,128)(2,1)S(1)} collective-permute-done((bf16[256,256]{1,0:T(8,128)(2,1)S(1)}, bf16[256,256]{1,0:T(8,128)(2,1)S(1)}, u32[]{:S(2)}, u32[]{:S(2)}) %collective-permute-start.2) | collective-permute-done | bytes 131104 | tf_op jit(solution)/shard_map/ppermute | solution.py:248
  15.6 1.6 %collective-permute-start.3 = (bf16[256,256]{1,0:T(8,128)(2,1)S(1)}, bf16[256,256]{1,0:T(8,128)(2,1)S(1)}, u32[]{:S(2)}, u32[]{:S(2)}) collective-permute-start(bf16[256,256]{1,0:T(8,128)(2,1)S(1)} %collective-permute-done.2.refs_2_), channel_id=1, source_target_pairs={{0,8},{8,16},{16,24},{24,28},{28,20},{20,12},{12,4},{4,0},{1,9},{9... | collective-permute-start | bytes 393224 | tf_op jit(solution)/shard_map/ppermute | solution.py:248
  17.6 4.7 %collective-permute-done.refs_0_ = bf16[96,4096]{1,0:T(8,128)(2,1)S(1)} collective-permute-done((bf16[96,4096]{1,0:T(8,128)(2,1)S(1)}, bf16[96,4096]{1,0:T(8,128)(2,1)S(1)}, u32[]{:S(2)}, u32[]{:S(2)}) %collective-permute-start) | collective-permute-done | bytes 786464 | tf_op jit(solution)/shard_map/ppermute | solution.py:28
  22.4 1.8 %collective-permute-start.7 = (bf16[32,4096]{1,0:T(8,128)(2,1)S(1)}, bf16[32,4096]{1,0:T(8,128)(2,1)S(1)}, u32[]{:S(2)}, u32[]{:S(2)}) collective-permute-start(bf16[32,4096]{1,0:T(8,128)(2,1)S(1)} %get-tuple-element.45), channel_id=1, source_target_pairs={{0,2},{1,3},{2,0},{3,1},{4,6},{5,7},{6,4},{7,5},{8,10},{9,11},{10,... | collective-permute-start | bytes 786440 | tf_op jit(solution)/shard_map/ppermute | solution.py:28
  24.2 1.6 %collective-permute-start.8 = (bf16[256,256]{1,0:T(8,128)(2,1)S(1)}, bf16[256,256]{1,0:T(8,128)(2,1)S(1)}, u32[]{:S(2)}, u32[]{:S(2)}) collective-permute-start(bf16[256,256]{1,0:T(8,128)(2,1)S(1)} %collective-permute-done.3.refs_4_), channel_id=1, source_target_pairs={{0,8},{8,16},{16,24},{24,28},{28,20},{20,12},{12,4},{4,0},{1,9},{9... | collective-permute-start | bytes 393224 | tf_op jit(solution)/shard_map/ppermute | solution.py:248
  26.2 3.2 %project.4 = (bf16[192,512]{1,0:T(8,128)(2,1)S(1)}, bf16[192,256]{1,0:T(8,128)(2,1)S(1)}) custom-call(s32[2]{0:T(128)S(1)} %pad_add_fusion.info_ref, bf16[96,4096]{1,0:T(8,128)(2,1)S(1)} %collective-permute-done.refs_0_, bf16[96,4096]{1,0:T(8,128)(2,1)S(1)} %collective-permute-done.6.refs_1_, f32[1,4096]{1,0:T(1,128)S(1)} %get-tuple-element.38.refs_2_, ...), custom_call_target="tpu_custom_call" | custom-call | flops 1207959552 | bytes 7864320 | tf_op jit(solution)/shard_map/project/pallas_call | solution.py:161
  29.4 1.6 %collective-permute-start.10 = (bf16[192,256]{1,0:T(8,128)(2,1)S(1)}, bf16[192,256]{1,0:T(8,128)(2,1)S(1)}, u32[]{:S(2)}, u32[]{:S(2)}) collective-permute-start(bf16[192,256]{1,0:T(8,128)(2,1)S(1)} %get-tuple-element.46.refs_2_), channel_id=1, source_target_pairs={{0,8},{8,16},{16,24},{24,28},{28,20},{20,12},{12,4},{4,0},{1,9},{9... | collective-permute-start | bytes 294920 | tf_op jit(solution)/shard_map/ppermute | solution.py:248
  31.5 2.6 %collective-permute-done.10.refs_3_ = bf16[192,256]{1,0:T(8,128)(2,1)S(1)} collective-permute-done((bf16[192,256]{1,0:T(8,128)(2,1)S(1)}, bf16[192,256]{1,0:T(8,128)(2,1)S(1)}, u32[]{:S(2)}, u32[]{:S(2)}) %collective-permute-start.10) | collective-permute-done | bytes 98336 | tf_op jit(solution)/shard_map/ppermute | solution.py:248
  34.1 1.6 %collective-permute-done.11.refs_4_ = bf16[192,256]{1,0:T(8,128)(2,1)S(1)} collective-permute-done((bf16[192,256]{1,0:T(8,128)(2,1)S(1)}, bf16[192,256]{1,0:T(8,128)(2,1)S(1)}, u32[]{:S(2)}, u32[]{:S(2)}) %collective-permute-start.11) | collective-permute-done | bytes 98336 | tf_op jit(solution)/shard_map/ppermute | solution.py:248
  35.7 1.6 %collective-permute-start.13 = (bf16[256,256]{1,0:T(8,128)(2,1)S(1)}, bf16[256,256]{1,0:T(8,128)(2,1)S(1)}, u32[]{:S(2)}, u32[]{:S(2)}) collective-permute-start(bf16[256,256]{1,0:T(8,128)(2,1)S(1)} %collective-permute-done.8.refs_6_), channel_id=1, source_target_pairs={{0,8},{8,16},{16,24},{24,28},{28,20},{20,12},{12,4},{4,0},{1,9},{9... | collective-permute-start | bytes 393224 | tf_op jit(solution)/shard_map/ppermute | solution.py:248
  37.2 1.6 %collective-permute-start.19 = (bf16[192,256]{1,0:T(8,128)(2,1)S(1)}, bf16[192,256]{1,0:T(8,128)(2,1)S(1)}, u32[]{:S(2)}, u32[]{:S(2)}) collective-permute-start(bf16[192,256]{1,0:T(8,128)(2,1)S(1)} %collective-permute-done.10.refs_3_), channel_id=1, source_target_pairs={{0,8},{8,16},{16,24},{24,28},{28,20},{20,12},{12,4},{4,0},{1,9},{9... | collective-permute-start | bytes 294920 | tf_op jit(solution)/shard_map/ppermute | solution.py:248
  39.3 1.8 %project.5 = (bf16[64,512]{1,0:T(8,128)(2,1)S(1)}, bf16[64,256]{1,0:T(8,128)(2,1)S(1)}) custom-call(s32[2]{0:T(128)S(1)} %pad_add_fusion.info_ref, bf16[32,4096]{1,0:T(8,128)(2,1)S(1)} %collective-permute-done.7.refs_0_, bf16[32,4096]{1,0:T(8,128)(2,1)S(1)} %collective-permute-done.12.refs_1_, f32[1,4096]{1,0:T(1,128)S(1)} %get-tuple-element.38.refs_2_, ...), custom_call_target="tpu_custom_call" | custom-call | flops 402653184 | bytes 6815744 | tf_op jit(solution)/shard_map/project/pallas_call | solution.py:161
  41.1 1.7 %collective-permute-start.15 = (bf16[64,256]{1,0:T(8,128)(2,1)S(1)}, bf16[64,256]{1,0:T(8,128)(2,1)S(1)}, u32[]{:S(2)}, u32[]{:S(2)}) collective-permute-start(bf16[64,256]{1,0:T(8,128)(2,1)S(1)} %get-tuple-element.48.refs_2_), channel_id=1, source_target_pairs={{0,8},{8,0},{16,24},{24,16},{28,20},{20,28},{12,4},{4,12},{1,9},{9... | collective-permute-start | bytes 98312 | tf_op jit(solution)/shard_map/ppermute | solution.py:291
  42.7 2.5 %attend.4 = (bf16[128,512]{1,0:T(8,128)(2,1)S(1)}, bf16[128,512]{1,0:T(8,128)(2,1)S(1)}) custom-call(s32[65]{0:T(128)S(1)} %plan.1.plan_ref, bf16[256,512]{1,0:T(8,128)(2,1)S(1)} %get-tuple-element.49.refs_0_, bf16[256,256]{1,0:T(8,128)(2,1)S(1)} %get-tuple-element.34.refs_1_, bf16[256,256]{1,0:T(8,128)(2,1)S(1)} %collective-permute-done.2.refs_2_, ...), custom_call_target="tpu_custom_call" | custom-call | flops 536870912 | bytes 1572864 | tf_op jit(solution)/shard_map/attend/pallas_call | solution.py:479
  45.3 0.8 %collective-permute-start.21 = (bf16[192,256]{1,0:T(8,128)(2,1)S(1)}, bf16[192,256]{1,0:T(8,128)(2,1)S(1)}, u32[]{:S(2)}, u32[]{:S(2)}) collective-permute-start(bf16[192,256]{1,0:T(8,128)(2,1)S(1)} %collective-permute-done.19.refs_5_), channel_id=1, source_target_pairs={{0,8},{8,16},{16,24},{24,28},{28,20},{20,12},{12,4},{4,0},{1,9},{9... | collective-permute-start | bytes 294920 | tf_op jit(solution)/shard_map/ppermute | solution.py:248
  46.1 1.3 %collective-permute-start.16 = (bf16[128,256]{1,0:T(8,128)(2,1)S(1)}, bf16[128,256]{1,0:T(8,128)(2,1)S(1)}, u32[]{:S(2)}, u32[]{:S(2)}) collective-permute-start(bf16[128,256]{1,0:T(8,128)(2,1)S(1)} %pad_maximum_fusion.1), channel_id=1, source_target_pairs={{0,4},{8,16},{16,8},{24,28},{28,24},{20,12},{12,20},{4,0},{1,5},{9... | collective-permute-start | bytes 196616 | tf_op jit(solution)/shard_map/ppermute | solution.py:291
  48.2 1.9 %collective-permute-done.21.refs_7_ = bf16[192,256]{1,0:T(8,128)(2,1)S(1)} collective-permute-done((bf16[192,256]{1,0:T(8,128)(2,1)S(1)}, bf16[192,256]{1,0:T(8,128)(2,1)S(1)}, u32[]{:S(2)}, u32[]{:S(2)}) %collective-permute-start.21) | collective-permute-done | bytes 98336 | tf_op jit(solution)/shard_map/ppermute | solution.py:248
  50.8 1.9 %collective-permute-start.17 = (bf16[128,256]{1,0:T(8,128)(2,1)S(1)}, bf16[128,256]{1,0:T(8,128)(2,1)S(1)}, u32[]{:S(2)}, u32[]{:S(2)}) collective-permute-start(bf16[128,256]{1,0:T(8,128)(2,1)S(1)} %collective-permute-done.16.refs_4_), channel_id=1, source_target_pairs={{0,8},{8,0},{16,24},{24,16},{28,20},{20,28},{12,4},{4,12},{1,9},{9... | collective-permute-start | bytes 196616 | tf_op jit(solution)/shard_map/ppermute | solution.py:291
  52.7 2.4 %collective-permute-done.17.refs_5_ = bf16[128,256]{1,0:T(8,128)(2,1)S(1)} collective-permute-done((bf16[128,256]{1,0:T(8,128)(2,1)S(1)}, bf16[128,256]{1,0:T(8,128)(2,1)S(1)}, u32[]{:S(2)}, u32[]{:S(2)}) %collective-permute-start.17) | collective-permute-done | bytes 65568 | tf_op jit(solution)/shard_map/ppermute | solution.py:291
  55.1 1.3 %collective-permute-start.18 = (bf16[128,256]{1,0:T(8,128)(2,1)S(1)}, bf16[128,256]{1,0:T(8,128)(2,1)S(1)}, u32[]{:S(2)}, u32[]{:S(2)}) collective-permute-start(bf16[128,256]{1,0:T(8,128)(2,1)S(1)} %collective-permute-done.17.refs_5_), channel_id=1, source_target_pairs={{0,4},{8,16},{16,8},{24,28},{28,24},{20,12},{12,20},{4,0},{1,5},{9... | collective-permute-start | bytes 196616 | tf_op jit(solution)/shard_map/ppermute | solution.py:291
  56.4 2.1 %attend.5 = (f32[1,1,512]{2,1,0:T(1,128)S(1)}, f32[1,1,512]{2,1,0:T(1,128)S(1)}, f32[1,128,512]{2,1,0:T(8,128)S(1)}, f32[1,1,512]{2,1,0:T(1,128)S(1)}, f32[1,1,5...) custom-call(s32[65]{0:T(128)S(1)} %plan.1.plan_ref, bf16[192,512]{1,0:T(8,128)(2,1)S(1)} %get-tuple-element.51.refs_0_, ...), custom_call_target="tpu_custom_call" | custom-call | flops 402653184 | bytes 1310720 | tf_op jit(solution)/shard_map/attend/pallas_call | solution.py:479
  59.3 1.1 %attend.7 = bf16[128,512]{1,0:T(8,128)(2,1)S(1)} custom-call(s32[65]{0:T(128)S(1)} %plan.1.plan_ref, bf16[192,512]{1,0:T(8,128)(2,1)S(1)} %get-tuple-element.51.refs_0_, bf16[64,512]{1,0:T(8,128)(2,1)S(1)} %get-tuple-element.52.refs_1_, bf16[64,256]{1,0:T(8,128)(2,1)S(1)} %get-tuple-element.48.refs_2_, bf16[64,256]{1,0:T(8,128)(2,1)S(1)} %collective-permute-done.15.refs_3_, ...), custom_call_target="tpu_custom_call" | custom-call | flops 67108864 | bytes 524288 | tf_op jit(solution)/shard_map/attend/pallas_call | solution.py:479
  60.5 1.1 %attend.6 = bf16[128,512]{1,0:T(8,128)(2,1)S(1)} custom-call(s32[65]{0:T(128)S(1)} %plan.1.plan_ref, bf16[192,512]{1,0:T(8,128)(2,1)S(1)} %get-tuple-element.51.refs_0_, bf16[64,512]{1,0:T(8,128)(2,1)S(1)} %get-tuple-element.52.refs_1_, bf16[64,256]{1,0:T(8,128)(2,1)S(1)} %get-tuple-element.48.refs_2_, bf16[64,256]{1,0:T(8,128)(2,1)S(1)} %collective-permute-done.15.refs_3_, ...), custom_call_target="tpu_custom_call" | custom-call | flops 67108864 | bytes 524288 | tf_op jit(solution)/shard_map/attend/pallas_call | solution.py:479
  62.2 1.3 %deliver.2.refs_2_ = bf16[1,128,2048]{2,1,0:T(8,128)(2,1)} custom-call(s32[2]{0:T(128)S(1)} %pad_add_fusion.info_ref, bf16[128,512]{1,0:T(8,128)(2,1)S(1)} %get-tuple-element.62.refs_0_, bf16[128,512]{1,0:T(8,128)(2,1)S(1)} %collective-permute-done.14.refs_1_), custom_call_target="tpu_custom_call" | custom-call | tf_op jit(solution)/shard_map/deliver/pallas_call | solution.py:509
  63.5 2.0 %collective-permute-done.25.refs_1_ = bf16[128,512]{1,0:T(8,128)(2,1)S(1)} collective-permute-done((bf16[128,512]{1,0:T(8,128)(2,1)S(1)}, bf16[128,512]{1,0:T(8,128)(2,1)S(1)}, u32[]{:S(2)}, u32[]{:S(2)}) %collective-permute-start.25) | collective-permute-done | bytes 131104 | tf_op jit(solution)/shard_map/ppermute | solution.py:28
  65.5 2.7 %collective-permute-done.24.refs_0_ = bf16[128,512]{1,0:T(8,128)(2,1)S(1)} collective-permute-done((bf16[128,512]{1,0:T(8,128)(2,1)S(1)}, bf16[128,512]{1,0:T(8,128)(2,1)S(1)}, u32[]{:S(2)}, u32[]{:S(2)}) %collective-permute-start.24) | collective-permute-done | bytes 131104 | tf_op jit(solution)/shard_map/ppermute | solution.py:28
  68.1 1.3 %deliver.3 = bf16[1,128,2048]{2,1,0:T(8,128)(2,1)} custom-call(s32[2]{0:T(128)S(1)} %pad_add_fusion.info_ref, bf16[128,512]{1,0:T(8,128)(2,1)S(1)} %collective-permute-done.24.refs_0_, bf16[128,512]{1,0:T(8,128)(2,1)S(1)} %collective-permute-done.25.refs_1_, bf16[1,128,2048]{2,1,0:T(8,128)(2,1)} %deliver.2.refs_2_), custom_call_target="tpu_custom_call", output_to_operand_aliasing={{}: (3, {})} | custom-call | tf_op jit(solution)/shard_map/deliver/pallas_call | solution.py:509
  (41 shorter events, 6.3 us)
Async XLA Ops:
  0.0 4.7 %collective-permute-start.1 = (bf16[128,4096]{1,0:T(8,128)(2,1)}, bf16[128,4096]{1,0:T(8,128)(2,1)S(1)}, u32[]{:S(2)}, u32[]{:S(2)}) collective-permute-start(bf16[128,4096]{1,0:T(8,128)(2,1)} %bitcast.4), channel_id=1, source_target_pairs={{0,1},{1,0},{2,3},{3,2},{4,5},{5,4},{6,7},{7,6},{8,9},{9,8},{10,11... | collective-permute-start | bytes 3145736 | tf_op jit(solution)/shard_map/ppermute | solution.py:28
  1.6 20.8 %collective-permute-start = (bf16[96,4096]{1,0:T(8,128)(2,1)S(1)}, bf16[96,4096]{1,0:T(8,128)(2,1)S(1)}, u32[]{:S(2)}, u32[]{:S(2)}) collective-permute-start(bf16[96,4096]{1,0:T(8,128)(2,1)S(1)} %cut.1), channel_id=1, source_target_pairs={{0,2},{1,3},{2,0},{3,1},{4,6},{5,7},{6,4},{7,5},{8,10},{9,11},{10,... | collective-permute-start | bytes 2359304 | tf_op jit(solution)/shard_map/ppermute | solution.py:28
  4.7 7.3 %copy-start = (s32[4,4,4]{2,1,0:T(4,128)S(1)}, s32[4,4,4]{2,1,0:T(4,128)}, u32[]{:S(2)}) copy-start(s32[4,4,4]{2,1,0:T(4,128)} %vertical_ref.1) | copy-start | bytes 772
  4.7 7.3 %copy-start.1 = (s32[4,4,4]{2,1,0:T(4,128)S(1)}, s32[4,4,4]{2,1,0:T(4,128)}, u32[]{:S(2)}) copy-start(s32[4,4,4]{2,1,0:T(4,128)} %slash_ref.1) | copy-start | bytes 772
  9.9 5.7 %collective-permute-start.2 = (bf16[256,256]{1,0:T(8,128)(2,1)S(1)}, bf16[256,256]{1,0:T(8,128)(2,1)S(1)}, u32[]{:S(2)}, u32[]{:S(2)}) collective-permute-start(bf16[256,256]{1,0:T(8,128)(2,1)S(1)} %get-tuple-element.34.refs_1_), channel_id=1, source_target_pairs={{0,8},{8,16},{16,24},{24,28},{28,20},{20,12},{12,4},{4,0},{1,9},{9... | collective-permute-start | bytes 393224 | tf_op jit(solution)/shard_map/ppermute | solution.py:248
  11.5 5.6 %collective-permute-start.4 = (bf16[256,256]{1,0:T(8,128)(2,1)S(1)}, bf16[256,256]{1,0:T(8,128)(2,1)S(1)}, u32[]{:S(2)}, u32[]{:S(2)}) collective-permute-start(bf16[256,256]{1,0:T(8,128)(2,1)S(1)} %get-tuple-element.34.refs_1_), channel_id=1, source_target_pairs={{0,4},{8,0},{16,8},{24,16},{28,24},{20,28},{12,20},{4,12},{1,5},{9... | collective-permute-start | bytes 393224 | tf_op jit(solution)/shard_map/ppermute | solution.py:248
  15.6 6.8 %collective-permute-start.3 = (bf16[256,256]{1,0:T(8,128)(2,1)S(1)}, bf16[256,256]{1,0:T(8,128)(2,1)S(1)}, u32[]{:S(2)}, u32[]{:S(2)}) collective-permute-start(bf16[256,256]{1,0:T(8,128)(2,1)S(1)} %collective-permute-done.2.refs_2_), channel_id=1, source_target_pairs={{0,8},{8,16},{16,24},{24,28},{28,20},{20,12},{12,4},{4,0},{1,9},{9... | collective-permute-start | bytes 393224 | tf_op jit(solution)/shard_map/ppermute | solution.py:248
  17.2 5.2 %collective-permute-start.5 = (bf16[256,256]{1,0:T(8,128)(2,1)S(1)}, bf16[256,256]{1,0:T(8,128)(2,1)S(1)}, u32[]{:S(2)}, u32[]{:S(2)}) collective-permute-start(bf16[256,256]{1,0:T(8,128)(2,1)S(1)} %collective-permute-done.4.refs_3_), channel_id=1, source_target_pairs={{0,4},{8,0},{16,8},{24,16},{28,24},{20,28},{12,20},{4,12},{1,5},{9... | collective-permute-start | bytes 393224 | tf_op jit(solution)/shard_map/ppermute | solution.py:248
  22.4 3.8 %collective-permute-start.6 = (bf16[96,4096]{1,0:T(8,128)(2,1)S(1)}, bf16[96,4096]{1,0:T(8,128)(2,1)S(1)}, u32[]{:S(2)}, u32[]{:S(2)}) collective-permute-start(bf16[96,4096]{1,0:T(8,128)(2,1)S(1)} %collective-permute-done.refs_0_), channel_id=1, source_target_pairs={{0,1},{1,0},{2,3},{3,2},{4,5},{5,4},{6,7},{7,6},{8,9},{9,8},{10,11... | collective-permute-start | bytes 2359304 | tf_op jit(solution)/shard_map/ppermute | solution.py:28
  22.4 9.1 %collective-permute-start.7 = (bf16[32,4096]{1,0:T(8,128)(2,1)S(1)}, bf16[32,4096]{1,0:T(8,128)(2,1)S(1)}, u32[]{:S(2)}, u32[]{:S(2)}) collective-permute-start(bf16[32,4096]{1,0:T(8,128)(2,1)S(1)} %get-tuple-element.45), channel_id=1, source_target_pairs={{0,2},{1,3},{2,0},{3,1},{4,6},{5,7},{6,4},{7,5},{8,10},{9,11},{10,... | collective-permute-start | bytes 786440 | tf_op jit(solution)/shard_map/ppermute | solution.py:28
  24.2 7.3 %collective-permute-start.8 = (bf16[256,256]{1,0:T(8,128)(2,1)S(1)}, bf16[256,256]{1,0:T(8,128)(2,1)S(1)}, u32[]{:S(2)}, u32[]{:S(2)}) collective-permute-start(bf16[256,256]{1,0:T(8,128)(2,1)S(1)} %collective-permute-done.3.refs_4_), channel_id=1, source_target_pairs={{0,8},{8,16},{16,24},{24,28},{28,20},{20,12},{12,4},{4,0},{1,9},{9... | collective-permute-start | bytes 393224 | tf_op jit(solution)/shard_map/ppermute | solution.py:248
  25.8 5.7 %collective-permute-start.9 = (bf16[256,256]{1,0:T(8,128)(2,1)S(1)}, bf16[256,256]{1,0:T(8,128)(2,1)S(1)}, u32[]{:S(2)}, u32[]{:S(2)}) collective-permute-start(bf16[256,256]{1,0:T(8,128)(2,1)S(1)} %collective-permute-done.5.refs_5_), channel_id=1, source_target_pairs={{0,4},{8,0},{16,8},{24,16},{28,24},{20,28},{12,20},{4,12},{1,5},{9... | collective-permute-start | bytes 393224 | tf_op jit(solution)/shard_map/ppermute | solution.py:248
  29.4 4.7 %collective-permute-start.10 = (bf16[192,256]{1,0:T(8,128)(2,1)S(1)}, bf16[192,256]{1,0:T(8,128)(2,1)S(1)}, u32[]{:S(2)}, u32[]{:S(2)}) collective-permute-start(bf16[192,256]{1,0:T(8,128)(2,1)S(1)} %get-tuple-element.46.refs_2_), channel_id=1, source_target_pairs={{0,8},{8,16},{16,24},{24,28},{28,20},{20,12},{12,4},{4,0},{1,9},{9... | collective-permute-start | bytes 294920 | tf_op jit(solution)/shard_map/ppermute | solution.py:248
  31.0 4.6 %collective-permute-start.11 = (bf16[192,256]{1,0:T(8,128)(2,1)S(1)}, bf16[192,256]{1,0:T(8,128)(2,1)S(1)}, u32[]{:S(2)}, u32[]{:S(2)}) collective-permute-start(bf16[192,256]{1,0:T(8,128)(2,1)S(1)} %get-tuple-element.46.refs_2_), channel_id=1, source_target_pairs={{0,4},{8,0},{16,8},{24,16},{28,24},{20,28},{12,20},{4,12},{1,5},{9... | collective-permute-start | bytes 294920 | tf_op jit(solution)/shard_map/ppermute | solution.py:248
  35.7 3.6 %collective-permute-start.12 = (bf16[32,4096]{1,0:T(8,128)(2,1)S(1)}, bf16[32,4096]{1,0:T(8,128)(2,1)S(1)}, u32[]{:S(2)}, u32[]{:S(2)}) collective-permute-start(bf16[32,4096]{1,0:T(8,128)(2,1)S(1)} %collective-permute-done.7.refs_0_), channel_id=1, source_target_pairs={{0,1},{1,0},{2,3},{3,2},{4,5},{5,4},{6,7},{7,6},{8,9},{9,8},{10,11... | collective-permute-start | bytes 786440 | tf_op jit(solution)/shard_map/ppermute | solution.py:28
  35.7 7.1 %collective-permute-start.13 = (bf16[256,256]{1,0:T(8,128)(2,1)S(1)}, bf16[256,256]{1,0:T(8,128)(2,1)S(1)}, u32[]{:S(2)}, u32[]{:S(2)}) collective-permute-start(bf16[256,256]{1,0:T(8,128)(2,1)S(1)} %collective-permute-done.8.refs_6_), channel_id=1, source_target_pairs={{0,8},{8,16},{16,24},{24,28},{28,20},{20,12},{12,4},{4,0},{1,9},{9... | collective-permute-start | bytes 393224 | tf_op jit(solution)/shard_map/ppermute | solution.py:248
  37.2 8.0 %collective-permute-start.19 = (bf16[192,256]{1,0:T(8,128)(2,1)S(1)}, bf16[192,256]{1,0:T(8,128)(2,1)S(1)}, u32[]{:S(2)}, u32[]{:S(2)}) collective-permute-start(bf16[192,256]{1,0:T(8,128)(2,1)S(1)} %collective-permute-done.10.refs_3_), channel_id=1, source_target_pairs={{0,8},{8,16},{16,24},{24,28},{28,20},{20,12},{12,4},{4,0},{1,9},{9... | collective-permute-start | bytes 294920 | tf_op jit(solution)/shard_map/ppermute | solution.py:248
  38.8 8.6 %collective-permute-start.20 = (bf16[192,256]{1,0:T(8,128)(2,1)S(1)}, bf16[192,256]{1,0:T(8,128)(2,1)S(1)}, u32[]{:S(2)}, u32[]{:S(2)}) collective-permute-start(bf16[192,256]{1,0:T(8,128)(2,1)S(1)} %collective-permute-done.11.refs_4_), channel_id=1, source_target_pairs={{0,4},{8,0},{16,8},{24,16},{28,24},{20,28},{12,20},{4,12},{1,5},{9... | collective-permute-start | bytes 294920 | tf_op jit(solution)/shard_map/ppermute | solution.py:248
  41.1 5.0 %collective-permute-start.15 = (bf16[64,256]{1,0:T(8,128)(2,1)S(1)}, bf16[64,256]{1,0:T(8,128)(2,1)S(1)}, u32[]{:S(2)}, u32[]{:S(2)}) collective-permute-start(bf16[64,256]{1,0:T(8,128)(2,1)S(1)} %get-tuple-element.48.refs_2_), channel_id=1, source_target_pairs={{0,8},{8,0},{16,24},{24,16},{28,20},{20,28},{12,4},{4,12},{1,9},{9... | collective-permute-start | bytes 98312 | tf_op jit(solution)/shard_map/ppermute | solution.py:291
  45.3 4.8 %collective-permute-start.21 = (bf16[192,256]{1,0:T(8,128)(2,1)S(1)}, bf16[192,256]{1,0:T(8,128)(2,1)S(1)}, u32[]{:S(2)}, u32[]{:S(2)}) collective-permute-start(bf16[192,256]{1,0:T(8,128)(2,1)S(1)} %collective-permute-done.19.refs_5_), channel_id=1, source_target_pairs={{0,8},{8,16},{16,24},{24,28},{28,20},{20,12},{12,4},{4,0},{1,9},{9... | collective-permute-start | bytes 294920 | tf_op jit(solution)/shard_map/ppermute | solution.py:248
  46.1 4.7 %collective-permute-start.16 = (bf16[128,256]{1,0:T(8,128)(2,1)S(1)}, bf16[128,256]{1,0:T(8,128)(2,1)S(1)}, u32[]{:S(2)}, u32[]{:S(2)}) collective-permute-start(bf16[128,256]{1,0:T(8,128)(2,1)S(1)} %pad_maximum_fusion.1), channel_id=1, source_target_pairs={{0,4},{8,16},{16,8},{24,28},{28,24},{20,12},{12,20},{4,0},{1,5},{9... | collective-permute-start | bytes 196616 | tf_op jit(solution)/shard_map/ppermute | solution.py:291
  47.4 9.0 %collective-permute-start.14 = (bf16[128,512]{1,0:T(8,128)(2,1)S(1)}, bf16[128,512]{1,0:T(8,128)(2,1)S(1)}, u32[]{:S(2)}, u32[]{:S(2)}) collective-permute-start(bf16[128,512]{1,0:T(8,128)(2,1)S(1)} %get-tuple-element.50), channel_id=1, source_target_pairs={{0,1},{1,0},{2,3},{3,2},{4,5},{5,4},{6,7},{7,6},{8,9},{9,8},{10,11... | collective-permute-start | bytes 393224 | tf_op jit(solution)/shard_map/ppermute | solution.py:28
  47.4 9.0 %collective-permute-start.22 = (bf16[192,256]{1,0:T(8,128)(2,1)S(1)}, bf16[192,256]{1,0:T(8,128)(2,1)S(1)}, u32[]{:S(2)}, u32[]{:S(2)}) collective-permute-start(bf16[192,256]{1,0:T(8,128)(2,1)S(1)} %collective-permute-done.20.refs_6_), channel_id=1, source_target_pairs={{0,4},{8,0},{16,8},{24,16},{28,24},{20,28},{12,20},{4,12},{1,5},{9... | collective-permute-start | bytes 294920 | tf_op jit(solution)/shard_map/ppermute | solution.py:248
  50.1 6.3 %collective-permute-start.23 = (bf16[192,256]{1,0:T(8,128)(2,1)S(1)}, bf16[192,256]{1,0:T(8,128)(2,1)S(1)}, u32[]{:S(2)}, u32[]{:S(2)}) collective-permute-start(bf16[192,256]{1,0:T(8,128)(2,1)S(1)} %collective-permute-done.21.refs_7_), channel_id=1, source_target_pairs={{0,8},{8,16},{16,24},{24,28},{28,20},{20,12},{12,4},{4,0},{1,9},{9... | collective-permute-start | bytes 294920 | tf_op jit(solution)/shard_map/ppermute | solution.py:248
  50.8 4.3 %collective-permute-start.17 = (bf16[128,256]{1,0:T(8,128)(2,1)S(1)}, bf16[128,256]{1,0:T(8,128)(2,1)S(1)}, u32[]{:S(2)}, u32[]{:S(2)}) collective-permute-start(bf16[128,256]{1,0:T(8,128)(2,1)S(1)} %collective-permute-done.16.refs_4_), channel_id=1, source_target_pairs={{0,8},{8,0},{16,24},{24,16},{28,20},{20,28},{12,4},{4,12},{1,9},{9... | collective-permute-start | bytes 196616 | tf_op jit(solution)/shard_map/ppermute | solution.py:291
  55.1 4.3 %collective-permute-start.18 = (bf16[128,256]{1,0:T(8,128)(2,1)S(1)}, bf16[128,256]{1,0:T(8,128)(2,1)S(1)}, u32[]{:S(2)}, u32[]{:S(2)}) collective-permute-start(bf16[128,256]{1,0:T(8,128)(2,1)S(1)} %collective-permute-done.17.refs_5_), channel_id=1, source_target_pairs={{0,4},{8,16},{16,8},{24,28},{28,24},{20,12},{12,20},{4,0},{1,5},{9... | collective-permute-start | bytes 196616 | tf_op jit(solution)/shard_map/ppermute | solution.py:291
  60.4 5.0 %collective-permute-start.25 = (bf16[128,512]{1,0:T(8,128)(2,1)S(1)}, bf16[128,512]{1,0:T(8,128)(2,1)S(1)}, u32[]{:S(2)}, u32[]{:S(2)}) collective-permute-start(bf16[128,512]{1,0:T(8,128)(2,1)S(1)} %attend.7), channel_id=1, source_target_pairs={{0,3},{1,2},{2,1},{3,0},{4,7},{5,6},{6,5},{7,4},{8,11},{9,10},{10,... | collective-permute-start | bytes 393224 | tf_op jit(solution)/shard_map/ppermute | solution.py:28
  61.6 6.5 %collective-permute-start.24 = (bf16[128,512]{1,0:T(8,128)(2,1)S(1)}, bf16[128,512]{1,0:T(8,128)(2,1)S(1)}, u32[]{:S(2)}, u32[]{:S(2)}) collective-permute-start(bf16[128,512]{1,0:T(8,128)(2,1)S(1)} %attend.6), channel_id=1, source_target_pairs={{0,2},{1,3},{2,0},{3,1},{4,6},{5,7},{6,4},{7,5},{8,10},{9,11},{10,... | collective-permute-start | bytes 393224 | tf_op jit(solution)/shard_map/ppermute | solution.py:28

commit v4 on v3

--- a/solution.py
+++ b/solution.py
@@ -566,10 +566,9 @@
     early = ring(kv_head)
     early.advance()
 
-    got_tail = after(got_tail, *near.latest, *early.latest)
+    got_tail = after(got_tail, *near.latest, kv_head)
     near.advance()
     tail_twin = swap(got_tail, "doc", 1)
-    early.advance()
     q_tail, kv_tail = project(
         info,
         [got_tail, tail_twin],
@@ -578,6 +577,7 @@
         *params,
         ready=True,
     )
+    early.advance(kv_tail)
     late = pairs(kv_tail)
     late.advance()
     mixed_own, mixed_twin = attend(

time: 69.5 us -> 69 us (level)
  waiting for transfers between devices: 20.1 us -> 17.5 us
  starting transfers between devices: 25.7 us -> 27.9 us
    ppermute x14, waiting for transfers between devices: 7.43 us -> 3.91 us  [advance(): self.front[way] = lax.ppermute(value, 'seq', pairs)]
    ppermute x14, starting transfers between devices: 14.1 us -> 17.1 us  [advance(): self.front[way] = lax.ppermute(value, 'seq', pairs)]
    ppermute x4, starting transfers between devices: 6.17 us -> 4.36 us  [advance(): got = lax.ppermute(value, 'seq', pairs)]
    ppermute x8, starting transfers between devices: 5.49 us -> 6.45 us  [swap(): lax.ppermute(value, axis, [(source, source ^ mask) for source in range(co...]
    ppermute x4, waiting for transfers between devices: 3.29 us -> 4.12 us  [advance(): got = lax.ppermute(value, 'seq', pairs)]
where the time goes in v4:
time: 69 us; the launch traced here: 68.9 us
  starting transfers between devices  27.9 us (40%)
  Pallas kernels  22.8 us (33%)
  waiting for transfers between devices  17.5 us (25%)
    ppermute x14, starting transfers between devices, advance(): self.front[way] = lax.ppermute(value, 'seq', pairs)  17.1 us
    pallas_call x3, Pallas kernels, project(): pl.pallas_call(functools.partial(project_kernel, places, table_rows, earl...  10.2 us
    ppermute x8, waiting for transfers between devices, swap(): lax.ppermute(value, axis, [(source, source ^ mask) for source in range(co...  9.47 us
    pallas_call x4, Pallas kernels, attend(): pl.pallas_call(kernel, in_specs=[SMEM] + [VMEM] * (len(queries) + len(arr...  6.78 us
    ppermute x8, starting transfers between devices, swap(): lax.ppermute(value, axis, [(source, source ^ mask) for source in range(co...  6.45 us
    ppermute x4, starting transfers between devices, advance(): got = lax.ppermute(value, 'seq', pairs)  4.36 us
    ppermute x4, waiting for transfers between devices, advance(): got = lax.ppermute(value, 'seq', pairs)  4.12 us
    ppermute x14, waiting for transfers between devices, advance(): self.front[way] = lax.ppermute(value, 'seq', pairs)  3.91 us
  transfers between devices with their start and end apart: 26, of which 10 were waited for; matrix products, arithmetic and copies ran while one was open for 1% of the time, Pallas kernels for 30%

profile of v4, /device:TPU:0, one launch (start us, length us, event | category | flops | bytes accessed | tf_op | source)
XLA Modules:
  0.0 68.9 jit_solution(7658169119178968967)
XLA Ops:
  0.5 1.1 %cut.1 = bf16[96,4096]{1,0:T(8,128)(2,1)S(1)} custom-call(bf16[128,4096]{1,0:T(8,128)(2,1)} %bitcast.5), custom_call_target="tpu_custom_call" | custom-call | tf_op jit(solution)/shard_map/cut/pallas_call | solution.py:184
  1.6 2.6 %collective-permute-start = (bf16[96,4096]{1,0:T(8,128)(2,1)S(1)}, bf16[96,4096]{1,0:T(8,128)(2,1)S(1)}, u32[]{:S(2)}, u32[]{:S(2)}) collective-permute-start(bf16[96,4096]{1,0:T(8,128)(2,1)S(1)} %cut.1), channel_id=1, source_target_pairs={{0,2},{1,3},{2,0},{3,1},{4,6},{5,7},{6,4},{7,5},{8,10},{9,11},{10,... | collective-permute-start | bytes 2359304 | tf_op jit(solution)/shard_map/ppermute | solution.py:28
  4.7 5.2 %project.3 = (bf16[256,512]{1,0:T(8,128)(2,1)S(1)}, bf16[256,256]{1,0:T(8,128)(2,1)S(1)}, bf16[32,4096]{1,0:T(8,128)(2,1)S(1)}, f32[1,4096]{1,0:T(1,128)S(1)}, b...) custom-call(s32[2]{0:T(128)S(1)} %pad_add_fusion.info_ref, ...), custom_call_target="tpu_custom_call" | custom-call | flops 1610612736 | bytes 8388608 | tf_op jit(solution)/shard_map/project/pallas_call | solution.py:161
  9.9 1.6 %collective-permute-start.2 = (bf16[256,256]{1,0:T(8,128)(2,1)S(1)}, bf16[256,256]{1,0:T(8,128)(2,1)S(1)}, u32[]{:S(2)}, u32[]{:S(2)}) collective-permute-start(bf16[256,256]{1,0:T(8,128)(2,1)S(1)} %get-tuple-element.36.refs_1_), channel_id=1, source_target_pairs={{0,8},{8,16},{16,24},{24,28},{28,20},{20,12},{12,4},{4,0},{1,9},{9... | collective-permute-start | bytes 393224 | tf_op jit(solution)/shard_map/ppermute | solution.py:248
  12.0 2.2 %plan.1.plan_ref = s32[65]{0:T(128)S(1)} custom-call(s32[2]{0:T(128)S(1)} %pad_add_fusion.info_ref, s32[4,4,4]{2,1,0:T(4,128)S(1)} %copy-done, s32[4,4,4]{2,1,0:T(4,128)S(1)} %copy-done.1), custom_call_target="tpu_custom_call" | custom-call | tf_op jit(solution)/shard_map/plan/pallas_call | solution.py:342
  14.2 1.4 %collective-permute-done.2.refs_2_ = bf16[256,256]{1,0:T(8,128)(2,1)S(1)} collective-permute-done((bf16[256,256]{1,0:T(8,128)(2,1)S(1)}, bf16[256,256]{1,0:T(8,128)(2,1)S(1)}, u32[]{:S(2)}, u32[]{:S(2)}) %collective-permute-start.2) | collective-permute-done | bytes 131104 | tf_op jit(solution)/shard_map/ppermute | solution.py:248
  15.6 1.6 %collective-permute-start.3 = (bf16[256,256]{1,0:T(8,128)(2,1)S(1)}, bf16[256,256]{1,0:T(8,128)(2,1)S(1)}, u32[]{:S(2)}, u32[]{:S(2)}) collective-permute-start(bf16[256,256]{1,0:T(8,128)(2,1)S(1)} %collective-permute-done.2.refs_2_), channel_id=1, source_target_pairs={{0,8},{8,16},{16,24},{24,28},{28,20},{20,12},{12,4},{4,0},{1,9},{9... | collective-permute-start | bytes 393224 | tf_op jit(solution)/shard_map/ppermute | solution.py:248
  17.6 4.7 %collective-permute-done.refs_0_ = bf16[96,4096]{1,0:T(8,128)(2,1)S(1)} collective-permute-done((bf16[96,4096]{1,0:T(8,128)(2,1)S(1)}, bf16[96,4096]{1,0:T(8,128)(2,1)S(1)}, u32[]{:S(2)}, u32[]{:S(2)}) %collective-permute-start) | collective-permute-done | bytes 786464 | tf_op jit(solution)/shard_map/ppermute | solution.py:28
  22.4 1.8 %collective-permute-start.7 = (bf16[32,4096]{1,0:T(8,128)(2,1)S(1)}, bf16[32,4096]{1,0:T(8,128)(2,1)S(1)}, u32[]{:S(2)}, u32[]{:S(2)}) collective-permute-start(bf16[32,4096]{1,0:T(8,128)(2,1)S(1)} %get-tuple-element.47), channel_id=1, source_target_pairs={{0,2},{1,3},{2,0},{3,1},{4,6},{5,7},{6,4},{7,5},{8,10},{9,11},{10,... | collective-permute-start | bytes 786440 | tf_op jit(solution)/shard_map/ppermute | solution.py:28
  24.2 1.6 %collective-permute-start.8 = (bf16[256,256]{1,0:T(8,128)(2,1)S(1)}, bf16[256,256]{1,0:T(8,128)(2,1)S(1)}, u32[]{:S(2)}, u32[]{:S(2)}) collective-permute-start(bf16[256,256]{1,0:T(8,128)(2,1)S(1)} %collective-permute-done.3.refs_4_), channel_id=1, source_target_pairs={{0,8},{8,16},{16,24},{24,28},{28,20},{20,12},{12,4},{4,0},{1,9},{9... | collective-permute-start | bytes 393224 | tf_op jit(solution)/shard_map/ppermute | solution.py:248
  26.2 3.2 %project.4 = (bf16[192,512]{1,0:T(8,128)(2,1)S(1)}, bf16[192,256]{1,0:T(8,128)(2,1)S(1)}) custom-call(s32[2]{0:T(128)S(1)} %pad_add_fusion.info_ref, bf16[96,4096]{1,0:T(8,128)(2,1)S(1)} %collective-permute-done.refs_0_, bf16[96,4096]{1,0:T(8,128)(2,1)S(1)} %collective-permute-done.6.refs_1_, f32[1,4096]{1,0:T(1,128)S(1)} %get-tuple-element.40.refs_2_, ...), custom_call_target="tpu_custom_call" | custom-call | flops 1207959552 | bytes 7864320 | tf_op jit(solution)/shard_map/project/pallas_call | solution.py:161
  29.8 1.3 %collective-permute-done.9.refs_7_ = bf16[256,256]{1,0:T(8,128)(2,1)S(1)} collective-permute-done((bf16[256,256]{1,0:T(8,128)(2,1)S(1)}, bf16[256,256]{1,0:T(8,128)(2,1)S(1)}, u32[]{:S(2)}, u32[]{:S(2)}) %collective-permute-start.9) | collective-permute-done | bytes 131104 | tf_op jit(solution)/shard_map/ppermute | solution.py:248
  31.1 1.8 %collective-permute-start.17 = (bf16[192,256]{1,0:T(8,128)(2,1)S(1)}, bf16[192,256]{1,0:T(8,128)(2,1)S(1)}, u32[]{:S(2)}, u32[]{:S(2)}) collective-permute-start(bf16[192,256]{1,0:T(8,128)(2,1)S(1)} %get-tuple-element.48.refs_2_), channel_id=1, source_target_pairs={{0,8},{8,16},{16,24},{24,28},{28,20},{20,12},{12,4},{4,0},{1,9},{9... | collective-permute-start | bytes 294920 | tf_op jit(solution)/shard_map/ppermute | solution.py:248
  32.9 1.6 %collective-permute-start.11 = (bf16[256,256]{1,0:T(8,128)(2,1)S(1)}, bf16[256,256]{1,0:T(8,128)(2,1)S(1)}, u32[]{:S(2)}, u32[]{:S(2)}) collective-permute-start(bf16[256,256]{1,0:T(8,128)(2,1)S(1)} %collective-permute-done.8.refs_6_), channel_id=1, source_target_pairs={{0,8},{8,16},{16,24},{24,28},{28,20},{20,12},{12,4},{4,0},{1,9},{9... | collective-permute-start | bytes 393224 | tf_op jit(solution)/shard_map/ppermute | solution.py:248
  35.0 1.8 %project.5 = (bf16[64,512]{1,0:T(8,128)(2,1)S(1)}, bf16[64,256]{1,0:T(8,128)(2,1)S(1)}) custom-call(s32[2]{0:T(128)S(1)} %pad_add_fusion.info_ref, bf16[32,4096]{1,0:T(8,128)(2,1)S(1)} %collective-permute-done.7.refs_0_, bf16[32,4096]{1,0:T(8,128)(2,1)S(1)} %collective-permute-done.10.refs_1_, f32[1,4096]{1,0:T(1,128)S(1)} %get-tuple-element.40.refs_2_, ...), custom_call_target="tpu_custom_call" | custom-call | flops 402653184 | bytes 6815744 | tf_op jit(solution)/shard_map/project/pallas_call | solution.py:161
  36.8 1.7 %collective-permute-start.19 = (bf16[192,256]{1,0:T(8,128)(2,1)S(1)}, bf16[192,256]{1,0:T(8,128)(2,1)S(1)}, u32[]{:S(2)}, u32[]{:S(2)}) collective-permute-start(bf16[192,256]{1,0:T(8,128)(2,1)S(1)} %collective-permute-done.17.refs_3_), channel_id=1, source_target_pairs={{0,8},{8,16},{16,24},{24,28},{28,20},{20,12},{12,4},{4,0},{1,9},{9... | collective-permute-start | bytes 294920 | tf_op jit(solution)/shard_map/ppermute | solution.py:248
  38.5 1.6 %collective-permute-start.13 = (bf16[64,256]{1,0:T(8,128)(2,1)S(1)}, bf16[64,256]{1,0:T(8,128)(2,1)S(1)}, u32[]{:S(2)}, u32[]{:S(2)}) collective-permute-start(bf16[64,256]{1,0:T(8,128)(2,1)S(1)} %get-tuple-element.50.refs_2_), channel_id=1, source_target_pairs={{0,8},{8,0},{16,24},{24,16},{28,20},{20,28},{12,4},{4,12},{1,9},{9... | collective-permute-start | bytes 98312 | tf_op jit(solution)/shard_map/ppermute | solution.py:291
  40.5 2.5 %attend.4 = (bf16[128,512]{1,0:T(8,128)(2,1)S(1)}, bf16[128,512]{1,0:T(8,128)(2,1)S(1)}) custom-call(s32[65]{0:T(128)S(1)} %plan.1.plan_ref, bf16[256,512]{1,0:T(8,128)(2,1)S(1)} %get-tuple-element.51.refs_0_, bf16[256,256]{1,0:T(8,128)(2,1)S(1)} %get-tuple-element.36.refs_1_, bf16[256,256]{1,0:T(8,128)(2,1)S(1)} %collective-permute-done.2.refs_2_, ...), custom_call_target="tpu_custom_call" | custom-call | flops 536870912 | bytes 1572864 | tf_op jit(solution)/shard_map/attend/pallas_call | solution.py:479
  43.0 1.7 %collective-permute-start.21 = (bf16[192,256]{1,0:T(8,128)(2,1)S(1)}, bf16[192,256]{1,0:T(8,128)(2,1)S(1)}, u32[]{:S(2)}, u32[]{:S(2)}) collective-permute-start(bf16[192,256]{1,0:T(8,128)(2,1)S(1)} %collective-permute-done.19.refs_5_), channel_id=1, source_target_pairs={{0,8},{8,16},{16,24},{24,28},{28,20},{20,12},{12,4},{4,0},{1,9},{9... | collective-permute-start | bytes 294920 | tf_op jit(solution)/shard_map/ppermute | solution.py:248
  45.2 1.6 %collective-permute-start.22 = (bf16[192,256]{1,0:T(8,128)(2,1)S(1)}, bf16[192,256]{1,0:T(8,128)(2,1)S(1)}, u32[]{:S(2)}, u32[]{:S(2)}) collective-permute-start(bf16[192,256]{1,0:T(8,128)(2,1)S(1)} %collective-permute-done.20.refs_6_), channel_id=1, source_target_pairs={{0,4},{8,0},{16,8},{24,16},{28,24},{20,28},{12,20},{4,12},{1,5},{9... | collective-permute-start | bytes 294920 | tf_op jit(solution)/shard_map/ppermute | solution.py:248
  47.7 1.6 %collective-permute-start.23 = (bf16[192,256]{1,0:T(8,128)(2,1)S(1)}, bf16[192,256]{1,0:T(8,128)(2,1)S(1)}, u32[]{:S(2)}, u32[]{:S(2)}) collective-permute-start(bf16[192,256]{1,0:T(8,128)(2,1)S(1)} %collective-permute-done.21.refs_7_), channel_id=1, source_target_pairs={{0,8},{8,16},{16,24},{24,28},{28,20},{20,12},{12,4},{4,0},{1,9},{9... | collective-permute-start | bytes 294920 | tf_op jit(solution)/shard_map/ppermute | solution.py:248
  49.3 1.2 %collective-permute-start.15 = (bf16[128,256]{1,0:T(8,128)(2,1)S(1)}, bf16[128,256]{1,0:T(8,128)(2,1)S(1)}, u32[]{:S(2)}, u32[]{:S(2)}) collective-permute-start(bf16[128,256]{1,0:T(8,128)(2,1)S(1)} %collective-permute-done.14.refs_4_), channel_id=1, source_target_pairs={{0,8},{8,0},{16,24},{24,16},{28,20},{20,28},{12,4},{4,12},{1,9},{9... | collective-permute-start | bytes 196616 | tf_op jit(solution)/shard_map/ppermute | solution.py:291
  50.6 3.0 %collective-permute-done.15.refs_5_ = bf16[128,256]{1,0:T(8,128)(2,1)S(1)} collective-permute-done((bf16[128,256]{1,0:T(8,128)(2,1)S(1)}, bf16[128,256]{1,0:T(8,128)(2,1)S(1)}, u32[]{:S(2)}, u32[]{:S(2)}) %collective-permute-start.15) | collective-permute-done | bytes 65568 | tf_op jit(solution)/shard_map/ppermute | solution.py:291
  54.7 2.1 %attend.5 = (f32[1,1,512]{2,1,0:T(1,128)S(1)}, f32[1,1,512]{2,1,0:T(1,128)S(1)}, f32[1,128,512]{2,1,0:T(8,128)S(1)}, f32[1,1,512]{2,1,0:T(1,128)S(1)}, f32[1,1,5...) custom-call(s32[65]{0:T(128)S(1)} %plan.1.plan_ref, bf16[192,512]{1,0:T(8,128)(2,1)S(1)} %get-tuple-element.53.refs_0_, ...), custom_call_target="tpu_custom_call" | custom-call | flops 402653184 | bytes 1310720 | tf_op jit(solution)/shard_map/attend/pallas_call | solution.py:479
  56.8 1.1 %collective-permute-done.16.refs_6_ = bf16[128,256]{1,0:T(8,128)(2,1)S(1)} collective-permute-done((bf16[128,256]{1,0:T(8,128)(2,1)S(1)}, bf16[128,256]{1,0:T(8,128)(2,1)S(1)}, u32[]{:S(2)}, u32[]{:S(2)}) %collective-permute-start.16) | collective-permute-done | bytes 65568 | tf_op jit(solution)/shard_map/ppermute | solution.py:291
  57.9 1.1 %attend.7 = bf16[128,512]{1,0:T(8,128)(2,1)S(1)} custom-call(s32[65]{0:T(128)S(1)} %plan.1.plan_ref, bf16[192,512]{1,0:T(8,128)(2,1)S(1)} %get-tuple-element.53.refs_0_, bf16[64,512]{1,0:T(8,128)(2,1)S(1)} %get-tuple-element.54.refs_1_, bf16[64,256]{1,0:T(8,128)(2,1)S(1)} %get-tuple-element.50.refs_2_, bf16[64,256]{1,0:T(8,128)(2,1)S(1)} %collective-permute-done.13.refs_3_, ...), custom_call_target="tpu_custom_call" | custom-call | flops 67108864 | bytes 524288 | tf_op jit(solution)/shard_map/attend/pallas_call | solution.py:479
  59.0 1.1 %attend.6 = bf16[128,512]{1,0:T(8,128)(2,1)S(1)} custom-call(s32[65]{0:T(128)S(1)} %plan.1.plan_ref, bf16[192,512]{1,0:T(8,128)(2,1)S(1)} %get-tuple-element.53.refs_0_, bf16[64,512]{1,0:T(8,128)(2,1)S(1)} %get-tuple-element.54.refs_1_, bf16[64,256]{1,0:T(8,128)(2,1)S(1)} %get-tuple-element.50.refs_2_, bf16[64,256]{1,0:T(8,128)(2,1)S(1)} %collective-permute-done.13.refs_3_, ...), custom_call_target="tpu_custom_call" | custom-call | flops 67108864 | bytes 524288 | tf_op jit(solution)/shard_map/attend/pallas_call | solution.py:479
  60.1 1.6 %collective-permute-start.24 = (bf16[128,512]{1,0:T(8,128)(2,1)S(1)}, bf16[128,512]{1,0:T(8,128)(2,1)S(1)}, u32[]{:S(2)}, u32[]{:S(2)}) collective-permute-start(bf16[128,512]{1,0:T(8,128)(2,1)S(1)} %attend.6), channel_id=1, source_target_pairs={{0,2},{1,3},{2,0},{3,1},{4,6},{5,7},{6,4},{7,5},{8,10},{9,11},{10,... | collective-permute-start | bytes 393224 | tf_op jit(solution)/shard_map/ppermute | solution.py:28
  61.7 1.3 %deliver.2.refs_2_ = bf16[1,128,2048]{2,1,0:T(8,128)(2,1)} custom-call(s32[2]{0:T(128)S(1)} %pad_add_fusion.info_ref, bf16[128,512]{1,0:T(8,128)(2,1)S(1)} %get-tuple-element.66.refs_0_, bf16[128,512]{1,0:T(8,128)(2,1)S(1)} %collective-permute-done.12.refs_1_), custom_call_target="tpu_custom_call" | custom-call | tf_op jit(solution)/shard_map/deliver/pallas_call | solution.py:509
  63.0 1.8 %collective-permute-done.25.refs_1_ = bf16[128,512]{1,0:T(8,128)(2,1)S(1)} collective-permute-done((bf16[128,512]{1,0:T(8,128)(2,1)S(1)}, bf16[128,512]{1,0:T(8,128)(2,1)S(1)}, u32[]{:S(2)}, u32[]{:S(2)}) %collective-permute-start.25) | collective-permute-done | bytes 131104 | tf_op jit(solution)/shard_map/ppermute | solution.py:28
  64.8 2.9 %collective-permute-done.24.refs_0_ = bf16[128,512]{1,0:T(8,128)(2,1)S(1)} collective-permute-done((bf16[128,512]{1,0:T(8,128)(2,1)S(1)}, bf16[128,512]{1,0:T(8,128)(2,1)S(1)}, u32[]{:S(2)}, u32[]{:S(2)}) %collective-permute-start.24) | collective-permute-done | bytes 131104 | tf_op jit(solution)/shard_map/ppermute | solution.py:28
  67.6 1.3 %deliver.3 = bf16[1,128,2048]{2,1,0:T(8,128)(2,1)} custom-call(s32[2]{0:T(128)S(1)} %pad_add_fusion.info_ref, bf16[128,512]{1,0:T(8,128)(2,1)S(1)} %collective-permute-done.24.refs_0_, bf16[128,512]{1,0:T(8,128)(2,1)S(1)} %collective-permute-done.25.refs_1_, bf16[1,128,2048]{2,1,0:T(8,128)(2,1)} %deliver.2.refs_2_), custom_call_target="tpu_custom_call", output_to_operand_aliasing={{}: (3, {})} | custom-call | tf_op jit(solution)/shard_map/deliver/pallas_call | solution.py:509
  (41 shorter events, 6.1 us)
Async XLA Ops:
  0.0 4.7 %collective-permute-start.1 = (bf16[128,4096]{1,0:T(8,128)(2,1)}, bf16[128,4096]{1,0:T(8,128)(2,1)S(1)}, u32[]{:S(2)}, u32[]{:S(2)}) collective-permute-start(bf16[128,4096]{1,0:T(8,128)(2,1)} %bitcast.4), channel_id=1, source_target_pairs={{0,1},{1,0},{2,3},{3,2},{4,5},{5,4},{6,7},{7,6},{8,9},{9,8},{10,11... | collective-permute-start | bytes 3145736 | tf_op jit(solution)/shard_map/ppermute | solution.py:28
  1.6 20.8 %collective-permute-start = (bf16[96,4096]{1,0:T(8,128)(2,1)S(1)}, bf16[96,4096]{1,0:T(8,128)(2,1)S(1)}, u32[]{:S(2)}, u32[]{:S(2)}) collective-permute-start(bf16[96,4096]{1,0:T(8,128)(2,1)S(1)} %cut.1), channel_id=1, source_target_pairs={{0,2},{1,3},{2,0},{3,1},{4,6},{5,7},{6,4},{7,5},{8,10},{9,11},{10,... | collective-permute-start | bytes 2359304 | tf_op jit(solution)/shard_map/ppermute | solution.py:28
  4.7 7.3 %copy-start = (s32[4,4,4]{2,1,0:T(4,128)S(1)}, s32[4,4,4]{2,1,0:T(4,128)}, u32[]{:S(2)}) copy-start(s32[4,4,4]{2,1,0:T(4,128)} %vertical_ref.1) | copy-start | bytes 772
  4.7 7.3 %copy-start.1 = (s32[4,4,4]{2,1,0:T(4,128)S(1)}, s32[4,4,4]{2,1,0:T(4,128)}, u32[]{:S(2)}) copy-start(s32[4,4,4]{2,1,0:T(4,128)} %slash_ref.1) | copy-start | bytes 772
  9.9 5.7 %collective-permute-start.2 = (bf16[256,256]{1,0:T(8,128)(2,1)S(1)}, bf16[256,256]{1,0:T(8,128)(2,1)S(1)}, u32[]{:S(2)}, u32[]{:S(2)}) collective-permute-start(bf16[256,256]{1,0:T(8,128)(2,1)S(1)} %get-tuple-element.36.refs_1_), channel_id=1, source_target_pairs={{0,8},{8,16},{16,24},{24,28},{28,20},{20,12},{12,4},{4,0},{1,9},{9... | collective-permute-start | bytes 393224 | tf_op jit(solution)/shard_map/ppermute | solution.py:248
  11.5 5.6 %collective-permute-start.4 = (bf16[256,256]{1,0:T(8,128)(2,1)S(1)}, bf16[256,256]{1,0:T(8,128)(2,1)S(1)}, u32[]{:S(2)}, u32[]{:S(2)}) collective-permute-start(bf16[256,256]{1,0:T(8,128)(2,1)S(1)} %get-tuple-element.36.refs_1_), channel_id=1, source_target_pairs={{0,4},{8,0},{16,8},{24,16},{28,24},{20,28},{12,20},{4,12},{1,5},{9... | collective-permute-start | bytes 393224 | tf_op jit(solution)/shard_map/ppermute | solution.py:248
  15.6 6.8 %collective-permute-start.3 = (bf16[256,256]{1,0:T(8,128)(2,1)S(1)}, bf16[256,256]{1,0:T(8,128)(2,1)S(1)}, u32[]{:S(2)}, u32[]{:S(2)}) collective-permute-start(bf16[256,256]{1,0:T(8,128)(2,1)S(1)} %collective-permute-done.2.refs_2_), channel_id=1, source_target_pairs={{0,8},{8,16},{16,24},{24,28},{28,20},{20,12},{12,4},{4,0},{1,9},{9... | collective-permute-start | bytes 393224 | tf_op jit(solution)/shard_map/ppermute | solution.py:248
  17.2 5.2 %collective-permute-start.5 = (bf16[256,256]{1,0:T(8,128)(2,1)S(1)}, bf16[256,256]{1,0:T(8,128)(2,1)S(1)}, u32[]{:S(2)}, u32[]{:S(2)}) collective-permute-start(bf16[256,256]{1,0:T(8,128)(2,1)S(1)} %collective-permute-done.4.refs_3_), channel_id=1, source_target_pairs={{0,4},{8,0},{16,8},{24,16},{28,24},{20,28},{12,20},{4,12},{1,5},{9... | collective-permute-start | bytes 393224 | tf_op jit(solution)/shard_map/ppermute | solution.py:248
  22.4 3.8 %collective-permute-start.6 = (bf16[96,4096]{1,0:T(8,128)(2,1)S(1)}, bf16[96,4096]{1,0:T(8,128)(2,1)S(1)}, u32[]{:S(2)}, u32[]{:S(2)}) collective-permute-start(bf16[96,4096]{1,0:T(8,128)(2,1)S(1)} %collective-permute-done.refs_0_), channel_id=1, source_target_pairs={{0,1},{1,0},{2,3},{3,2},{4,5},{5,4},{6,7},{7,6},{8,9},{9,8},{10,11... | collective-permute-start | bytes 2359304 | tf_op jit(solution)/shard_map/ppermute | solution.py:28
  22.4 8.7 %collective-permute-start.7 = (bf16[32,4096]{1,0:T(8,128)(2,1)S(1)}, bf16[32,4096]{1,0:T(8,128)(2,1)S(1)}, u32[]{:S(2)}, u32[]{:S(2)}) collective-permute-start(bf16[32,4096]{1,0:T(8,128)(2,1)S(1)} %get-tuple-element.47), channel_id=1, source_target_pairs={{0,2},{1,3},{2,0},{3,1},{4,6},{5,7},{6,4},{7,5},{8,10},{9,11},{10,... | collective-permute-start | bytes 786440 | tf_op jit(solution)/shard_map/ppermute | solution.py:28
  24.2 5.6 %collective-permute-start.8 = (bf16[256,256]{1,0:T(8,128)(2,1)S(1)}, bf16[256,256]{1,0:T(8,128)(2,1)S(1)}, u32[]{:S(2)}, u32[]{:S(2)}) collective-permute-start(bf16[256,256]{1,0:T(8,128)(2,1)S(1)} %collective-permute-done.3.refs_4_), channel_id=1, source_target_pairs={{0,8},{8,16},{16,24},{24,28},{28,20},{20,12},{12,4},{4,0},{1,9},{9... | collective-permute-start | bytes 393224 | tf_op jit(solution)/shard_map/ppermute | solution.py:248
  25.8 5.3 %collective-permute-start.9 = (bf16[256,256]{1,0:T(8,128)(2,1)S(1)}, bf16[256,256]{1,0:T(8,128)(2,1)S(1)}, u32[]{:S(2)}, u32[]{:S(2)}) collective-permute-start(bf16[256,256]{1,0:T(8,128)(2,1)S(1)} %collective-permute-done.5.refs_5_), channel_id=1, source_target_pairs={{0,4},{8,0},{16,8},{24,16},{28,24},{20,28},{12,20},{4,12},{1,5},{9... | collective-permute-start | bytes 393224 | tf_op jit(solution)/shard_map/ppermute | solution.py:248
  31.1 3.9 %collective-permute-start.10 = (bf16[32,4096]{1,0:T(8,128)(2,1)S(1)}, bf16[32,4096]{1,0:T(8,128)(2,1)S(1)}, u32[]{:S(2)}, u32[]{:S(2)}) collective-permute-start(bf16[32,4096]{1,0:T(8,128)(2,1)S(1)} %collective-permute-done.7.refs_0_), channel_id=1, source_target_pairs={{0,1},{1,0},{2,3},{3,2},{4,5},{5,4},{6,7},{7,6},{8,9},{9,8},{10,11... | collective-permute-start | bytes 786440 | tf_op jit(solution)/shard_map/ppermute | solution.py:28
  31.1 5.7 %collective-permute-start.17 = (bf16[192,256]{1,0:T(8,128)(2,1)S(1)}, bf16[192,256]{1,0:T(8,128)(2,1)S(1)}, u32[]{:S(2)}, u32[]{:S(2)}) collective-permute-start(bf16[192,256]{1,0:T(8,128)(2,1)S(1)} %get-tuple-element.48.refs_2_), channel_id=1, source_target_pairs={{0,8},{8,16},{16,24},{24,28},{28,20},{20,12},{12,4},{4,0},{1,9},{9... | collective-permute-start | bytes 294920 | tf_op jit(solution)/shard_map/ppermute | solution.py:248
  32.9 7.6 %collective-permute-start.11 = (bf16[256,256]{1,0:T(8,128)(2,1)S(1)}, bf16[256,256]{1,0:T(8,128)(2,1)S(1)}, u32[]{:S(2)}, u32[]{:S(2)}) collective-permute-start(bf16[256,256]{1,0:T(8,128)(2,1)S(1)} %collective-permute-done.8.refs_6_), channel_id=1, source_target_pairs={{0,8},{8,16},{16,24},{24,28},{28,20},{20,12},{12,4},{4,0},{1,9},{9... | collective-permute-start | bytes 393224 | tf_op jit(solution)/shard_map/ppermute | solution.py:248
  34.5 5.6 %collective-permute-start.18 = (bf16[192,256]{1,0:T(8,128)(2,1)S(1)}, bf16[192,256]{1,0:T(8,128)(2,1)S(1)}, u32[]{:S(2)}, u32[]{:S(2)}) collective-permute-start(bf16[192,256]{1,0:T(8,128)(2,1)S(1)} %get-tuple-element.48.refs_2_), channel_id=1, source_target_pairs={{0,4},{8,0},{16,8},{24,16},{28,24},{20,28},{12,20},{4,12},{1,5},{9... | collective-permute-start | bytes 294920 | tf_op jit(solution)/shard_map/ppermute | solution.py:248
  36.8 6.2 %collective-permute-start.19 = (bf16[192,256]{1,0:T(8,128)(2,1)S(1)}, bf16[192,256]{1,0:T(8,128)(2,1)S(1)}, u32[]{:S(2)}, u32[]{:S(2)}) collective-permute-start(bf16[192,256]{1,0:T(8,128)(2,1)S(1)} %collective-permute-done.17.refs_3_), channel_id=1, source_target_pairs={{0,8},{8,16},{16,24},{24,28},{28,20},{20,12},{12,4},{4,0},{1,9},{9... | collective-permute-start | bytes 294920 | tf_op jit(solution)/shard_map/ppermute | solution.py:248
  38.5 6.2 %collective-permute-start.13 = (bf16[64,256]{1,0:T(8,128)(2,1)S(1)}, bf16[64,256]{1,0:T(8,128)(2,1)S(1)}, u32[]{:S(2)}, u32[]{:S(2)}) collective-permute-start(bf16[64,256]{1,0:T(8,128)(2,1)S(1)} %get-tuple-element.50.refs_2_), channel_id=1, source_target_pairs={{0,8},{8,0},{16,24},{24,16},{28,20},{20,28},{12,4},{4,12},{1,9},{9... | collective-permute-start | bytes 98312 | tf_op jit(solution)/shard_map/ppermute | solution.py:291
  40.1 5.1 %collective-permute-start.20 = (bf16[192,256]{1,0:T(8,128)(2,1)S(1)}, bf16[192,256]{1,0:T(8,128)(2,1)S(1)}, u32[]{:S(2)}, u32[]{:S(2)}) collective-permute-start(bf16[192,256]{1,0:T(8,128)(2,1)S(1)} %collective-permute-done.18.refs_4_), channel_id=1, source_target_pairs={{0,4},{8,0},{16,8},{24,16},{28,24},{20,28},{12,20},{4,12},{1,5},{9... | collective-permute-start | bytes 294920 | tf_op jit(solution)/shard_map/ppermute | solution.py:248
  43.0 4.7 %collective-permute-start.21 = (bf16[192,256]{1,0:T(8,128)(2,1)S(1)}, bf16[192,256]{1,0:T(8,128)(2,1)S(1)}, u32[]{:S(2)}, u32[]{:S(2)}) collective-permute-start(bf16[192,256]{1,0:T(8,128)(2,1)S(1)} %collective-permute-done.19.refs_5_), channel_id=1, source_target_pairs={{0,8},{8,16},{16,24},{24,28},{28,20},{20,12},{12,4},{4,0},{1,9},{9... | collective-permute-start | bytes 294920 | tf_op jit(solution)/shard_map/ppermute | solution.py:248
  44.7 4.6 %collective-permute-start.14 = (bf16[128,256]{1,0:T(8,128)(2,1)S(1)}, bf16[128,256]{1,0:T(8,128)(2,1)S(1)}, u32[]{:S(2)}, u32[]{:S(2)}) collective-permute-start(bf16[128,256]{1,0:T(8,128)(2,1)S(1)} %pad_maximum_fusion.1), channel_id=1, source_target_pairs={{0,4},{8,16},{16,8},{24,28},{28,24},{20,12},{12,20},{4,0},{1,5},{9... | collective-permute-start | bytes 196616 | tf_op jit(solution)/shard_map/ppermute | solution.py:291
  45.2 9.5 %collective-permute-start.12 = (bf16[128,512]{1,0:T(8,128)(2,1)S(1)}, bf16[128,512]{1,0:T(8,128)(2,1)S(1)}, u32[]{:S(2)}, u32[]{:S(2)}) collective-permute-start(bf16[128,512]{1,0:T(8,128)(2,1)S(1)} %get-tuple-element.52), channel_id=1, source_target_pairs={{0,1},{1,0},{2,3},{3,2},{4,5},{5,4},{6,7},{7,6},{8,9},{9,8},{10,11... | collective-permute-start | bytes 393224 | tf_op jit(solution)/shard_map/ppermute | solution.py:28
  45.2 9.5 %collective-permute-start.22 = (bf16[192,256]{1,0:T(8,128)(2,1)S(1)}, bf16[192,256]{1,0:T(8,128)(2,1)S(1)}, u32[]{:S(2)}, u32[]{:S(2)}) collective-permute-start(bf16[192,256]{1,0:T(8,128)(2,1)S(1)} %collective-permute-done.20.refs_6_), channel_id=1, source_target_pairs={{0,4},{8,0},{16,8},{24,16},{28,24},{20,28},{12,20},{4,12},{1,5},{9... | collective-permute-start | bytes 294920 | tf_op jit(solution)/shard_map/ppermute | solution.py:248
  47.7 7.0 %collective-permute-start.23 = (bf16[192,256]{1,0:T(8,128)(2,1)S(1)}, bf16[192,256]{1,0:T(8,128)(2,1)S(1)}, u32[]{:S(2)}, u32[]{:S(2)}) collective-permute-start(bf16[192,256]{1,0:T(8,128)(2,1)S(1)} %collective-permute-done.21.refs_7_), channel_id=1, source_target_pairs={{0,8},{8,16},{16,24},{24,28},{28,20},{20,12},{12,4},{4,0},{1,9},{9... | collective-permute-start | bytes 294920 | tf_op jit(solution)/shard_map/ppermute | solution.py:248
  49.3 4.3 %collective-permute-start.15 = (bf16[128,256]{1,0:T(8,128)(2,1)S(1)}, bf16[128,256]{1,0:T(8,128)(2,1)S(1)}, u32[]{:S(2)}, u32[]{:S(2)}) collective-permute-start(bf16[128,256]{1,0:T(8,128)(2,1)S(1)} %collective-permute-done.14.refs_4_), channel_id=1, source_target_pairs={{0,8},{8,0},{16,24},{24,16},{28,20},{20,28},{12,4},{4,12},{1,9},{9... | collective-permute-start | bytes 196616 | tf_op jit(solution)/shard_map/ppermute | solution.py:291
  53.6 4.3 %collective-permute-start.16 = (bf16[128,256]{1,0:T(8,128)(2,1)S(1)}, bf16[128,256]{1,0:T(8,128)(2,1)S(1)}, u32[]{:S(2)}, u32[]{:S(2)}) collective-permute-start(bf16[128,256]{1,0:T(8,128)(2,1)S(1)} %collective-permute-done.15.refs_5_), channel_id=1, source_target_pairs={{0,4},{8,16},{16,8},{24,28},{28,24},{20,12},{12,20},{4,0},{1,5},{9... | collective-permute-start | bytes 196616 | tf_op jit(solution)/shard_map/ppermute | solution.py:291
  59.0 5.8 %collective-permute-start.25 = (bf16[128,512]{1,0:T(8,128)(2,1)S(1)}, bf16[128,512]{1,0:T(8,128)(2,1)S(1)}, u32[]{:S(2)}, u32[]{:S(2)}) collective-permute-start(bf16[128,512]{1,0:T(8,128)(2,1)S(1)} %attend.7), channel_id=1, source_target_pairs={{0,3},{1,2},{2,1},{3,0},{4,7},{5,6},{6,5},{7,4},{8,11},{9,10},{10,... | collective-permute-start | bytes 393224 | tf_op jit(solution)/shard_map/ppermute | solution.py:28
  60.1 7.5 %collective-permute-start.24 = (bf16[128,512]{1,0:T(8,128)(2,1)S(1)}, bf16[128,512]{1,0:T(8,128)(2,1)S(1)}, u32[]{:S(2)}, u32[]{:S(2)}) collective-permute-start(bf16[128,512]{1,0:T(8,128)(2,1)S(1)} %attend.6), channel_id=1, source_target_pairs={{0,2},{1,3},{2,0},{3,1},{4,6},{5,7},{6,4},{7,5},{8,10},{9,11},{10,... | collective-permute-start | bytes 393224 | tf_op jit(solution)/shard_map/ppermute | solution.py:28
